TPU v7x, 32 devices: a whole 2x2x4 slice. The times are simulated.
32 devices in a mesh: dom: 2 (over y), row: 4 (over z), aux: 2 (over x), sub: 2 (over core).
Axes of the slice: x: 2, y: 2, z: 4, core: 2. Of those that a mesh axis runs over, the one named last changes fastest.
Arguments:
- factor: float32 [512, 32, 256], P(('dom', 'row'), 'aux', 'sub'), parts along dimension 0, may hold values from -2 to 2
- density: float32 [512, 256], P(('dom', 'row')), parts along dimension 0, as said below
- screen: int32 [8, 4], P(('dom', 'row'), 'sub'), parts along dimension 0, may hold values from 0 to 3, as said below
Outputs:
- fock_exchange: float32 [512, 256], P(('dom', 'row'), ('aux', 'sub')), parts along dimension 0
There are 2 independent parts, one for each index of `dom`. A program takes and returns all parts, laid end to end along the dimension named above; each array names one. Nothing has to cross between parts.
Inputs may be any that keep to these rules, and one draw needn't show every extreme that they name: `screen`: row I lists 4 distinct block indices, the first being I itself. density is exactly symmetric.
All inputs are finite; a program needn't handle non-finite values.
Results may differ from a plain program's by a relative error of at most 0.0003.
Values sent between devices are 32-bit elements; how exact they have to be, the bound alone decides.
No kernel may reach another device: no remote copies, remote signals or barrier semaphores. Data moves between devices by JAX's collectives and lax.ppermute only.
A program may use at most 128 MiB of HBM per device.

v0:
```python
import jax
import jax.numpy as jnp
from jax import lax
from jax.sharding import PartitionSpec as P

precise = lax.Precision.HIGHEST


def pair_block(tiled, block_rows, block_cols):
    block_size = tiled.shape[0]
    picked = jnp.take(tiled, block_cols, axis=2)
    others = block_rows.reshape(
        block_rows.shape[0], block_rows.shape[1], block_cols.shape[0], block_size
    )
    return jnp.einsum(
        "ipsl,jpsl->ij", picked, others, precision=precise, preferred_element_type=jnp.float32
    )


def body(factor, density, screen):
    block_size = density.shape[0]
    orbitals = density.shape[1]
    nblocks = orbitals // block_size
    aux_local = factor.shape[1]
    own_block = lax.axis_index("row")
    full_rows, full_screen = (
        lax.all_gather(factor, "sub", axis=2, tiled=True),
        lax.all_gather(screen, "sub", axis=1, tiled=True),
    )
    whole = lax.all_gather(density, "row", axis=0, tiled=True)
    stacked = whole.reshape(nblocks, block_size, orbitals)
    panel = jnp.take(stacked, screen[0], axis=0).reshape(-1, orbitals)
    contracted = jnp.einsum(
        "ipk,kl->ipl", factor, panel, precision=precise, preferred_element_type=jnp.float32
    )
    tiled = contracted.reshape(block_size, aux_local, nblocks, block_size)
    zero_block = jnp.zeros((block_size, block_size), jnp.float32)
    rows_piece = lax.all_gather(full_rows[None], "row", axis=0, tiled=True)
    screen_piece = lax.all_gather(full_screen, "row", axis=0, tiled=True)
    count = rows_piece.shape[0]

    def single(member):
        offset, rows_one, screen_one = member
        return lax.cond(
            offset >= own_block, lambda: pair_block(tiled, rows_one, screen_one), lambda: zero_block
        )

    computed = lax.map(single, (jnp.arange(count, dtype=jnp.int32), rows_piece, screen_piece))
    updated = jnp.transpose(computed, (1, 0, 2))
    keep_mask = (jnp.arange(nblocks, dtype=jnp.int32) != own_block).astype(jnp.float32)
    received = lax.all_to_all(updated, "row", split_axis=1, concat_axis=1, tiled=True)
    mirrored = jnp.transpose(received, (2, 1, 0)) * keep_mask[None, :, None]
    partial_value = (updated + mirrored).reshape(block_size, orbitals)
    return lax.psum_scatter(partial_value, ("aux", "sub"), scatter_dimension=1, tiled=True)


def solution(mesh):
    return jax.shard_map(
        body,
        mesh=mesh,
        in_specs=(
            P(("dom", "row"), "aux", "sub"),
            P(("dom", "row"), None),
            P(("dom", "row"), "sub"),
        ),
        out_specs=P(("dom", "row"), ("aux", "sub")),
        check_vma=False,
    )
```

profile of v0, /device:TPU:0, one launch (start us, length us, event | category | flops | bytes accessed | tf_op | source)
XLA Modules:
  0.0 197.3 jit_solution(639090490352244349)
XLA Ops:
  7.3 13.3 %all-gather.5.cloned.1.call-done = f32[64,16,256]{2,1,0:T(8,128)} async-done(((f32[64,16,128]{2,1,0:T(8,128)}), f32[64,16,256]{2,1,0:T(8,128)}) %all-gather.5.cloned.1.call-update) | async-done | bytes 1048592 | tf_op jit(solution)/shard_map/all_gather | solution.py:27
  25.1 11.3 %all-gather.1 = s32[4,1,4]{2,1,0:T(1,128)S(1)} all-gather(s32[1,1,4]{2,1,0:T(1,128)S(1)} %bitcast.58), channel_id=1, replica_groups=mesh['dom'=2,'row'=4,'aux'=2,'sub'=2] {'row'}, dimensions={0}, use_global_device_ids=true | all-gather | bytes 80 | tf_op jit(solution)/shard_map/all_gather | solution.py:39
  37.3 17.0 %all_gather.17 = f32[256,256]{1,0:T(8,128)S(1)} all-gather(f32[64,256]{1,0:T(8,128)} %param.8), channel_id=1, replica_groups=mesh['dom'=2,'row'=4,'aux'=2,'sub'=2] {'row'}, dimensions={0}, use_global_device_ids=true | all-gather | bytes 327680 | tf_op jit(solution)/shard_map/all_gather | solution.py:30
  57.5 2.5 %copy.18 = f32[64,16,4,64]{3,1,2,0:T(8,128)} copy(f32[64,16,4,64]{3,2,0,1:T(4,128)S(1)} %reshape.84) | data formatting | bytes 2097152 | tf_op jit(solution)/shard_map/while | solution.py:48
  60.0 48.3 %all-gather.7.cloned.1.call-done = f32[256,16,256]{2,1,0:T(8,128)} async-done(((f32[64,16,256]{2,1,0:T(8,128)}), f32[256,16,256]{2,1,0:T(8,128)}) %all-gather.7.cloned.1.call-update) | async-done | bytes 4194320 | tf_op jit(solution)/shard_map/all_gather | solution.py:38
  108.3 50.6 %while.10 = (s32[]{:T(128)}, f32[4,64,64]{2,1,0:T(8,128)S(1)}, s32[4]{0:T(128)S(1)}, s32[]{:T(128)}, s32[4,4]{1,0:T(4,128)S(1)}, /*index=5*/f32[64,16,4,64]{3,1,2,0:T(8,128)}, f32[4,64,16,256]{3,2,1,0:T(8,128)}, s32[]{:T(128)}) while((s32[]{:T(128)}, f32[4,64,64]{2,1,0:T(8,128)S(1)}, s32[4]{0:T(128)S(1)}, s32[]{:T(128)}, ...), condition=%wide.region_3.4_spmd, body=%wide.region_0.3_spmd.sunk | while | flops 201589792 | bytes 10572039 | solution.py:48
  109.5 11.4 %conditional.2 = (f32[1,64,64]{2,1,0:T(8,128)S(1)}) conditional(s32[]{:T(128)} %convert_element_type.13, () %tuple.35, (s32[4,4]{1,0:T(4,128)S(1)}, s32[]{:T(128)}, f32[64,16,4,64]{3,1,2,0:T(8,128)}, f32[4,64,16,256]{3,2,1,0:T(8,128)}) %tuple.36), branch_computations={%region_1.1_spmd, %region_2.2_spmd} | conditional | flops 201589792 | bytes 10506348 | solution.py:44
  111.8 3.6 %gather_fusion = f32[4,64,16,64]{3,2,1,0:T(8,128)} fusion(f32[64,16,4,64]{3,1,2,0:T(8,128)} %get-tuple-element.74, s32[1024]{0:T(1024)S(1)} %pad_clamp_fusion), kind=kCustom, calls=%fused_computation | custom fusion | bytes 2097168 | tf_op jit(solution)/shard_map/while/body/eval_jaxpr/cond/branch_1_fun/jit(_take)/gather | solution.py:11
  115.4 1.8 select_bitcast_fusion
  117.3 3.6 %fusion.3 = f32[1,64,64]{2,1,0:T(8,128)S(1)} fusion(f32[64,16,4,64]{3,2,1,0:T(4,128)S(1)} %reshape.79, f32[64,16,4,64]{3,1,0,2:T(8,128)S(1)} %select_bitcast_fusion), kind=kOutput, calls=%fused_computation.6 | convolution fusion | flops 201326592 | bytes 2113536 | tf_op jit(solution)/shard_map/while/body/eval_jaxpr/cond/branch_1_fun/ipsl,jpsl->ij/dot_general | solution.py:15
  122.2 11.4 %conditional.2 = (f32[1,64,64]{2,1,0:T(8,128)S(1)}) conditional(s32[]{:T(128)} %convert_element_type.13, () %tuple.35, (s32[4,4]{1,0:T(4,128)S(1)}, s32[]{:T(128)}, f32[64,16,4,64]{3,1,2,0:T(8,128)}, f32[4,64,16,256]{3,2,1,0:T(8,128)}) %tuple.36), branch_computations={%region_1.1_spmd, %region_2.2_spmd} | conditional | flops 201589792 | bytes 10506348 | solution.py:44
  124.4 3.6 %gather_fusion = f32[4,64,16,64]{3,2,1,0:T(8,128)} fusion(f32[64,16,4,64]{3,1,2,0:T(8,128)} %get-tuple-element.74, s32[1024]{0:T(1024)S(1)} %pad_clamp_fusion), kind=kCustom, calls=%fused_computation | custom fusion | bytes 2097168 | tf_op jit(solution)/shard_map/while/body/eval_jaxpr/cond/branch_1_fun/jit(_take)/gather | solution.py:11
  128.1 1.8 select_bitcast_fusion
  129.9 3.6 %fusion.3 = f32[1,64,64]{2,1,0:T(8,128)S(1)} fusion(f32[64,16,4,64]{3,2,1,0:T(4,128)S(1)} %reshape.79, f32[64,16,4,64]{3,1,0,2:T(8,128)S(1)} %select_bitcast_fusion), kind=kOutput, calls=%fused_computation.6 | convolution fusion | flops 201326592 | bytes 2113536 | tf_op jit(solution)/shard_map/while/body/eval_jaxpr/cond/branch_1_fun/ipsl,jpsl->ij/dot_general | solution.py:15
  134.8 11.4 %conditional.2 = (f32[1,64,64]{2,1,0:T(8,128)S(1)}) conditional(s32[]{:T(128)} %convert_element_type.13, () %tuple.35, (s32[4,4]{1,0:T(4,128)S(1)}, s32[]{:T(128)}, f32[64,16,4,64]{3,1,2,0:T(8,128)}, f32[4,64,16,256]{3,2,1,0:T(8,128)}) %tuple.36), branch_computations={%region_1.1_spmd, %region_2.2_spmd} | conditional | flops 201589792 | bytes 10506348 | solution.py:44
  137.1 3.6 %gather_fusion = f32[4,64,16,64]{3,2,1,0:T(8,128)} fusion(f32[64,16,4,64]{3,1,2,0:T(8,128)} %get-tuple-element.74, s32[1024]{0:T(1024)S(1)} %pad_clamp_fusion), kind=kCustom, calls=%fused_computation | custom fusion | bytes 2097168 | tf_op jit(solution)/shard_map/while/body/eval_jaxpr/cond/branch_1_fun/jit(_take)/gather | solution.py:11
  140.7 1.8 select_bitcast_fusion
  142.6 3.6 %fusion.3 = f32[1,64,64]{2,1,0:T(8,128)S(1)} fusion(f32[64,16,4,64]{3,2,1,0:T(4,128)S(1)} %reshape.79, f32[64,16,4,64]{3,1,0,2:T(8,128)S(1)} %select_bitcast_fusion), kind=kOutput, calls=%fused_computation.6 | convolution fusion | flops 201326592 | bytes 2113536 | tf_op jit(solution)/shard_map/while/body/eval_jaxpr/cond/branch_1_fun/ipsl,jpsl->ij/dot_general | solution.py:15
  147.5 11.4 %conditional.2 = (f32[1,64,64]{2,1,0:T(8,128)S(1)}) conditional(s32[]{:T(128)} %convert_element_type.13, () %tuple.35, (s32[4,4]{1,0:T(4,128)S(1)}, s32[]{:T(128)}, f32[64,16,4,64]{3,1,2,0:T(8,128)}, f32[4,64,16,256]{3,2,1,0:T(8,128)}) %tuple.36), branch_computations={%region_1.1_spmd, %region_2.2_spmd} | conditional | flops 201589792 | bytes 10506348 | solution.py:44
  149.7 3.6 %gather_fusion = f32[4,64,16,64]{3,2,1,0:T(8,128)} fusion(f32[64,16,4,64]{3,1,2,0:T(8,128)} %get-tuple-element.74, s32[1024]{0:T(1024)S(1)} %pad_clamp_fusion), kind=kCustom, calls=%fused_computation | custom fusion | bytes 2097168 | tf_op jit(solution)/shard_map/while/body/eval_jaxpr/cond/branch_1_fun/jit(_take)/gather | solution.py:11
  155.2 3.6 %fusion.3 = f32[1,64,64]{2,1,0:T(8,128)S(1)} fusion(f32[64,16,4,64]{3,2,1,0:T(4,128)S(1)} %reshape.79, f32[64,16,4,64]{3,1,0,2:T(8,128)S(1)} %select_bitcast_fusion), kind=kOutput, calls=%fused_computation.6 | convolution fusion | flops 201326592 | bytes 2113536 | tf_op jit(solution)/shard_map/while/body/eval_jaxpr/cond/branch_1_fun/ipsl,jpsl->ij/dot_general | solution.py:15
  159.7 3.3 %all-to-all-start = ((f32[4,1,4096]{2,1,0:T(1,128)}), f32[4,1,4096]{2,1,0:T(1,128)S(1)}, u32[]{:S(2)}, u32[]{:S(2)}) async-start(f32[4,1,4096]{2,1,0:T(1,128)} %reshape.115), calls=%async_computation | async-start | bytes 131072 | tf_op jit(solution)/shard_map/all_to_all | solution.py:51
  163.1 5.6 %all-to-all-done = f32[4,1,4096]{2,1,0:T(1,128)S(1)} async-done(((f32[4,1,4096]{2,1,0:T(1,128)}), f32[4,1,4096]{2,1,0:T(1,128)S(1)}, u32[]{:S(2)}, u32[]{:S(2)}) %all-to-all-start) | async-done | bytes 65568 | tf_op jit(solution)/shard_map/all_to_all | solution.py:51
  171.0 18.3 %reduce-scatter.4.cloned.1.call-done = f32[64,64]{1,0:T(8,128)} async-done(((f32[256,64]{1,0:T(8,128)}), f32[64,64]{1,0:T(8,128)}) %reduce-scatter.4.cloned.1.call-update) | async-done | bytes 16400
  (61 shorter events, 26.4 us)
Async XLA Ops:
  6.5 49.1 %copy-start = (f32[64,16,128]{2,1,0:T(8,128)S(1)}, f32[64,16,128]{2,1,0:T(8,128)}, u32[]{:S(2)}) copy-start(f32[64,16,128]{2,1,0:T(8,128)} %param.7) | copy-start | bytes 1572868
  6.5 14.1 %all-gather.5.cloned.1.call-start = ((), (), s32[]{:S(2)}) async-start(), calls=%async_computation.2 | async-start | bytes 1572864 | tf_op jit(solution)/shard_map/all_gather | solution.py:27
  7.3 101.0 %all-gather.7.cloned.1.call-start = ((), (), s32[]{:S(2)}) async-start(), calls=%async_computation.3 | async-start | bytes 5242880 | tf_op jit(solution)/shard_map/all_gather | solution.py:38
  159.7 9.0 %all-to-all-start = ((f32[4,1,4096]{2,1,0:T(1,128)}), f32[4,1,4096]{2,1,0:T(1,128)S(1)}, u32[]{:S(2)}, u32[]{:S(2)}) async-start(f32[4,1,4096]{2,1,0:T(1,128)} %reshape.115), calls=%async_computation | async-start | bytes 131072 | tf_op jit(solution)/shard_map/all_to_all | solution.py:51
  163.0 26.3 %reduce-scatter.4.cloned.1.call-start = ((), (), s32[]{:S(2)}) async-start(), calls=%async_computation.4 | async-start | bytes 163840
Sparse Core Ops, SparseCore 0:
  8.9 11.6 all-gather.4
  22.2 86.0 all-gather.6
  171.2 18.0 reduce-scatter.3
where the time goes:
time: 198 us; the launch traced here: 197 us
  waiting for transfers between devices  86.2 us (44%)
  local copies, waits for them, and re-layouts  35.6 us (18%)
  blocking collectives  30.1 us (15%)
  matrix products  15.5 us (8%)
  between operations  13.9 us (7%)
  other arithmetic  9.69 us (5%)
  starting transfers between devices  3.36 us (2%)
  loops' own time  2.88 us (1%)
    all_gather x1, waiting for transfers between devices, body(): rows_piece = lax.all_gather(full_rows[None], 'row', axis=0, tiled=True)  48.3 us
    unnamed x4, waiting for transfers between devices  19 us
    all_gather x1, blocking collectives, body(): whole = lax.all_gather(density, 'row', axis=0, tiled=True)  17 us
    gather x4, local copies, waits for them, and re-layouts, pair_block(): picked = jnp.take(tiled, block_cols, axis=2)  14.6 us
    dot_general x4, matrix products, pair_block(): jnp.einsum('ipsl,jpsl->ij', picked, others, precision=precise, preferred_...  14.5 us
    all_gather x1, waiting for transfers between devices, body(): lax.all_gather(factor, 'sub', axis=2, tiled=True)  13.3 us
    all_gather x1, blocking collectives, body(): screen_piece = lax.all_gather(full_screen, 'row', axis=0, tiled=True)  11.3 us
    dynamic_slice x8, local copies, waits for them, and re-layouts, body(): lax.map(single, (jnp.arange(count, dtype=jnp.int32), rows_piece, screen_p...  7.63 us
  transfers between devices with their start and end apart: 4, of which 4 were waited for; matrix products, arithmetic and copies ran while one was open for 4% of the time, Pallas kernels for 0%

commit v1 on v0

--- a/solution.py
+++ b/solution.py
@@ -1,9 +1,165 @@
+import functools
+
 import jax
 import jax.numpy as jnp
 from jax import lax
+from jax.experimental import pallas as pl
+from jax.experimental.pallas import tpu as pltpu
 from jax.sharding import PartitionSpec as P
 
 precise = lax.Precision.HIGHEST
+VMEM = pl.BlockSpec(memory_space=pltpu.VMEM)
+SMEM = pl.BlockSpec(memory_space=pltpu.SMEM)
+F32 = jnp.float32
+BF16 = jnp.bfloat16
+
+
+def call(kernel, outs, scratch=(), ins=None, count=0):
+    return pl.pallas_call(
+        kernel,
+        out_shape=tuple(jax.ShapeDtypeStruct(s, F32) for s in outs),
+        in_specs=ins if ins is not None else [VMEM] * count,
+        out_specs=tuple(VMEM for _ in outs),
+        scratch_shapes=list(scratch),
+        compiler_params=pltpu.CompilerParams(vmem_limit_bytes=12 * 1024 * 1024),
+    )
+
+
+def swap(x, axes, size, k):
+    return lax.ppermute(x, axes, [(a, a ^ k) for a in range(size)])
+
+
+def split(x):
+    high = x.astype(BF16)
+    return high, (x - high.astype(F32)).astype(BF16)
+
+
+def pack_kernel(aux_local, share, screen_ref, other_ref, own_ref, par_ref, *outs):
+    r, s = lax.axis_index("row"), lax.axis_index("sub")
+    size = own_ref.shape[0] // aux_local
+    low = lax.broadcasted_iota(jnp.int32, (size, 128), 1) < 64
+    half = jnp.where(low, 0, 1)
+    places = []
+    for ref in (screen_ref, other_ref):
+        a, b = ref[0, 0], ref[0, 1]
+        places += [jnp.where(low, a, b), jnp.where(low, b, a)]
+    subs = 2
+    for k, out in enumerate(outs):
+        for j in range(share):
+            p = ((r ^ k) * subs + s) * share + j
+            v = own_ref[pl.ds(p, size, stride=aux_local), :]
+            w = par_ref[pl.ds(p, size, stride=aux_local), :]
+            parts = [v, pltpu.roll(v, 64, 1), w, pltpu.roll(w, 64, 1)]
+            for h in range(out.shape[1] // 128):
+                block = half + 2 * h
+                value = jnp.zeros((size, 128), F32)
+                for place, part in zip(places, parts):
+                    value = jnp.where(place == block, part, value)
+                out[j * size:(j + 1) * size, h * 128:(h + 1) * 128] = value
+
+
+def fock_kernel(share, nrow, nquarter, *refs):
+    chunks, refs = refs[:nrow], refs[nrow:]
+    near, far, refs = refs[0], refs[1], refs[2:]
+    outs, (dh, dl, bh, bl, total) = refs[:nquarter], refs[nquarter:]
+    r = lax.axis_index("row")
+    q = lax.axis_index("aux") * 2 + lax.axis_index("sub")
+    size = chunks[0].shape[0] // share
+    piece = near.shape[2]
+    for dq in range(nquarter):
+        for k in range(nrow):
+            source = (near if dq % 2 == 0 else far)[dq // 2, k]
+            start = pl.multiple_of((r ^ k) * size + (q ^ dq) * piece, piece)
+            high, lower = split(source)
+            dh[pl.ds(start, piece), :] = high
+            dl[pl.ds(start, piece), :] = lower
+    for k in range(nrow):
+        start = pl.multiple_of((r ^ k) * size, size)
+        for j in range(share):
+            high, lower = split(chunks[k][j * size:(j + 1) * size, :])
+            bh[j, pl.ds(start, size), :] = high
+            bl[j, pl.ds(start, size), :] = lower
+    dot = functools.partial(jnp.dot, preferred_element_type=F32)
+    dot_t = lambda a, b: lax.dot_general(a, b, (((1,), (1,)), ((), ())), preferred_element_type=F32)
+    result = None
+    for j in range(share):
+        b1, b2 = bh[j], bl[j]
+        c = dot(b1, dh[...]) + (dot(b1, dl[...]) + dot(b2, dh[...]))
+        c1, c2 = split(c)
+        f = dot_t(c1, b1) + (dot_t(c1, b2) + dot_t(c2, b1))
+        result = f if result is None else result + f
+    total[...] = result
+    for dq in range(nquarter):
+        start = pl.multiple_of((q ^ dq) * size, size)
+        outs[dq][...] = total[pl.ds(start, size), :]
+
+
+def cut_kernel(nrow, *refs):
+    ins, outs = refs[:-nrow], refs[-nrow:]
+    r = lax.axis_index("row")
+    value = ins[0][...] + ins[1][...] + (ins[2][...] + ins[3][...])
+    size = value.shape[0]
+    low = lax.broadcasted_iota(jnp.int32, (size // 2, 128), 1) < 64
+    for k in range(nrow):
+        block = r ^ k
+        picked = value[:, :128]
+        for h in range(1, value.shape[1] // 128):
+            picked = jnp.where(block // 2 == h, value[:, h * 128:(h + 1) * 128], picked)
+        turned = pltpu.roll(picked, 64, 1)
+        odd = block % 2 == 1
+        first = jnp.where(odd, turned, picked)[:size // 2]
+        second = jnp.where(odd, picked, turned)[size // 2:]
+        outs[k][...] = jnp.where(low, first, second)
+
+
+def final_kernel(a, b, c, d, out):
+    value = a[...] + b[...] + (c[...] + d[...])
+    both = jnp.transpose(jnp.concatenate([value, pltpu.roll(value, 64, 1)], axis=0))
+    size = out.shape[0]
+    out[...] = both[:size, :]
+
+
+def dealt_body(sizes, factor, density, screen):
+    nrow, naux, nsub = sizes
+    block_size, orbitals = density.shape
+    aux_local = factor.shape[1]
+    share = aux_local // (nrow * nsub)
+    flat = factor.reshape(block_size * aux_local, factor.shape[2])
+    other_screen = swap(screen, "sub", nsub, 1)
+    other = swap(flat, "sub", nsub, 1)
+    q = lax.axis_index("aux") * nsub + lax.axis_index("sub")
+    nquarter = naux * nsub
+    piece = block_size // nquarter
+    quarter = lax.dynamic_slice_in_dim(density, q * piece, piece, 0)
+    chunks = call(
+        functools.partial(pack_kernel, aux_local, share),
+        [(share * block_size, orbitals)] * nrow,
+        ins=[SMEM, SMEM, VMEM, VMEM],
+    )(screen, other_screen, flat, other)
+    order = [3, 2, 1]
+    moved = {k: swap(quarter, "row", nrow, k) for k in order}
+    got = {k: swap(chunks[k], "row", nrow, k) for k in order}
+    near = jnp.stack([quarter] + [moved[k] for k in range(1, nrow)])
+    near = jnp.stack([near, swap(near, "aux", naux, 1)])
+    far = swap(near, "sub", nsub, 1)
+    parts = call(
+        functools.partial(fock_kernel, share, nrow, nquarter),
+        [(block_size, orbitals)] * nquarter,
+        scratch=[
+            pltpu.VMEM((orbitals, orbitals), BF16),
+            pltpu.VMEM((orbitals, orbitals), BF16),
+            pltpu.VMEM((share, orbitals, orbitals), BF16),
+            pltpu.VMEM((share, orbitals, orbitals), BF16),
+            pltpu.VMEM((orbitals, orbitals), F32),
+        ],
+        count=nrow + 2,
+    )(chunks[0], *[got[k] for k in range(1, nrow)], near, far)
+    sums = [parts[0]] + [swap(parts[k], ("aux", "sub"), nquarter, k) for k in range(1, nquarter)]
+    cuts = call(
+        functools.partial(cut_kernel, nrow), [(block_size // 2, 2 * block_size)] * nrow, count=nquarter
+    )(*sums)
+    last = [cuts[0]] + [swap(cuts[k], "row", nrow, k) for k in range(1, nrow)]
+    return call(final_kernel, [(block_size, block_size)], count=nrow)(*last)[0]
 
 
 def pair_block(tiled, block_rows, block_cols):
@@ -17,7 +173,7 @@
     )
 
 
-def body(factor, density, screen):
+def gathered_body(factor, density, screen):
     block_size = density.shape[0]
     orbitals = density.shape[1]
     nblocks = orbitals // block_size
@@ -55,6 +211,24 @@
 
 
 def solution(mesh):
+    sizes = tuple(mesh.shape[a] for a in ("row", "aux", "sub"))
+
+    def body(factor, density, screen):
+        nrow, naux, nsub = sizes
+        block_size, orbitals = density.shape
+        fits = (
+            naux * nsub == 4
+            and nsub == 2
+            and nrow == 4
+            and block_size == 64
+            and orbitals == nrow * block_size
+            and factor.shape[2] == 128
+            and factor.shape[1] % (nrow * nsub * 2) == 0
+        )
+        if fits:
+            return dealt_body(sizes, factor, density, screen)
+        return gathered_body(factor, density, screen)
+
     return jax.shard_map(
         body,
         mesh=mesh,

time: 198 us -> 46.7 us (0.24)
  waiting for transfers between devices: 86.2 us -> 23.3 us
  local copies, waits for them, and re-layouts: 35.6 us -> 0.92 us
  blocking collectives: 30.1 us -> 0 us
  starting transfers between devices: 3.36 us -> 19.7 us
  matrix products: 15.5 us -> 0 us
  between operations: 13.9 us -> 0.1 us
  other arithmetic: 9.69 us -> 0.02 us
  loops' own time: 2.88 us -> 0 us
  Pallas kernels: 0 us -> 2.62 us
    all_gather x2 -> x0, waiting for transfers between devices: 61.6 us -> none  [the longest x1 48.3 us: body(): rows_piece = lax.all_gather(full_rows[None], 'row', axis=0, tiled=True)]
    all_gather x2 -> x0, blocking collectives: 28.3 us -> none  [the longest x1 17 us: body(): whole = lax.all_gather(density, 'row', axis=0, tiled=True)]
    ppermute x0 -> x16, waiting for transfers between devices: none -> 23.3 us  [swap(): return lax.ppermute(x, axes, [(a, a ^ k) for a in range(size)])]
    ppermute x0 -> x16, starting transfers between devices: none -> 19.7 us  [swap(): return lax.ppermute(x, axes, [(a, a ^ k) for a in range(size)])]
    unnamed x4 -> x0, waiting for transfers between devices: 19 us -> none
    dot_general x5 -> x0, matrix products: 15.5 us -> none  [the longest x4 14.5 us: pair_block(): jnp.einsum('ipsl,jpsl->ij', picked, others, precision=precise, preferred_...]
    gather x5 -> x0, local copies, waits for them, and re-layouts: 15.1 us -> none  [the longest x4 14.6 us: pair_block(): picked = jnp.take(tiled, block_cols, axis=2)]
    select_n x10 -> x0, other arithmetic: 8.06 us -> none  [the longest x8 7.31 us: pair_block(): picked = jnp.take(tiled, block_cols, axis=2)]
  transfers between devices with their start and end apart: 4 -> 16, of which waited for: 4 -> 9; matrix products, arithmetic and copies ran while one was open for 4% -> 0% of each run, Pallas kernels for 0% -> 2%
where the time goes in v1:
time: 46.7 us; the launch traced here: 46.6 us
  waiting for transfers between devices  23.3 us (50%)
  starting transfers between devices  19.7 us (42%)
  Pallas kernels  2.62 us (6%)
  local copies, waits for them, and re-layouts  0.92 us (2%)
    ppermute x16, waiting for transfers between devices, swap(): return lax.ppermute(x, axes, [(a, a ^ k) for a in range(size)])  23.3 us
    ppermute x16, starting transfers between devices, swap(): return lax.ppermute(x, axes, [(a, a ^ k) for a in range(size)])  19.7 us
  transfers between devices with their start and end apart: 16, of which 9 were waited for; matrix products, arithmetic and copies ran while one was open for 0% of the time, Pallas kernels for 2%

profile of v1, /device:TPU:0, one launch (start us, length us, event | category | flops | bytes accessed | tf_op | source)
XLA Modules:
  0.0 46.6 jit_solution(17411404796425981885)
XLA Ops:
  0.0 0.5 collective-permute-start.1
  0.5 0.4 copy-done
  0.8 5.0 %collective-permute-start.7 = (f32[16,256]{1,0:T(8,128)S(1)}, f32[16,256]{1,0:T(8,128)S(1)}, u32[]{:S(2)}, u32[]{:S(2)}) collective-permute-start(f32[16,256]{1,0:T(8,128)S(1)} %constant_dynamic-slice_fusion), channel_id=1, source_target_pairs={{0,12},{4,8},{8,4},{12,0},{1,13},{5,9},{9,5},{13,1},{2,14},{6,10},... | collective-permute-start | bytes 49160 | tf_op jit(solution)/shard_map/ppermute | solution.py:29
  5.9 0.6 %collective-permute-start.5 = (f32[16,256]{1,0:T(8,128)S(1)}, f32[16,256]{1,0:T(8,128)S(1)}, u32[]{:S(2)}, u32[]{:S(2)}) collective-permute-start(f32[16,256]{1,0:T(8,128)S(1)} %constant_dynamic-slice_fusion), channel_id=1, source_target_pairs={{0,4},{4,0},{8,12},{12,8},{1,5},{5,1},{9,13},{13,9},{2,6},{6,2},{1... | collective-permute-start | bytes 49160 | tf_op jit(solution)/shard_map/ppermute | solution.py:29
  6.5 1.1 %collective-permute-done.7 = f32[16,256]{1,0:T(8,128)S(1)} collective-permute-done((f32[16,256]{1,0:T(8,128)S(1)}, f32[16,256]{1,0:T(8,128)S(1)}, u32[]{:S(2)}, u32[]{:S(2)}) %collective-permute-start.7) | collective-permute-done | bytes 16416 | tf_op jit(solution)/shard_map/ppermute | solution.py:29
  7.6 2.9 %collective-permute-done.6 = f32[16,256]{1,0:T(8,128)S(1)} collective-permute-done((f32[16,256]{1,0:T(8,128)S(1)}, f32[16,256]{1,0:T(8,128)S(1)}, u32[]{:S(2)}, u32[]{:S(2)}) %collective-permute-start.6) | collective-permute-done | bytes 16416 | tf_op jit(solution)/shard_map/ppermute | solution.py:29
  10.5 1.6 %collective-permute-start.8 = (f32[4,16,256]{2,1,0:T(8,128)S(1)}, f32[4,16,256]{2,1,0:T(8,128)S(1)}, u32[]{:S(2)}, u32[]{:S(2)}) collective-permute-start(f32[4,16,256]{2,1,0:T(8,128)S(1)} %get-tuple-element.30), channel_id=1, source_target_pairs={{0,2},{2,0},{1,3},{3,1},{4,6},{6,4},{5,7},{7,5},{8,10},{10,8},{9,1... | collective-permute-start | bytes 196616 | tf_op jit(solution)/shard_map/ppermute | solution.py:29
  12.1 2.8 %collective-permute-done.8 = f32[4,16,256]{2,1,0:T(8,128)S(1)} collective-permute-done((f32[4,16,256]{2,1,0:T(8,128)S(1)}, f32[4,16,256]{2,1,0:T(8,128)S(1)}, u32[]{:S(2)}, u32[]{:S(2)}) %collective-permute-start.8) | collective-permute-done | bytes 65568 | tf_op jit(solution)/shard_map/ppermute | solution.py:29
  15.0 0.5 %copy-done.2 = s32[1,2]{1,0:T(1,128)S(1)} copy-done((s32[1,2]{1,0:T(1,128)S(1)}, s32[1,2]{1,0:T(1,128)}, u32[]{:S(2)}) %copy-start.2) | copy-done | bytes 32
  15.5 0.9 %shard_map.37 = (f32[128,256]{1,0:T(8,128)S(1)}, f32[128,256]{1,0:T(8,128)S(1)}, f32[128,256]{1,0:T(8,128)S(1)}, f32[128,256]{1,0:T(8,128)S(1)}) custom-call(s32[1,2]{1,0:T(1,128)S(1)} %copy-done.2, s32[1,2]{1,0:T(1,128)S(1)} %collective-permute-done.other_ref, f32[1024,128]{1,0:T(8,128)S(1)} %bitcast.10, f32[1024,128]{1,0:T(8,128)S(1)} %collective-permute-done.1.par_ref), custom_call_target="tpu_custom_call" | custom-call | tf_op jit(solution)/shard_map/pallas_call | solution.py:134
  16.5 2.1 %collective-permute-start.3 = (f32[128,256]{1,0:T(8,128)S(1)}, f32[128,256]{1,0:T(8,128)S(1)}, u32[]{:S(2)}, u32[]{:S(2)}) collective-permute-start(f32[128,256]{1,0:T(8,128)S(1)} %get-tuple-element.19), channel_id=1, source_target_pairs={{0,8},{4,12},{8,0},{12,4},{1,9},{5,13},{9,1},{13,5},{2,10},{6,14},... | collective-permute-start | bytes 393224 | tf_op jit(solution)/shard_map/ppermute | solution.py:29
  18.6 2.3 %collective-permute-start.4 = (f32[128,256]{1,0:T(8,128)S(1)}, f32[128,256]{1,0:T(8,128)S(1)}, u32[]{:S(2)}, u32[]{:S(2)}) collective-permute-start(f32[128,256]{1,0:T(8,128)S(1)} %get-tuple-element.20), channel_id=1, source_target_pairs={{0,12},{4,8},{8,4},{12,0},{1,13},{5,9},{9,5},{13,1},{2,14},{6,10},... | collective-permute-start | bytes 393224 | tf_op jit(solution)/shard_map/ppermute | solution.py:29
  20.9 3.6 %collective-permute-done.2.refs_1_ = f32[128,256]{1,0:T(8,128)S(1)} collective-permute-done((f32[128,256]{1,0:T(8,128)S(1)}, f32[128,256]{1,0:T(8,128)S(1)}, u32[]{:S(2)}, u32[]{:S(2)}) %collective-permute-start.2) | collective-permute-done | bytes 131104 | tf_op jit(solution)/shard_map/ppermute | solution.py:29
  24.4 5.0 %collective-permute-done.3.refs_2_ = f32[128,256]{1,0:T(8,128)S(1)} collective-permute-done((f32[128,256]{1,0:T(8,128)S(1)}, f32[128,256]{1,0:T(8,128)S(1)}, u32[]{:S(2)}, u32[]{:S(2)}) %collective-permute-start.3) | collective-permute-done | bytes 131104 | tf_op jit(solution)/shard_map/ppermute | solution.py:29
  29.4 0.9 %shard_map.38 = (f32[64,256]{1,0:T(8,128)S(1)}, f32[64,256]{1,0:T(8,128)S(1)}, f32[64,256]{1,0:T(8,128)S(1)}, f32[64,256]{1,0:T(8,128)S(1)}) custom-call(f32[128,256]{1,0:T(8,128)S(1)} %get-tuple-element.17.refs_0_, f32[128,256]{1,0:T(8,128)S(1)} %collective-permute-done.2.refs_1_, f32[128,256]{1,0:T(8,128)S(1)} %collective-permute-done.3.refs_2_, ...), custom_call_target="tpu_custom_call" | custom-call | tf_op jit(solution)/shard_map/pallas_call | solution.py:145
  30.4 1.6 %collective-permute-start.11 = (f32[64,256]{1,0:T(8,128)S(1)}, f32[64,256]{1,0:T(8,128)S(1)}, u32[]{:S(2)}, u32[]{:S(2)}) collective-permute-start(f32[64,256]{1,0:T(8,128)S(1)} %get-tuple-element.23), channel_id=1, source_target_pairs={{0,2},{1,3},{2,0},{3,1},{4,6},{5,7},{6,4},{7,5},{8,10},{9,11},{10,... | collective-permute-start | bytes 196616 | tf_op jit(solution)/shard_map/ppermute | solution.py:29
  32.2 2.6 %collective-permute-done.11.refs_2_ = f32[64,256]{1,0:T(8,128)S(1)} collective-permute-done((f32[64,256]{1,0:T(8,128)S(1)}, f32[64,256]{1,0:T(8,128)S(1)}, u32[]{:S(2)}, u32[]{:S(2)}) %collective-permute-start.11) | collective-permute-done | bytes 65568 | tf_op jit(solution)/shard_map/ppermute | solution.py:29
  34.9 1.1 %collective-permute-done.12.refs_3_ = f32[64,256]{1,0:T(8,128)S(1)} collective-permute-done((f32[64,256]{1,0:T(8,128)S(1)}, f32[64,256]{1,0:T(8,128)S(1)}, u32[]{:S(2)}, u32[]{:S(2)}) %collective-permute-start.12) | collective-permute-done | bytes 65568 | tf_op jit(solution)/shard_map/ppermute | solution.py:29
  36.1 2.5 %collective-permute-start.13 = (f32[32,128]{1,0:T(8,128)S(1)}, f32[32,128]{1,0:T(8,128)S(1)}, u32[]{:S(2)}, u32[]{:S(2)}) collective-permute-start(f32[32,128]{1,0:T(8,128)S(1)} %get-tuple-element.26), channel_id=1, source_target_pairs={{0,4},{4,0},{8,12},{12,8},{1,5},{5,1},{9,13},{13,9},{2,6},{6,2},{1... | collective-permute-start | bytes 49160 | tf_op jit(solution)/shard_map/ppermute | solution.py:29
  38.6 1.7 %collective-permute-start.14 = (f32[32,128]{1,0:T(8,128)S(1)}, f32[32,128]{1,0:T(8,128)S(1)}, u32[]{:S(2)}, u32[]{:S(2)}) collective-permute-start(f32[32,128]{1,0:T(8,128)S(1)} %get-tuple-element.27), channel_id=1, source_target_pairs={{0,8},{4,12},{8,0},{12,4},{1,9},{5,13},{9,1},{13,5},{2,10},{6,14},... | collective-permute-start | bytes 49160 | tf_op jit(solution)/shard_map/ppermute | solution.py:29
  40.3 1.4 %collective-permute-start.15 = (f32[32,128]{1,0:T(8,128)S(1)}, f32[32,128]{1,0:T(8,128)S(1)}, u32[]{:S(2)}, u32[]{:S(2)}) collective-permute-start(f32[32,128]{1,0:T(8,128)S(1)} %get-tuple-element.28), channel_id=1, source_target_pairs={{0,12},{4,8},{8,4},{12,0},{1,13},{5,9},{9,5},{13,1},{2,14},{6,10},... | collective-permute-start | bytes 49160 | tf_op jit(solution)/shard_map/ppermute | solution.py:29
  41.7 1.6 %collective-permute-done.14.c = f32[32,128]{1,0:T(8,128)S(1)} collective-permute-done((f32[32,128]{1,0:T(8,128)S(1)}, f32[32,128]{1,0:T(8,128)S(1)}, u32[]{:S(2)}, u32[]{:S(2)}) %collective-permute-start.14) | collective-permute-done | bytes 16416 | tf_op jit(solution)/shard_map/ppermute | solution.py:29
  43.3 2.6 %collective-permute-done.15.d = f32[32,128]{1,0:T(8,128)S(1)} collective-permute-done((f32[32,128]{1,0:T(8,128)S(1)}, f32[32,128]{1,0:T(8,128)S(1)}, u32[]{:S(2)}, u32[]{:S(2)}) %collective-permute-start.15) | collective-permute-done | bytes 16416 | tf_op jit(solution)/shard_map/ppermute | solution.py:29
  45.8 0.8 %shard_map.40 = f32[64,64]{1,0:T(8,128)} custom-call(f32[32,128]{1,0:T(8,128)S(1)} %get-tuple-element.25.a, f32[32,128]{1,0:T(8,128)S(1)} %collective-permute-done.13.b, f32[32,128]{1,0:T(8,128)S(1)} %collective-permute-done.14.c, f32[32,128]{1,0:T(8,128)S(1)} %collective-permute-done.15.d), custom_call_target="tpu_custom_call" | custom-call | tf_op jit(solution)/shard_map/pallas_call | solution.py:162
  (22 shorter events, 0.7 us)
Async XLA Ops:
  0.0 0.8 %copy-start = (f32[64,256]{1,0:T(8,128)S(1)}, f32[64,256]{1,0:T(8,128)}, u32[]{:S(2)}) copy-start(f32[64,256]{1,0:T(8,128)} %param.4) | copy-start | bytes 196612
  0.0 15.0 %copy-start.1 = (f32[64,16,128]{2,1,0:T(8,128)S(1)}, f32[64,16,128]{2,1,0:T(8,128)}, u32[]{:S(2)}) copy-start(f32[64,16,128]{2,1,0:T(8,128)} %param.3) | copy-start | bytes 1572868
  0.0 15.0 %collective-permute-start.1 = (f32[1024,128]{1,0:T(8,128)}, f32[1024,128]{1,0:T(8,128)S(1)}, u32[]{:S(2)}, u32[]{:S(2)}) collective-permute-start(f32[1024,128]{1,0:T(8,128)} %bitcast.9), channel_id=1, source_target_pairs={{0,1},{1,0},{2,3},{3,2},{4,5},{5,4},{6,7},{7,6},{8,9},{9,8},{10,11... | collective-permute-start | bytes 1572872 | tf_op jit(solution)/shard_map/ppermute | solution.py:29
  0.8 6.8 %collective-permute-start.7 = (f32[16,256]{1,0:T(8,128)S(1)}, f32[16,256]{1,0:T(8,128)S(1)}, u32[]{:S(2)}, u32[]{:S(2)}) collective-permute-start(f32[16,256]{1,0:T(8,128)S(1)} %constant_dynamic-slice_fusion), channel_id=1, source_target_pairs={{0,12},{4,8},{8,4},{12,0},{1,13},{5,9},{9,5},{13,1},{2,14},{6,10},... | collective-permute-start | bytes 49160 | tf_op jit(solution)/shard_map/ppermute | solution.py:29
  5.9 4.6 %collective-permute-start.6 = (f32[16,256]{1,0:T(8,128)S(1)}, f32[16,256]{1,0:T(8,128)S(1)}, u32[]{:S(2)}, u32[]{:S(2)}) collective-permute-start(f32[16,256]{1,0:T(8,128)S(1)} %constant_dynamic-slice_fusion), channel_id=1, source_target_pairs={{0,8},{4,12},{8,0},{12,4},{1,9},{5,13},{9,1},{13,5},{2,10},{6,14},... | collective-permute-start | bytes 49160 | tf_op jit(solution)/shard_map/ppermute | solution.py:29
  5.9 4.6 %collective-permute-start.5 = (f32[16,256]{1,0:T(8,128)S(1)}, f32[16,256]{1,0:T(8,128)S(1)}, u32[]{:S(2)}, u32[]{:S(2)}) collective-permute-start(f32[16,256]{1,0:T(8,128)S(1)} %constant_dynamic-slice_fusion), channel_id=1, source_target_pairs={{0,4},{4,0},{8,12},{12,8},{1,5},{5,1},{9,13},{13,9},{2,6},{6,2},{1... | collective-permute-start | bytes 49160 | tf_op jit(solution)/shard_map/ppermute | solution.py:29
  10.5 4.3 %collective-permute-start.8 = (f32[4,16,256]{2,1,0:T(8,128)S(1)}, f32[4,16,256]{2,1,0:T(8,128)S(1)}, u32[]{:S(2)}, u32[]{:S(2)}) collective-permute-start(f32[4,16,256]{2,1,0:T(8,128)S(1)} %get-tuple-element.30), channel_id=1, source_target_pairs={{0,2},{2,0},{1,3},{3,1},{4,6},{6,4},{5,7},{7,5},{8,10},{10,8},{9,1... | collective-permute-start | bytes 196616 | tf_op jit(solution)/shard_map/ppermute | solution.py:29
  12.1 2.9 %collective-permute-start = (s32[1,2]{1,0:T(1,128)}, s32[1,2]{1,0:T(1,128)S(1)}, u32[]{:S(2)}, u32[]{:S(2)}) collective-permute-start(s32[1,2]{1,0:T(1,128)} %screen_ref.1), channel_id=1, source_target_pairs={{0,1},{1,0},{2,3},{3,2},{4,5},{5,4},{6,7},{7,6},{8,9},{9,8},{10,11... | collective-permute-start | bytes 32 | tf_op jit(solution)/shard_map/ppermute | solution.py:29
  14.9 0.7 %copy-start.2 = (s32[1,2]{1,0:T(1,128)S(1)}, s32[1,2]{1,0:T(1,128)}, u32[]{:S(2)}) copy-start(s32[1,2]{1,0:T(1,128)} %screen_ref.1) | copy-start | bytes 28
  14.9 6.0 %collective-permute-start.9 = (f32[2,4,16,256]{3,2,1,0:T(8,128)S(1)}, f32[2,4,16,256]{3,2,1,0:T(8,128)S(1)}, u32[]{:S(2)}, u32[]{:S(2)}) collective-permute-start(f32[2,4,16,256]{3,2,1,0:T(8,128)S(1)} %pad_maximum_fusion.refs_4_), channel_id=1, source_target_pairs={{0,1},{1,0},{2,3},{3,2},{4,5},{5,4},{6,7},{7,6},{8,9},{9,8},{10,11... | collective-permute-start | bytes 393224 | tf_op jit(solution)/shard_map/ppermute | solution.py:29
  16.4 8.0 %collective-permute-start.2 = (f32[128,256]{1,0:T(8,128)S(1)}, f32[128,256]{1,0:T(8,128)S(1)}, u32[]{:S(2)}, u32[]{:S(2)}) collective-permute-start(f32[128,256]{1,0:T(8,128)S(1)} %get-tuple-element.18), channel_id=1, source_target_pairs={{0,4},{4,0},{8,12},{12,8},{1,5},{5,1},{9,13},{13,9},{2,6},{6,2},{1... | collective-permute-start | bytes 393224 | tf_op jit(solution)/shard_map/ppermute | solution.py:29
  16.5 12.9 %collective-permute-start.3 = (f32[128,256]{1,0:T(8,128)S(1)}, f32[128,256]{1,0:T(8,128)S(1)}, u32[]{:S(2)}, u32[]{:S(2)}) collective-permute-start(f32[128,256]{1,0:T(8,128)S(1)} %get-tuple-element.19), channel_id=1, source_target_pairs={{0,8},{4,12},{8,0},{12,4},{1,9},{5,13},{9,1},{13,5},{2,10},{6,14},... | collective-permute-start | bytes 393224 | tf_op jit(solution)/shard_map/ppermute | solution.py:29
  18.6 10.8 %collective-permute-start.4 = (f32[128,256]{1,0:T(8,128)S(1)}, f32[128,256]{1,0:T(8,128)S(1)}, u32[]{:S(2)}, u32[]{:S(2)}) collective-permute-start(f32[128,256]{1,0:T(8,128)S(1)} %get-tuple-element.20), channel_id=1, source_target_pairs={{0,12},{4,8},{8,4},{12,0},{1,13},{5,9},{9,5},{13,1},{2,14},{6,10},... | collective-permute-start | bytes 393224 | tf_op jit(solution)/shard_map/ppermute | solution.py:29
  30.3 1.9 %collective-permute-start.10 = (f32[64,256]{1,0:T(8,128)S(1)}, f32[64,256]{1,0:T(8,128)S(1)}, u32[]{:S(2)}, u32[]{:S(2)}) collective-permute-start(f32[64,256]{1,0:T(8,128)S(1)} %get-tuple-element.22), channel_id=1, source_target_pairs={{0,1},{1,0},{2,3},{3,2},{4,5},{5,4},{6,7},{7,6},{8,9},{9,8},{10,11... | collective-permute-start | bytes 196616 | tf_op jit(solution)/shard_map/ppermute | solution.py:29
  30.4 4.5 %collective-permute-start.11 = (f32[64,256]{1,0:T(8,128)S(1)}, f32[64,256]{1,0:T(8,128)S(1)}, u32[]{:S(2)}, u32[]{:S(2)}) collective-permute-start(f32[64,256]{1,0:T(8,128)S(1)} %get-tuple-element.23), channel_id=1, source_target_pairs={{0,2},{1,3},{2,0},{3,1},{4,6},{5,7},{6,4},{7,5},{8,10},{9,11},{10,... | collective-permute-start | bytes 196616 | tf_op jit(solution)/shard_map/ppermute | solution.py:29
  31.9 4.0 %collective-permute-start.12 = (f32[64,256]{1,0:T(8,128)S(1)}, f32[64,256]{1,0:T(8,128)S(1)}, u32[]{:S(2)}, u32[]{:S(2)}) collective-permute-start(f32[64,256]{1,0:T(8,128)S(1)} %get-tuple-element.24), channel_id=1, source_target_pairs={{0,3},{1,2},{2,1},{3,0},{4,7},{5,6},{6,5},{7,4},{8,11},{9,10},{10,... | collective-permute-start | bytes 196616 | tf_op jit(solution)/shard_map/ppermute | solution.py:29
  36.1 5.6 %collective-permute-start.13 = (f32[32,128]{1,0:T(8,128)S(1)}, f32[32,128]{1,0:T(8,128)S(1)}, u32[]{:S(2)}, u32[]{:S(2)}) collective-permute-start(f32[32,128]{1,0:T(8,128)S(1)} %get-tuple-element.26), channel_id=1, source_target_pairs={{0,4},{4,0},{8,12},{12,8},{1,5},{5,1},{9,13},{13,9},{2,6},{6,2},{1... | collective-permute-start | bytes 49160 | tf_op jit(solution)/shard_map/ppermute | solution.py:29
  38.6 4.6 %collective-permute-start.14 = (f32[32,128]{1,0:T(8,128)S(1)}, f32[32,128]{1,0:T(8,128)S(1)}, u32[]{:S(2)}, u32[]{:S(2)}) collective-permute-start(f32[32,128]{1,0:T(8,128)S(1)} %get-tuple-element.27), channel_id=1, source_target_pairs={{0,8},{4,12},{8,0},{12,4},{1,9},{5,13},{9,1},{13,5},{2,10},{6,14},... | collective-permute-start | bytes 49160 | tf_op jit(solution)/shard_map/ppermute | solution.py:29
  40.3 5.5 %collective-permute-start.15 = (f32[32,128]{1,0:T(8,128)S(1)}, f32[32,128]{1,0:T(8,128)S(1)}, u32[]{:S(2)}, u32[]{:S(2)}) collective-permute-start(f32[32,128]{1,0:T(8,128)S(1)} %get-tuple-element.28), channel_id=1, source_target_pairs={{0,12},{4,8},{8,4},{12,0},{1,13},{5,9},{9,5},{13,1},{2,14},{6,10},... | collective-permute-start | bytes 49160 | tf_op jit(solution)/shard_map/ppermute | solution.py:29

commit v2 on v0

--- a/solution.py
+++ b/solution.py
@@ -1,9 +1,232 @@
+import functools
+
 import jax
 import jax.numpy as jnp
 from jax import lax
+from jax.experimental import pallas as pl
+from jax.experimental.pallas import tpu as pltpu
 from jax.sharding import PartitionSpec as P
 
 precise = lax.Precision.HIGHEST
+VMEM = pl.BlockSpec(memory_space=pltpu.VMEM)
+SMEM = pl.BlockSpec(memory_space=pltpu.SMEM)
+HBM = pl.BlockSpec(memory_space=pltpu.HBM)
+FIRST = 54272 * 1024
+F32 = jnp.float32
+BF16 = jnp.bfloat16
+
+
+def call(kernel, outs, scratch=(), ins=None, count=0, limit=12 << 20, alias={}):
+    return pl.pallas_call(
+        kernel,
+        out_shape=tuple(jax.ShapeDtypeStruct(s, F32) for s in outs),
+        in_specs=ins if ins is not None else [VMEM] * count,
+        out_specs=tuple(VMEM for _ in outs),
+        scratch_shapes=list(scratch),
+        input_output_aliases=alias,
+        compiler_params=pltpu.CompilerParams(vmem_limit_bytes=limit),
+    )
+
+
+def swap(x, axes, size, k):
+    return lax.ppermute(x, axes, [(a, a ^ k) for a in range(size)])
+
+
+def split(x):
+    high = x.astype(BF16)
+    return high, (x - high.astype(F32)).astype(BF16)
+
+
+def lanes(ref, size):
+    low = lax.broadcasted_iota(jnp.int32, (size, 128), 1) < 64
+    a, b = ref[0, 0], ref[0, 1]
+    return [jnp.where(low, a, b), jnp.where(low, b, a)]
+
+
+def spread(places, part, start):
+    size = part.shape[0]
+    turned = pltpu.roll(part, 64, 1)
+    half = jnp.where(lax.broadcasted_iota(jnp.int32, (size, 128), 1) < 64, 0, 1)
+    columns = []
+    for h, value in enumerate(start):
+        value = jnp.where(places[0] == half + 2 * h, part, value)
+        columns.append(jnp.where(places[1] == half + 2 * h, turned, value))
+    return columns
+
+
+def fold(block):
+    size = block.shape[0]
+    low = lax.broadcasted_iota(jnp.int32, (size // 2, 128), 1) < 64
+    return jnp.where(low, block[:size // 2], pltpu.roll(block, 64, 1)[size // 2:])
+
+
+def unfold(folded):
+    return jnp.concatenate([folded, pltpu.roll(folded, 64, 1)], axis=0)
+
+
+def column_block(value, b):
+    picked = value[:, :128]
+    for h in range(1, value.shape[1] // 128):
+        picked = jnp.where(b // 2 == h, value[:, h * 128:(h + 1) * 128], picked)
+    return jnp.where(b % 2 == 1, pltpu.roll(picked, 64, 1), picked)
+
+
+def near_kernel(share, screen_hbm, own_hbm, density_hbm, *refs):
+    outs, (screen_ref, own_ref, density_ref, sems) = refs[:4], refs[4:]
+    r, s = lax.axis_index("row"), lax.axis_index("sub")
+    size, orbitals = density_ref.shape
+    aux_local = own_ref.shape[0] // size
+    cut = orbitals // 128
+    pairs = ((screen_hbm, screen_ref), (density_hbm, density_ref), (own_hbm, own_ref))
+    copies = [pltpu.make_async_copy(a, b, sems.at[i]) for i, (a, b) in enumerate(pairs)]
+    for copy in copies:
+        copy.start()
+    for copy in copies:
+        copy.wait()
+    places = lanes(screen_ref, size)
+    for k, out in enumerate(outs):
+        for j in range(share):
+            p = ((r ^ k) * 2 + s) * share + j
+            part = own_ref[pl.ds(p, size, stride=aux_local), :]
+            start = [jnp.zeros((size, 128), F32)] * cut
+            for h, value in enumerate(spread(places, part, start)):
+                at = (j * cut + h) * size
+                out[at:at + size, :] = value
+    at = share * cut * size
+    density = density_ref[...]
+    for h in range(cut):
+        outs[1][at + h * size:at + (h + 1) * size, :] = density[:, h * 128:(h + 1) * 128]
+    corner = fold(column_block(density, r))
+    outs[3][at:, :] = corner
+    outs[2][at:at + size // 2, :] = corner
+    outs[2][at + size // 2:, :] = fold(column_block(density, r ^ 1))
+
+
+def far_kernel(share, size, screen_ref, par_ref, *refs):
+    ins, outs = refs[:4], refs[4:]
+    r, s = lax.axis_index("row"), lax.axis_index("sub")
+    aux_local = par_ref.shape[0] // size
+    places = lanes(screen_ref, size)
+    cut = ins[0].shape[0] // (share * size)
+    for k, (start, out) in enumerate(zip(ins, outs)):
+        for j in range(share):
+            p = ((r ^ k) * 2 + s) * share + j
+            part = par_ref[pl.ds(p, size, stride=aux_local), :]
+            spots = [slice((j * cut + h) * size, (j * cut + h + 1) * size) for h in range(cut)]
+            for spot, value in zip(spots, spread(places, part, [start[x, :] for x in spots])):
+                out[spot, :] = value
+        at = share * cut * size
+        if out.shape[0] > at:
+            out[at:, :] = start[at:, :]
+
+
+def fock_kernel(share, own, one, two, three, density, *refs):
+    outs, (dense, dh, dl, bh, bl, total) = refs[:4], refs[4:]
+    r, s = lax.axis_index("row"), lax.axis_index("sub")
+    q = lax.axis_index("aux") * 2 + s
+    size, orbitals = density.shape
+    cut = orbitals // 128
+    rows_of = lambda k: pl.ds(pl.multiple_of((r ^ k) * size, size), size)
+    half = jnp.where(lax.broadcasted_iota(jnp.int32, (size, 128), 1) < 64, 0, 1)
+
+    def complete(k, came):
+        across = jnp.transpose(column_block(dense[...], r ^ k))[:size, :]
+        came = [(column, unfold(block)) for column, block in came]
+        came = [(column, jnp.where(half == 0, block, pltpu.roll(block, 64, 1))) for column, block in came]
+        for h in range(cut):
+            value = across[:, h * 128:(h + 1) * 128]
+            for column, block in came:
+                value = jnp.where(half + 2 * h == column, block, value)
+            dense[rows_of(k), h * 128:(h + 1) * 128] = value
+
+    dense[rows_of(0), :] = density[...]
+    at = share * cut * size
+    at = share * cut * size
+    for h in range(cut):
+        dense[rows_of(1), h * 128:(h + 1) * 128] = one[at + h * size:at + (h + 1) * size, :]
+    complete(2, [(r ^ 2, two[at:at + size // 2, :]), (r ^ 3, two[at + size // 2:, :])])
+    complete(3, [(r ^ 3, three[at:, :])])
+    dh[...], dl[...] = split(dense[...])
+    for k, chunk in enumerate((own, one, two, three)):
+        for j in range(share):
+            for h in range(cut):
+                at = (j * cut + h) * size
+                high, lower = split(chunk[at:at + size, :])
+                bh[j, rows_of(k), h * 128:(h + 1) * 128] = high
+                bl[j, rows_of(k), h * 128:(h + 1) * 128] = lower
+    dot = functools.partial(jnp.dot, preferred_element_type=F32)
+    dot_t = lambda a, b: lax.dot_general(a, b, (((1,), (1,)), ((), ())), preferred_element_type=F32)
+    result = None
+    for j in range(share):
+        b1, b2 = bh[j], bl[j]
+        c = dot(b1, dh[...]) + (dot(b1, dl[...]) + dot(b2, dh[...]))
+        c1, c2 = split(c)
+        f = dot_t(c1, b1) + (dot_t(c1, b2) + dot_t(c2, b1))
+        result = f if result is None else result + f
+    total[...] = result
+    for dq in range(4):
+        outs[dq][...] = total[pl.ds(pl.multiple_of((q ^ dq) * size, size), size), :]
+
+
+def cut_kernel(*refs):
+    ins, outs = refs[:4], refs[4:]
+    r = lax.axis_index("row")
+    value = ins[0][...] + ins[1][...] + (ins[2][...] + ins[3][...])
+    for k in range(4):
+        outs[k][...] = fold(column_block(value, r ^ k))
+
+
+def final_kernel(a, b, c, d, out):
+    value = a[...] + b[...] + (c[...] + d[...])
+    out[...] = jnp.transpose(unfold(value))[:out.shape[0], :]
+
+
+def dealt_body(factor, density, screen):
+    block_size, orbitals = density.shape
+    aux_local = factor.shape[1]
+    share = aux_local // 8
+    packed = share * orbitals // 128 * block_size
+    flat = factor.reshape(block_size * aux_local, factor.shape[2])
+    row = lambda x, k: swap(x, "row", 4, k)
+    core = lambda x: swap(x, "sub", 2, 1)
+    other = core(flat)
+    shapes = [(packed + more, 128) for more in (0, orbitals // 2, block_size, block_size // 2)]
+    sent = call(
+        functools.partial(near_kernel, share),
+        shapes,
+        ins=[HBM] * 3,
+        scratch=[
+            pltpu.SMEM(screen.shape, jnp.int32),
+            pltpu.VMEM(flat.shape, F32),
+            pltpu.VMEM(density.shape, F32),
+            pltpu.SemaphoreType.DMA((3,)),
+        ],
+        limit=FIRST,
+    )(screen, flat, density)
+    sent = call(
+        functools.partial(far_kernel, share, block_size),
+        shapes,
+        ins=[SMEM] + [VMEM] * 5,
+        alias={2 + k: k for k in range(4)},
+    )(core(screen), other, *sent)
+    three, two, one = [row(sent[k], k) for k in (3, 2, 1)]
+    parts = call(
+        functools.partial(fock_kernel, share),
+        [(block_size, orbitals)] * 4,
+        scratch=[
+            pltpu.VMEM((orbitals, orbitals), F32),
+            pltpu.VMEM((orbitals, orbitals), BF16),
+            pltpu.VMEM((orbitals, orbitals), BF16),
+            pltpu.VMEM((share, orbitals, orbitals), BF16),
+            pltpu.VMEM((share, orbitals, orbitals), BF16),
+            pltpu.VMEM((orbitals, orbitals), F32),
+        ],
+        count=5,
+    )(sent[0], one, two, three, density)
+    sums = [parts[0]] + [swap(parts[k], ("aux", "sub"), 4, k) for k in (1, 2, 3)]
+    cuts = call(cut_kernel, [(block_size // 2, 2 * block_size)] * 4, count=4)(*sums)
+    last = [cuts[0]] + [row(cuts[k], k) for k in (1, 2, 3)]
+    return call(final_kernel, [(block_size, block_size)], count=4)(*last)[0]
 
 
 def pair_block(tiled, block_rows, block_cols):
@@ -17,7 +240,7 @@
     )
 
 
-def body(factor, density, screen):
+def gathered_body(factor, density, screen):
     block_size = density.shape[0]
     orbitals = density.shape[1]
     nblocks = orbitals // block_size
@@ -55,6 +278,24 @@
 
 
 def solution(mesh):
+    sizes = tuple(mesh.shape[a] for a in ("row", "aux", "sub"))
+
+    def body(factor, density, screen):
+        nrow, naux, nsub = sizes
+        block_size, orbitals = density.shape
+        fits = (
+            naux * nsub == 4
+            and nsub == 2
+            and nrow == 4
+            and block_size == 64
+            and orbitals == nrow * block_size
+            and factor.shape[2] == 128
+            and factor.shape[1] % (nrow * nsub * 2) == 0
+        )
+        if fits:
+            return dealt_body(factor, density, screen)
+        return gathered_body(factor, density, screen)
+
     return jax.shard_map(
         body,
         mesh=mesh,

time: 198 us -> 39.1 us (0.20)
  waiting for transfers between devices: 86.2 us -> 20 us
  local copies, waits for them, and re-layouts: 35.6 us -> 1.04 us
  blocking collectives: 30.1 us -> 0 us
  matrix products: 15.5 us -> 0 us
  between operations: 13.9 us -> 0.06 us
  starting transfers between devices: 3.36 us -> 13.6 us
  other arithmetic: 9.69 us -> 0 us
  Pallas kernels: 0 us -> 4.24 us
  loops' own time: 2.88 us -> 0 us
    all_gather x2 -> x0, waiting for transfers between devices: 61.6 us -> none  [the longest x1 48.3 us: body(): rows_piece = lax.all_gather(full_rows[None], 'row', axis=0, tiled=True)]
    all_gather x2 -> x0, blocking collectives: 28.3 us -> none  [the longest x1 17 us: body(): whole = lax.all_gather(density, 'row', axis=0, tiled=True)]
    ppermute x0 -> x11, waiting for transfers between devices: none -> 20 us  [swap(): return lax.ppermute(x, axes, [(a, a ^ k) for a in range(size)])]
    unnamed x4 -> x0, waiting for transfers between devices: 19 us -> none
    dot_general x5 -> x0, matrix products: 15.5 us -> none  [the longest x4 14.5 us: pair_block(): jnp.einsum('ipsl,jpsl->ij', picked, others, precision=precise, preferred_...]
    gather x5 -> x0, local copies, waits for them, and re-layouts: 15.1 us -> none  [the longest x4 14.6 us: pair_block(): picked = jnp.take(tiled, block_cols, axis=2)]
    ppermute x0 -> x11, starting transfers between devices: none -> 13.6 us  [swap(): return lax.ppermute(x, axes, [(a, a ^ k) for a in range(size)])]
    select_n x10 -> x0, other arithmetic: 8.06 us -> none  [the longest x8 7.31 us: pair_block(): picked = jnp.take(tiled, block_cols, axis=2)]
  transfers between devices with their start and end apart: 4 -> 11, of which waited for: 4 -> 6; matrix products, arithmetic and copies ran while one was open for 4% -> 0% of each run, Pallas kernels for 0% -> 3%
where the time goes in v2:
time: 39.1 us; the launch traced here: 38.9 us
  waiting for transfers between devices  20 us (51%)
  starting transfers between devices  13.6 us (35%)
  Pallas kernels  4.24 us (11%)
  local copies, waits for them, and re-layouts  1.04 us (3%)
    ppermute x11, waiting for transfers between devices, swap(): return lax.ppermute(x, axes, [(a, a ^ k) for a in range(size)])  20 us
    ppermute x11, starting transfers between devices, swap(): return lax.ppermute(x, axes, [(a, a ^ k) for a in range(size)])  13.6 us
    pallas_call x1, Pallas kernels, dealt_body(): call(functools.partial(near_kernel, share), shapes, ins=[HBM] * 3, scratc...  1.3 us
    pallas_call x1, Pallas kernels, dealt_body(): call(functools.partial(fock_kernel, share), [(block_size, orbitals)] * 4,...  1.26 us
    unnamed x4, local copies, waits for them, and re-layouts  1.04 us
  transfers between devices with their start and end apart: 11, of which 6 were waited for; matrix products, arithmetic and copies ran while one was open for 0% of the time, Pallas kernels for 3%

profile of v2, /device:TPU:0, one launch (start us, length us, event | category | flops | bytes accessed | tf_op | source)
XLA Modules:
  0.0 38.9 jit_solution(15136753549134699894)
XLA Ops:
  0.0 0.5 %collective-permute-start.1 = (f32[1024,128]{1,0:T(8,128)}, f32[1024,128]{1,0:T(8,128)S(1)}, u32[]{:S(2)}, u32[]{:S(2)}) collective-permute-start(f32[1024,128]{1,0:T(8,128)} %bitcast.1), channel_id=1, source_target_pairs={{0,1},{1,0},{2,3},{3,2},{4,5},{5,4},{6,7},{7,6},{8,9},{9,8},{10,11... | collective-permute-start | bytes 1572872 | tf_op jit(solution)/shard_map/ppermute | solution.py:32
  0.5 0.2 copy-done.1
  0.7 0.5 %collective-permute-start = (s32[1,2]{1,0:T(1,128)S(1)}, s32[1,2]{1,0:T(1,128)S(1)}, u32[]{:S(2)}, u32[]{:S(2)}) collective-permute-start(s32[1,2]{1,0:T(1,128)S(1)} %copy-done.1), channel_id=1, source_target_pairs={{0,1},{1,0},{2,3},{3,2},{4,5},{5,4},{6,7},{7,6},{8,9},{9,8},{10,11... | collective-permute-start | bytes 32 | tf_op jit(solution)/shard_map/ppermute | solution.py:32
  1.1 0.8 %copy-done = f32[64,256]{1,0:T(8,128)S(1)} copy-done((f32[64,256]{1,0:T(8,128)S(1)}, f32[64,256]{1,0:T(8,128)}, u32[]{:S(2)}) %copy-start) | copy-done | bytes 65560
  1.9 1.3 %shard_map.37 = (f32[256,128]{1,0:T(8,128)S(1)}, f32[384,128]{1,0:T(8,128)S(1)}, f32[320,128]{1,0:T(8,128)S(1)}, f32[288,128]{1,0:T(8,128)S(1)}) custom-call(s32[1,2]{1,0:T(1,128)S(1)} %copy-done.1, f32[1024,128]{1,0:T(8,128)} %bitcast.2, f32[64,256]{1,0:T(8,128)S(1)} %copy-done), custom_call_target="tpu_custom_call" | custom-call | tf_op jit(solution)/shard_map/pallas_call | solution.py:194
  3.3 0.0 collective-permute-done.screen_ref
  3.3 0.8 %shard_map.38 = (f32[256,128]{1,0:T(8,128)S(1)}, f32[384,128]{1,0:T(8,128)S(1)}, f32[320,128]{1,0:T(8,128)S(1)}, f32[288,128]{1,0:T(8,128)S(1)}) custom-call(s32[1,2]{1,0:T(1,128)S(1)} %collective-permute-done.screen_ref, f32[1024,128]{1,0:T(8,128)S(1)} %collective-permute-done.1.par_ref, ...), custom_call_target="tpu_custom_call", output_to_operand_aliasing={{0}: (2, {}), {1}: (3, {}), {2}: (4, {}), {3}: (5, {})} | custom-call | tf_op jit(solution)/shard_map/pallas_call | solution.py:206
  4.0 2.6 %collective-permute-start.2 = (f32[384,128]{1,0:T(8,128)S(1)}, f32[384,128]{1,0:T(8,128)S(1)}, u32[]{:S(2)}, u32[]{:S(2)}) collective-permute-start(f32[384,128]{1,0:T(8,128)S(1)} %get-tuple-element.26), channel_id=1, source_target_pairs={{0,4},{4,0},{8,12},{12,8},{1,5},{5,1},{9,13},{13,9},{2,6},{6,2},{1... | collective-permute-start | bytes 589832 | tf_op jit(solution)/shard_map/ppermute | solution.py:32
  6.7 2.6 %collective-permute-start.3 = (f32[320,128]{1,0:T(8,128)S(1)}, f32[320,128]{1,0:T(8,128)S(1)}, u32[]{:S(2)}, u32[]{:S(2)}) collective-permute-start(f32[320,128]{1,0:T(8,128)S(1)} %get-tuple-element.27), channel_id=1, source_target_pairs={{0,8},{4,12},{8,0},{12,4},{1,9},{5,13},{9,1},{13,5},{2,10},{6,14},... | collective-permute-start | bytes 491528 | tf_op jit(solution)/shard_map/ppermute | solution.py:32
  9.3 11.9 %collective-permute-done.4.three = f32[288,128]{1,0:T(8,128)S(1)} collective-permute-done((f32[288,128]{1,0:T(8,128)S(1)}, f32[288,128]{1,0:T(8,128)S(1)}, u32[]{:S(2)}, u32[]{:S(2)}) %collective-permute-start.4) | collective-permute-done | bytes 147488 | tf_op jit(solution)/shard_map/ppermute | solution.py:32
  21.2 0.1 collective-permute-done.3.two
  21.3 1.3 %shard_map.39 = (f32[64,256]{1,0:T(8,128)S(1)}, f32[64,256]{1,0:T(8,128)S(1)}, f32[64,256]{1,0:T(8,128)S(1)}, f32[64,256]{1,0:T(8,128)S(1)}) custom-call(f32[256,128]{1,0:T(8,128)S(1)} %get-tuple-element.25.own, f32[384,128]{1,0:T(8,128)S(1)} %collective-permute-done.2.one, f32[320,128]{1,0:T(8,128)S(1)} %collective-permute-done.3.two, ...), custom_call_target="tpu_custom_call" | custom-call | tf_op jit(solution)/shard_map/pallas_call | solution.py:213
  22.6 0.1 collective-permute-start.5
  22.7 1.6 %collective-permute-start.6 = (f32[64,256]{1,0:T(8,128)S(1)}, f32[64,256]{1,0:T(8,128)S(1)}, u32[]{:S(2)}, u32[]{:S(2)}) collective-permute-start(f32[64,256]{1,0:T(8,128)S(1)} %get-tuple-element.31), channel_id=1, source_target_pairs={{0,2},{1,3},{2,0},{3,1},{4,6},{5,7},{6,4},{7,5},{8,10},{9,11},{10,... | collective-permute-start | bytes 196616 | tf_op jit(solution)/shard_map/ppermute | solution.py:32
  24.2 0.3 collective-permute-start.7
  24.5 2.6 %collective-permute-done.6.refs_2_ = f32[64,256]{1,0:T(8,128)S(1)} collective-permute-done((f32[64,256]{1,0:T(8,128)S(1)}, f32[64,256]{1,0:T(8,128)S(1)}, u32[]{:S(2)}, u32[]{:S(2)}) %collective-permute-start.6) | collective-permute-done | bytes 65568 | tf_op jit(solution)/shard_map/ppermute | solution.py:32
  27.2 1.1 %collective-permute-done.7.refs_3_ = f32[64,256]{1,0:T(8,128)S(1)} collective-permute-done((f32[64,256]{1,0:T(8,128)S(1)}, f32[64,256]{1,0:T(8,128)S(1)}, u32[]{:S(2)}, u32[]{:S(2)}) %collective-permute-start.7) | collective-permute-done | bytes 65568 | tf_op jit(solution)/shard_map/ppermute | solution.py:32
  28.3 0.2 shard_map.40
  28.5 3.1 %collective-permute-start.8 = (f32[32,128]{1,0:T(8,128)S(1)}, f32[32,128]{1,0:T(8,128)S(1)}, u32[]{:S(2)}, u32[]{:S(2)}) collective-permute-start(f32[32,128]{1,0:T(8,128)S(1)} %get-tuple-element.34), channel_id=1, source_target_pairs={{0,4},{4,0},{8,12},{12,8},{1,5},{5,1},{9,13},{13,9},{2,6},{6,2},{1... | collective-permute-start | bytes 49160 | tf_op jit(solution)/shard_map/ppermute | solution.py:32
  31.6 1.1 %collective-permute-start.9 = (f32[32,128]{1,0:T(8,128)S(1)}, f32[32,128]{1,0:T(8,128)S(1)}, u32[]{:S(2)}, u32[]{:S(2)}) collective-permute-start(f32[32,128]{1,0:T(8,128)S(1)} %get-tuple-element.35), channel_id=1, source_target_pairs={{0,8},{4,12},{8,0},{12,4},{1,9},{5,13},{9,1},{13,5},{2,10},{6,14},... | collective-permute-start | bytes 49160 | tf_op jit(solution)/shard_map/ppermute | solution.py:32
  32.6 1.4 %collective-permute-start.10 = (f32[32,128]{1,0:T(8,128)S(1)}, f32[32,128]{1,0:T(8,128)S(1)}, u32[]{:S(2)}, u32[]{:S(2)}) collective-permute-start(f32[32,128]{1,0:T(8,128)S(1)} %get-tuple-element.36), channel_id=1, source_target_pairs={{0,12},{4,8},{8,4},{12,0},{1,13},{5,9},{9,5},{13,1},{2,14},{6,10},... | collective-permute-start | bytes 49160 | tf_op jit(solution)/shard_map/ppermute | solution.py:32
  34.0 2.2 %collective-permute-done.9.c = f32[32,128]{1,0:T(8,128)S(1)} collective-permute-done((f32[32,128]{1,0:T(8,128)S(1)}, f32[32,128]{1,0:T(8,128)S(1)}, u32[]{:S(2)}, u32[]{:S(2)}) %collective-permute-start.9) | collective-permute-done | bytes 16416 | tf_op jit(solution)/shard_map/ppermute | solution.py:32
  36.2 2.0 %collective-permute-done.10.d = f32[32,128]{1,0:T(8,128)S(1)} collective-permute-done((f32[32,128]{1,0:T(8,128)S(1)}, f32[32,128]{1,0:T(8,128)S(1)}, u32[]{:S(2)}, u32[]{:S(2)}) %collective-permute-start.10) | collective-permute-done | bytes 16416 | tf_op jit(solution)/shard_map/ppermute | solution.py:32
  38.2 0.8 %shard_map.41 = f32[64,64]{1,0:T(8,128)} custom-call(f32[32,128]{1,0:T(8,128)S(1)} %get-tuple-element.33.a, f32[32,128]{1,0:T(8,128)S(1)} %collective-permute-done.8.b, f32[32,128]{1,0:T(8,128)S(1)} %collective-permute-done.9.c, f32[32,128]{1,0:T(8,128)S(1)} %collective-permute-done.10.d), custom_call_target="tpu_custom_call" | custom-call | tf_op jit(solution)/shard_map/pallas_call | solution.py:229
  (7 shorter events, 0.0 us)
Async XLA Ops:
  0.0 0.7 %copy-start.1 = (s32[1,2]{1,0:T(1,128)S(1)}, s32[1,2]{1,0:T(1,128)}, u32[]{:S(2)}) copy-start(s32[1,2]{1,0:T(1,128)} %screen_hbm.1) | copy-start | bytes 28
  0.0 3.3 %collective-permute-start.1 = (f32[1024,128]{1,0:T(8,128)}, f32[1024,128]{1,0:T(8,128)S(1)}, u32[]{:S(2)}, u32[]{:S(2)}) collective-permute-start(f32[1024,128]{1,0:T(8,128)} %bitcast.1), channel_id=1, source_target_pairs={{0,1},{1,0},{2,3},{3,2},{4,5},{5,4},{6,7},{7,6},{8,9},{9,8},{10,11... | collective-permute-start | bytes 1572872 | tf_op jit(solution)/shard_map/ppermute | solution.py:32
  0.7 2.6 %collective-permute-start = (s32[1,2]{1,0:T(1,128)S(1)}, s32[1,2]{1,0:T(1,128)S(1)}, u32[]{:S(2)}, u32[]{:S(2)}) collective-permute-start(s32[1,2]{1,0:T(1,128)S(1)} %copy-done.1), channel_id=1, source_target_pairs={{0,1},{1,0},{2,3},{3,2},{4,5},{5,4},{6,7},{7,6},{8,9},{9,8},{10,11... | collective-permute-start | bytes 32 | tf_op jit(solution)/shard_map/ppermute | solution.py:32
  1.1 0.8 %copy-start = (f32[64,256]{1,0:T(8,128)S(1)}, f32[64,256]{1,0:T(8,128)}, u32[]{:S(2)}) copy-start(f32[64,256]{1,0:T(8,128)} %density.1) | copy-start | bytes 196612
  4.0 17.3 %collective-permute-start.2 = (f32[384,128]{1,0:T(8,128)S(1)}, f32[384,128]{1,0:T(8,128)S(1)}, u32[]{:S(2)}, u32[]{:S(2)}) collective-permute-start(f32[384,128]{1,0:T(8,128)S(1)} %get-tuple-element.26), channel_id=1, source_target_pairs={{0,4},{4,0},{8,12},{12,8},{1,5},{5,1},{9,13},{13,9},{2,6},{6,2},{1... | collective-permute-start | bytes 589832 | tf_op jit(solution)/shard_map/ppermute | solution.py:32
  6.7 14.7 %collective-permute-start.3 = (f32[320,128]{1,0:T(8,128)S(1)}, f32[320,128]{1,0:T(8,128)S(1)}, u32[]{:S(2)}, u32[]{:S(2)}) collective-permute-start(f32[320,128]{1,0:T(8,128)S(1)} %get-tuple-element.27), channel_id=1, source_target_pairs={{0,8},{4,12},{8,0},{12,4},{1,9},{5,13},{9,1},{13,5},{2,10},{6,14},... | collective-permute-start | bytes 491528 | tf_op jit(solution)/shard_map/ppermute | solution.py:32
  9.3 11.9 %collective-permute-start.4 = (f32[288,128]{1,0:T(8,128)S(1)}, f32[288,128]{1,0:T(8,128)S(1)}, u32[]{:S(2)}, u32[]{:S(2)}) collective-permute-start(f32[288,128]{1,0:T(8,128)S(1)} %get-tuple-element.28), channel_id=1, source_target_pairs={{0,12},{4,8},{8,4},{12,0},{1,13},{5,9},{9,5},{13,1},{2,14},{6,10},... | collective-permute-start | bytes 442376 | tf_op jit(solution)/shard_map/ppermute | solution.py:32
  22.6 1.9 %collective-permute-start.5 = (f32[64,256]{1,0:T(8,128)S(1)}, f32[64,256]{1,0:T(8,128)S(1)}, u32[]{:S(2)}, u32[]{:S(2)}) collective-permute-start(f32[64,256]{1,0:T(8,128)S(1)} %get-tuple-element.30), channel_id=1, source_target_pairs={{0,1},{1,0},{2,3},{3,2},{4,5},{5,4},{6,7},{7,6},{8,9},{9,8},{10,11... | collective-permute-start | bytes 196616 | tf_op jit(solution)/shard_map/ppermute | solution.py:32
  22.7 4.5 %collective-permute-start.6 = (f32[64,256]{1,0:T(8,128)S(1)}, f32[64,256]{1,0:T(8,128)S(1)}, u32[]{:S(2)}, u32[]{:S(2)}) collective-permute-start(f32[64,256]{1,0:T(8,128)S(1)} %get-tuple-element.31), channel_id=1, source_target_pairs={{0,2},{1,3},{2,0},{3,1},{4,6},{5,7},{6,4},{7,5},{8,10},{9,11},{10,... | collective-permute-start | bytes 196616 | tf_op jit(solution)/shard_map/ppermute | solution.py:32
  24.2 4.0 %collective-permute-start.7 = (f32[64,256]{1,0:T(8,128)S(1)}, f32[64,256]{1,0:T(8,128)S(1)}, u32[]{:S(2)}, u32[]{:S(2)}) collective-permute-start(f32[64,256]{1,0:T(8,128)S(1)} %get-tuple-element.32), channel_id=1, source_target_pairs={{0,3},{1,2},{2,1},{3,0},{4,7},{5,6},{6,5},{7,4},{8,11},{9,10},{10,... | collective-permute-start | bytes 196616 | tf_op jit(solution)/shard_map/ppermute | solution.py:32
  28.5 5.6 %collective-permute-start.8 = (f32[32,128]{1,0:T(8,128)S(1)}, f32[32,128]{1,0:T(8,128)S(1)}, u32[]{:S(2)}, u32[]{:S(2)}) collective-permute-start(f32[32,128]{1,0:T(8,128)S(1)} %get-tuple-element.34), channel_id=1, source_target_pairs={{0,4},{4,0},{8,12},{12,8},{1,5},{5,1},{9,13},{13,9},{2,6},{6,2},{1... | collective-permute-start | bytes 49160 | tf_op jit(solution)/shard_map/ppermute | solution.py:32
  31.6 4.6 %collective-permute-start.9 = (f32[32,128]{1,0:T(8,128)S(1)}, f32[32,128]{1,0:T(8,128)S(1)}, u32[]{:S(2)}, u32[]{:S(2)}) collective-permute-start(f32[32,128]{1,0:T(8,128)S(1)} %get-tuple-element.35), channel_id=1, source_target_pairs={{0,8},{4,12},{8,0},{12,4},{1,9},{5,13},{9,1},{13,5},{2,10},{6,14},... | collective-permute-start | bytes 49160 | tf_op jit(solution)/shard_map/ppermute | solution.py:32
  32.6 5.5 %collective-permute-start.10 = (f32[32,128]{1,0:T(8,128)S(1)}, f32[32,128]{1,0:T(8,128)S(1)}, u32[]{:S(2)}, u32[]{:S(2)}) collective-permute-start(f32[32,128]{1,0:T(8,128)S(1)} %get-tuple-element.36), channel_id=1, source_target_pairs={{0,12},{4,8},{8,4},{12,0},{1,13},{5,9},{9,5},{13,1},{2,14},{6,10},... | collective-permute-start | bytes 49160 | tf_op jit(solution)/shard_map/ppermute | solution.py:32

commit v3 on v2

--- a/solution.py
+++ b/solution.py
@@ -9,7 +9,6 @@
 
 precise = lax.Precision.HIGHEST
 VMEM = pl.BlockSpec(memory_space=pltpu.VMEM)
-SMEM = pl.BlockSpec(memory_space=pltpu.SMEM)
 HBM = pl.BlockSpec(memory_space=pltpu.HBM)
 FIRST = 54272 * 1024
 F32 = jnp.float32
@@ -39,7 +38,7 @@
 
 def lanes(ref, size):
     low = lax.broadcasted_iota(jnp.int32, (size, 128), 1) < 64
-    a, b = ref[0, 0], ref[0, 1]
+    a, b = [jnp.broadcast_to(ref[0:1, i:i + 1], (size, 128)) for i in range(2)]
     return [jnp.where(low, a, b), jnp.where(low, b, a)]
 
 
@@ -64,50 +63,48 @@
     return jnp.concatenate([folded, pltpu.roll(folded, 64, 1)], axis=0)
 
 
+def half_of(value, h):
+    return jnp.where(h == 0, value[:, :128], value[:, 128:])
+
+
 def column_block(value, b):
-    picked = value[:, :128]
-    for h in range(1, value.shape[1] // 128):
-        picked = jnp.where(b // 2 == h, value[:, h * 128:(h + 1) * 128], picked)
+    picked = half_of(value, b // 2)
     return jnp.where(b % 2 == 1, pltpu.roll(picked, 64, 1), picked)
 
 
-def near_kernel(share, screen_hbm, own_hbm, density_hbm, *refs):
-    outs, (screen_ref, own_ref, density_ref, sems) = refs[:4], refs[4:]
+def near_kernel(share, size, screen_hbm, own_hbm, *refs):
+    outs, (screen_ref, own_ref, sems) = refs[:4], refs[4:]
+    r, s = lax.axis_index("row"), lax.axis_index("sub")
+    aux_local = own_ref.shape[0] // size
+    cut = outs[0].shape[0] // (share * size)
+    part_size = size // 2
+    length = part_size * aux_local
+    halves = [pl.ds(i * length, length) for i in range(2)]
+    copies = [pltpu.make_async_copy(screen_hbm, screen_ref, sems.at[2])]
+    copies += [pltpu.make_async_copy(own_hbm.at[x], own_ref.at[x], sems.at[i]) for i, x in enumerate(halves)]
+    for copy in copies:
+        copy.start()
+    copies[0].wait()
+    places = lanes(screen_ref, part_size)
+    for i in range(2):
+        copies[1 + i].wait()
+        for k, out in enumerate(outs):
+            for j in range(share):
+                p = ((r ^ k) * 2 + s) * share + j + i * length
+                part = own_ref[pl.ds(p, part_size, stride=aux_local), :]
+                start = [jnp.zeros((part_size, 128), F32)] * cut
+                for h, value in enumerate(spread(places, part, start)):
+                    at = (j * cut + h) * size + i * part_size
+                    out[at:at + part_size, :] = value
+
+
+def far_kernel(share, screen_ref, par_ref, density_ref, *refs):
+    ins, outs = refs[:4], refs[4:]
     r, s = lax.axis_index("row"), lax.axis_index("sub")
     size, orbitals = density_ref.shape
-    aux_local = own_ref.shape[0] // size
-    cut = orbitals // 128
-    pairs = ((screen_hbm, screen_ref), (density_hbm, density_ref), (own_hbm, own_ref))
-    copies = [pltpu.make_async_copy(a, b, sems.at[i]) for i, (a, b) in enumerate(pairs)]
-    for copy in copies:
-        copy.start()
-    for copy in copies:
-        copy.wait()
-    places = lanes(screen_ref, size)
-    for k, out in enumerate(outs):
-        for j in range(share):
-            p = ((r ^ k) * 2 + s) * share + j
-            part = own_ref[pl.ds(p, size, stride=aux_local), :]
-            start = [jnp.zeros((size, 128), F32)] * cut
-            for h, value in enumerate(spread(places, part, start)):
-                at = (j * cut + h) * size
-                out[at:at + size, :] = value
-    at = share * cut * size
-    density = density_ref[...]
-    for h in range(cut):
-        outs[1][at + h * size:at + (h + 1) * size, :] = density[:, h * 128:(h + 1) * 128]
-    corner = fold(column_block(density, r))
-    outs[3][at:, :] = corner
-    outs[2][at:at + size // 2, :] = corner
-    outs[2][at + size // 2:, :] = fold(column_block(density, r ^ 1))
-
-
-def far_kernel(share, size, screen_ref, par_ref, *refs):
-    ins, outs = refs[:4], refs[4:]
-    r, s = lax.axis_index("row"), lax.axis_index("sub")
     aux_local = par_ref.shape[0] // size
     places = lanes(screen_ref, size)
-    cut = ins[0].shape[0] // (share * size)
+    cut = orbitals // 128
     for k, (start, out) in enumerate(zip(ins, outs)):
         for j in range(share):
             p = ((r ^ k) * 2 + s) * share + j
@@ -115,45 +112,55 @@
             spots = [slice((j * cut + h) * size, (j * cut + h + 1) * size) for h in range(cut)]
             for spot, value in zip(spots, spread(places, part, [start[x, :] for x in spots])):
                 out[spot, :] = value
-        at = share * cut * size
-        if out.shape[0] > at:
-            out[at:, :] = start[at:, :]
+    at = share * cut * size
+    density = density_ref[...]
+    for h in range(cut):
+        outs[1][at + h * size:at + (h + 1) * size, :] = density[:, h * 128:(h + 1) * 128]
+    outs[2][at:, :] = half_of(density, r // 2)
+    outs[3][at:, :] = fold(column_block(density, r))
 
 
 def fock_kernel(share, own, one, two, three, density, *refs):
-    outs, (dense, dh, dl, bh, bl, total) = refs[:4], refs[4:]
-    r, s = lax.axis_index("row"), lax.axis_index("sub")
-    q = lax.axis_index("aux") * 2 + s
+    outs, (dh, dl, bh, bl, total) = refs[:4], refs[4:]
+    r = lax.axis_index("row")
+    q = lax.axis_index("aux") * 2 + lax.axis_index("sub")
     size, orbitals = density.shape
     cut = orbitals // 128
+    h, odd = r // 2, r % 2 == 1
     rows_of = lambda k: pl.ds(pl.multiple_of((r ^ k) * size, size), size)
-    half = jnp.where(lax.broadcasted_iota(jnp.int32, (size, 128), 1) < 64, 0, 1)
-
-    def complete(k, came):
-        across = jnp.transpose(column_block(dense[...], r ^ k))[:size, :]
-        came = [(column, unfold(block)) for column, block in came]
-        came = [(column, jnp.where(half == 0, block, pltpu.roll(block, 64, 1))) for column, block in came]
-        for h in range(cut):
-            value = across[:, h * 128:(h + 1) * 128]
-            for column, block in came:
-                value = jnp.where(half + 2 * h == column, block, value)
-            dense[rows_of(k), h * 128:(h + 1) * 128] = value
-
-    dense[rows_of(0), :] = density[...]
     at = share * cut * size
-    at = share * cut * size
-    for h in range(cut):
-        dense[rows_of(1), h * 128:(h + 1) * 128] = one[at + h * size:at + (h + 1) * size, :]
-    complete(2, [(r ^ 2, two[at:at + size // 2, :]), (r ^ 3, two[at + size // 2:, :])])
-    complete(3, [(r ^ 3, three[at:, :])])
-    dh[...], dl[...] = split(dense[...])
+
+    def keep(k, left, right):
+        for x, value in enumerate((left, right)):
+            high, lower = split(value)
+            dh[rows_of(k), x * 128:(x + 1) * 128] = high
+            dl[rows_of(k), x * 128:(x + 1) * 128] = lower
+
+    mine = [density[:, x * 128:(x + 1) * 128] for x in range(2)]
+    beside = [one[at + x * size:at + (x + 1) * size, :] for x in range(2)]
+    keep(0, *mine)
+    keep(1, *beside)
+    a, b = [jnp.where(h == 0, x[1], x[0]) for x in (mine, beside)]
+    across = jnp.transpose(jnp.concatenate([jnp.where(odd, b, a), jnp.where(odd, a, b)], axis=0))
+    here = two[at:at + size, :]
+    mirror = jnp.transpose(jnp.concatenate([here, here], axis=0))
+    mirror = jnp.where(odd, mirror[:size], mirror[size:])
+    corner = unfold(three[at:, :])
+    corner = jnp.where(odd, corner, pltpu.roll(corner, 64, 1))
+    low = lax.broadcasted_iota(jnp.int32, (size, 128), 1) < 64
+    last = jnp.where(low ^ odd, mirror, corner)
+    for k, inner, outer in (
+        (2, here, jnp.where(odd, across[size:], across[:size])),
+        (3, last, jnp.where(odd, across[:size], across[size:])),
+    ):
+        keep(k, jnp.where(h == 0, outer, inner), jnp.where(h == 0, inner, outer))
     for k, chunk in enumerate((own, one, two, three)):
         for j in range(share):
-            for h in range(cut):
-                at = (j * cut + h) * size
+            for x in range(cut):
+                at = (j * cut + x) * size
                 high, lower = split(chunk[at:at + size, :])
-                bh[j, rows_of(k), h * 128:(h + 1) * 128] = high
-                bl[j, rows_of(k), h * 128:(h + 1) * 128] = lower
+                bh[j, rows_of(k), x * 128:(x + 1) * 128] = high
+                bl[j, rows_of(k), x * 128:(x + 1) * 128] = lower
     dot = functools.partial(jnp.dot, preferred_element_type=F32)
     dot_t = lambda a, b: lax.dot_general(a, b, (((1,), (1,)), ((), ())), preferred_element_type=F32)
     result = None
@@ -172,13 +179,20 @@
     ins, outs = refs[:4], refs[4:]
     r = lax.axis_index("row")
     value = ins[0][...] + ins[1][...] + (ins[2][...] + ins[3][...])
+    half = value.shape[0] // 2
     for k in range(4):
-        outs[k][...] = fold(column_block(value, r ^ k))
-
-
-def final_kernel(a, b, c, d, out):
-    value = a[...] + b[...] + (c[...] + d[...])
-    out[...] = jnp.transpose(unfold(value))[:out.shape[0], :]
+        outs[k % 2][k // 2 * half:(k // 2 + 1) * half, :] = fold(column_block(value, r ^ k))
+
+
+def merge_kernel(kept, came, out, away):
+    value = kept[...] + came[...]
+    half = out.shape[0]
+    out[...] = value[:half]
+    away[...] = value[half:]
+
+
+def final_kernel(kept, came, out):
+    out[...] = jnp.transpose(unfold(kept[...] + came[...]))[:out.shape[0], :]
 
 
 def dealt_body(factor, density, screen):
@@ -192,29 +206,27 @@
     other = core(flat)
     shapes = [(packed + more, 128) for more in (0, orbitals // 2, block_size, block_size // 2)]
     sent = call(
-        functools.partial(near_kernel, share),
+        functools.partial(near_kernel, share, block_size),
         shapes,
-        ins=[HBM] * 3,
+        ins=[HBM] * 2,
         scratch=[
-            pltpu.SMEM(screen.shape, jnp.int32),
+            pltpu.VMEM(screen.shape, jnp.int32),
             pltpu.VMEM(flat.shape, F32),
-            pltpu.VMEM(density.shape, F32),
             pltpu.SemaphoreType.DMA((3,)),
         ],
         limit=FIRST,
-    )(screen, flat, density)
+    )(screen, flat)
     sent = call(
-        functools.partial(far_kernel, share, block_size),
+        functools.partial(far_kernel, share),
         shapes,
-        ins=[SMEM] + [VMEM] * 5,
-        alias={2 + k: k for k in range(4)},
-    )(core(screen), other, *sent)
+        count=7,
+        alias={3 + k: k for k in range(4)},
+    )(core(screen), other, density, *sent)
     three, two, one = [row(sent[k], k) for k in (3, 2, 1)]
     parts = call(
         functools.partial(fock_kernel, share),
         [(block_size, orbitals)] * 4,
         scratch=[
-            pltpu.VMEM((orbitals, orbitals), F32),
             pltpu.VMEM((orbitals, orbitals), BF16),
             pltpu.VMEM((orbitals, orbitals), BF16),
             pltpu.VMEM((share, orbitals, orbitals), BF16),
@@ -224,9 +236,9 @@
         count=5,
     )(sent[0], one, two, three, density)
     sums = [parts[0]] + [swap(parts[k], ("aux", "sub"), 4, k) for k in (1, 2, 3)]
-    cuts = call(cut_kernel, [(block_size // 2, 2 * block_size)] * 4, count=4)(*sums)
-    last = [cuts[0]] + [row(cuts[k], k) for k in (1, 2, 3)]
-    return call(final_kernel, [(block_size, block_size)], count=4)(*last)[0]
+    kept, away = call(cut_kernel, [(block_size, 2 * block_size)] * 2, count=4)(*sums)
+    kept, away = call(merge_kernel, [(block_size // 2, 2 * block_size)] * 2, count=2)(kept, row(away, 1))
+    return call(final_kernel, [(block_size, block_size)], count=2)(kept, row(away, 2))[0]
 
 
 def pair_block(tiled, block_rows, block_cols):

time: 39.1 us -> 37.4 us (0.957)
  Pallas kernels: 4.24 us -> 3.35 us
  local copies, waits for them, and re-layouts: 1.04 us -> 0.2 us
  waiting for transfers between devices: 20 us -> 19.4 us
  starting transfers between devices: 13.6 us -> 14.2 us
    unnamed x4, local copies, waits for them, and re-layouts: 1.04 us -> 0.2 us
    pallas_call x4 -> x5, Pallas kernels: 2.98 us -> 2.32 us  [the longest x1 1.2 us: dealt_body(): call(functools.partial(near_kernel, share, block_size), shapes, ins=[HBM]...]
    ppermute x11 -> x10, starting transfers between devices: 13.6 us -> 14.2 us  [swap(): return lax.ppermute(x, axes, [(a, a ^ k) for a in range(size)])]
    ppermute x11 -> x10, waiting for transfers between devices: 20 us -> 19.4 us  [swap(): return lax.ppermute(x, axes, [(a, a ^ k) for a in range(size)])]
  transfers between devices with their start and end apart: 11 -> 10, of which waited for: 6 -> 6; matrix products, arithmetic and copies ran while one was open for 0% -> 0% of each run, Pallas kernels for 3% -> 3%
where the time goes in v3:
time: 37.4 us; the launch traced here: 37.2 us
  waiting for transfers between devices  19.4 us (52%)
  starting transfers between devices  14.2 us (38%)
  Pallas kernels  3.35 us (9%)
    ppermute x10, waiting for transfers between devices, swap(): return lax.ppermute(x, axes, [(a, a ^ k) for a in range(size)])  19.4 us
    ppermute x10, starting transfers between devices, swap(): return lax.ppermute(x, axes, [(a, a ^ k) for a in range(size)])  14.2 us
    pallas_call x1, Pallas kernels, dealt_body(): call(functools.partial(near_kernel, share, block_size), shapes, ins=[HBM]...  1.2 us
    pallas_call x1, Pallas kernels, dealt_body(): call(functools.partial(fock_kernel, share), [(block_size, orbitals)] * 4,...  1.03 us
    pallas_call x1, Pallas kernels, dealt_body(): call(final_kernel, [(block_size, block_size)], count=2)(kept, row(away, 2))  0.76 us
  transfers between devices with their start and end apart: 10, of which 6 were waited for; matrix products, arithmetic and copies ran while one was open for 0% of the time, Pallas kernels for 3%

profile of v3, /device:TPU:0, one launch (start us, length us, event | category | flops | bytes accessed | tf_op | source)
XLA Modules:
  0.0 37.2 jit_solution(12118105957639412921)
XLA Ops:
  0.0 0.5 %collective-permute-start.1 = (f32[1024,128]{1,0:T(8,128)}, f32[1024,128]{1,0:T(8,128)S(1)}, u32[]{:S(2)}, u32[]{:S(2)}) collective-permute-start(f32[1024,128]{1,0:T(8,128)} %bitcast.1), channel_id=1, source_target_pairs={{0,1},{1,0},{2,3},{3,2},{4,5},{5,4},{6,7},{7,6},{8,9},{9,8},{10,11... | collective-permute-start | bytes 1572872 | tf_op jit(solution)/shard_map/ppermute | solution.py:31
  0.5 0.2 copy-done.1
  0.7 0.5 %collective-permute-start = (s32[1,2]{1,0:T(1,128)S(1)}, s32[1,2]{1,0:T(1,128)S(1)}, u32[]{:S(2)}, u32[]{:S(2)}) collective-permute-start(s32[1,2]{1,0:T(1,128)S(1)} %copy-done.1), channel_id=1, source_target_pairs={{0,1},{1,0},{2,3},{3,2},{4,5},{5,4},{6,7},{7,6},{8,9},{9,8},{10,11... | collective-permute-start | bytes 32 | tf_op jit(solution)/shard_map/ppermute | solution.py:31
  1.1 1.2 %shard_map.37 = (f32[256,128]{1,0:T(8,128)S(1)}, f32[384,128]{1,0:T(8,128)S(1)}, f32[320,128]{1,0:T(8,128)S(1)}, f32[288,128]{1,0:T(8,128)S(1)}) custom-call(s32[1,2]{1,0:T(1,128)S(1)} %copy-done.1, f32[1024,128]{1,0:T(8,128)} %bitcast.2), custom_call_target="tpu_custom_call" | custom-call | tf_op jit(solution)/shard_map/pallas_call | solution.py:208
  2.3 0.0 collective-permute-done.1.par_ref
  2.3 0.2 shard_map.38
  2.6 2.9 %collective-permute-start.2 = (f32[384,128]{1,0:T(8,128)S(1)}, f32[384,128]{1,0:T(8,128)S(1)}, u32[]{:S(2)}, u32[]{:S(2)}) collective-permute-start(f32[384,128]{1,0:T(8,128)S(1)} %get-tuple-element.26), channel_id=1, source_target_pairs={{0,4},{4,0},{8,12},{12,8},{1,5},{5,1},{9,13},{13,9},{2,6},{6,2},{1... | collective-permute-start | bytes 589832 | tf_op jit(solution)/shard_map/ppermute | solution.py:31
  5.4 2.6 %collective-permute-start.3 = (f32[320,128]{1,0:T(8,128)S(1)}, f32[320,128]{1,0:T(8,128)S(1)}, u32[]{:S(2)}, u32[]{:S(2)}) collective-permute-start(f32[320,128]{1,0:T(8,128)S(1)} %get-tuple-element.27), channel_id=1, source_target_pairs={{0,8},{4,12},{8,0},{12,4},{1,9},{5,13},{9,1},{13,5},{2,10},{6,14},... | collective-permute-start | bytes 491528 | tf_op jit(solution)/shard_map/ppermute | solution.py:31
  8.0 0.0 collective-permute-start.4
  8.0 11.7 %collective-permute-done.4.three = f32[288,128]{1,0:T(8,128)S(1)} collective-permute-done((f32[288,128]{1,0:T(8,128)S(1)}, f32[288,128]{1,0:T(8,128)S(1)}, u32[]{:S(2)}, u32[]{:S(2)}) %collective-permute-start.4) | collective-permute-done | bytes 147488 | tf_op jit(solution)/shard_map/ppermute | solution.py:31
  19.7 0.4 %collective-permute-done.3.two = f32[320,128]{1,0:T(8,128)S(1)} collective-permute-done((f32[320,128]{1,0:T(8,128)S(1)}, f32[320,128]{1,0:T(8,128)S(1)}, u32[]{:S(2)}, u32[]{:S(2)}) %collective-permute-start.3) | collective-permute-done | bytes 163872 | tf_op jit(solution)/shard_map/ppermute | solution.py:31
  20.1 0.0 collective-permute-done.2.one
  20.1 1.0 %shard_map.39 = (f32[64,256]{1,0:T(8,128)S(1)}, f32[64,256]{1,0:T(8,128)S(1)}, f32[64,256]{1,0:T(8,128)S(1)}, f32[64,256]{1,0:T(8,128)S(1)}) custom-call(f32[256,128]{1,0:T(8,128)S(1)} %get-tuple-element.25.own, f32[384,128]{1,0:T(8,128)S(1)} %collective-permute-done.2.one, f32[320,128]{1,0:T(8,128)S(1)} %collective-permute-done.3.two, ...), custom_call_target="tpu_custom_call" | custom-call | tf_op jit(solution)/shard_map/pallas_call | solution.py:226
  21.1 0.1 collective-permute-start.5
  21.2 1.6 %collective-permute-start.6 = (f32[64,256]{1,0:T(8,128)S(1)}, f32[64,256]{1,0:T(8,128)S(1)}, u32[]{:S(2)}, u32[]{:S(2)}) collective-permute-start(f32[64,256]{1,0:T(8,128)S(1)} %get-tuple-element.31), channel_id=1, source_target_pairs={{0,2},{1,3},{2,0},{3,1},{4,6},{5,7},{6,4},{7,5},{8,10},{9,11},{10,... | collective-permute-start | bytes 196616 | tf_op jit(solution)/shard_map/ppermute | solution.py:31
  22.8 0.3 collective-permute-start.7
  23.1 2.6 %collective-permute-done.6.refs_2_ = f32[64,256]{1,0:T(8,128)S(1)} collective-permute-done((f32[64,256]{1,0:T(8,128)S(1)}, f32[64,256]{1,0:T(8,128)S(1)}, u32[]{:S(2)}, u32[]{:S(2)}) %collective-permute-start.6) | collective-permute-done | bytes 65568 | tf_op jit(solution)/shard_map/ppermute | solution.py:31
  25.7 1.1 %collective-permute-done.7.refs_3_ = f32[64,256]{1,0:T(8,128)S(1)} collective-permute-done((f32[64,256]{1,0:T(8,128)S(1)}, f32[64,256]{1,0:T(8,128)S(1)}, u32[]{:S(2)}, u32[]{:S(2)}) %collective-permute-start.7) | collective-permute-done | bytes 65568 | tf_op jit(solution)/shard_map/ppermute | solution.py:31
  26.8 0.2 shard_map.40
  27.0 2.8 %collective-permute-start.8 = (f32[64,128]{1,0:T(8,128)S(1)}, f32[64,128]{1,0:T(8,128)S(1)}, u32[]{:S(2)}, u32[]{:S(2)}) collective-permute-start(f32[64,128]{1,0:T(8,128)S(1)} %get-tuple-element.34), channel_id=1, source_target_pairs={{0,4},{4,0},{8,12},{12,8},{1,5},{5,1},{9,13},{13,9},{2,6},{6,2},{1... | collective-permute-start | bytes 98312 | tf_op jit(solution)/shard_map/ppermute | solution.py:31
  29.8 1.9 %collective-permute-done.8.came = f32[64,128]{1,0:T(8,128)S(1)} collective-permute-done((f32[64,128]{1,0:T(8,128)S(1)}, f32[64,128]{1,0:T(8,128)S(1)}, u32[]{:S(2)}, u32[]{:S(2)}) %collective-permute-start.8) | collective-permute-done | bytes 32800 | tf_op jit(solution)/shard_map/ppermute | solution.py:31
  31.7 3.0 %collective-permute-start.9 = (f32[32,128]{1,0:T(8,128)S(1)}, f32[32,128]{1,0:T(8,128)S(1)}, u32[]{:S(2)}, u32[]{:S(2)}) collective-permute-start(f32[32,128]{1,0:T(8,128)S(1)} %get-tuple-element.36), channel_id=1, source_target_pairs={{0,8},{4,12},{8,0},{12,4},{1,9},{5,13},{9,1},{13,5},{2,10},{6,14},... | collective-permute-start | bytes 49160 | tf_op jit(solution)/shard_map/ppermute | solution.py:31
  34.8 1.7 %collective-permute-done.9.came = f32[32,128]{1,0:T(8,128)S(1)} collective-permute-done((f32[32,128]{1,0:T(8,128)S(1)}, f32[32,128]{1,0:T(8,128)S(1)}, u32[]{:S(2)}, u32[]{:S(2)}) %collective-permute-start.9) | collective-permute-done | bytes 16416 | tf_op jit(solution)/shard_map/ppermute | solution.py:31
  36.5 0.8 %shard_map.42 = f32[64,64]{1,0:T(8,128)} custom-call(f32[32,128]{1,0:T(8,128)S(1)} %get-tuple-element.35.kept, f32[32,128]{1,0:T(8,128)S(1)} %collective-permute-done.9.came), custom_call_target="tpu_custom_call" | custom-call | tf_op jit(solution)/shard_map/pallas_call | solution.py:241
  (6 shorter events, 0.0 us)
Async XLA Ops:
  0.0 0.7 %copy-start.1 = (s32[1,2]{1,0:T(1,128)S(1)}, s32[1,2]{1,0:T(1,128)}, u32[]{:S(2)}) copy-start(s32[1,2]{1,0:T(1,128)} %screen_hbm.1) | copy-start | bytes 28
  0.0 2.3 %copy-start = (f32[64,256]{1,0:T(8,128)S(1)}, f32[64,256]{1,0:T(8,128)}, u32[]{:S(2)}) copy-start(f32[64,256]{1,0:T(8,128)} %density.1) | copy-start | bytes 196612
  0.0 2.3 %collective-permute-start.1 = (f32[1024,128]{1,0:T(8,128)}, f32[1024,128]{1,0:T(8,128)S(1)}, u32[]{:S(2)}, u32[]{:S(2)}) collective-permute-start(f32[1024,128]{1,0:T(8,128)} %bitcast.1), channel_id=1, source_target_pairs={{0,1},{1,0},{2,3},{3,2},{4,5},{5,4},{6,7},{7,6},{8,9},{9,8},{10,11... | collective-permute-start | bytes 1572872 | tf_op jit(solution)/shard_map/ppermute | solution.py:31
  0.7 1.7 %collective-permute-start = (s32[1,2]{1,0:T(1,128)S(1)}, s32[1,2]{1,0:T(1,128)S(1)}, u32[]{:S(2)}, u32[]{:S(2)}) collective-permute-start(s32[1,2]{1,0:T(1,128)S(1)} %copy-done.1), channel_id=1, source_target_pairs={{0,1},{1,0},{2,3},{3,2},{4,5},{5,4},{6,7},{7,6},{8,9},{9,8},{10,11... | collective-permute-start | bytes 32 | tf_op jit(solution)/shard_map/ppermute | solution.py:31
  2.6 17.5 %collective-permute-start.2 = (f32[384,128]{1,0:T(8,128)S(1)}, f32[384,128]{1,0:T(8,128)S(1)}, u32[]{:S(2)}, u32[]{:S(2)}) collective-permute-start(f32[384,128]{1,0:T(8,128)S(1)} %get-tuple-element.26), channel_id=1, source_target_pairs={{0,4},{4,0},{8,12},{12,8},{1,5},{5,1},{9,13},{13,9},{2,6},{6,2},{1... | collective-permute-start | bytes 589832 | tf_op jit(solution)/shard_map/ppermute | solution.py:31
  5.4 14.7 %collective-permute-start.3 = (f32[320,128]{1,0:T(8,128)S(1)}, f32[320,128]{1,0:T(8,128)S(1)}, u32[]{:S(2)}, u32[]{:S(2)}) collective-permute-start(f32[320,128]{1,0:T(8,128)S(1)} %get-tuple-element.27), channel_id=1, source_target_pairs={{0,8},{4,12},{8,0},{12,4},{1,9},{5,13},{9,1},{13,5},{2,10},{6,14},... | collective-permute-start | bytes 491528 | tf_op jit(solution)/shard_map/ppermute | solution.py:31
  8.0 11.7 %collective-permute-start.4 = (f32[288,128]{1,0:T(8,128)S(1)}, f32[288,128]{1,0:T(8,128)S(1)}, u32[]{:S(2)}, u32[]{:S(2)}) collective-permute-start(f32[288,128]{1,0:T(8,128)S(1)} %get-tuple-element.28), channel_id=1, source_target_pairs={{0,12},{4,8},{8,4},{12,0},{1,13},{5,9},{9,5},{13,1},{2,14},{6,10},... | collective-permute-start | bytes 442376 | tf_op jit(solution)/shard_map/ppermute | solution.py:31
  21.1 1.9 %collective-permute-start.5 = (f32[64,256]{1,0:T(8,128)S(1)}, f32[64,256]{1,0:T(8,128)S(1)}, u32[]{:S(2)}, u32[]{:S(2)}) collective-permute-start(f32[64,256]{1,0:T(8,128)S(1)} %get-tuple-element.30), channel_id=1, source_target_pairs={{0,1},{1,0},{2,3},{3,2},{4,5},{5,4},{6,7},{7,6},{8,9},{9,8},{10,11... | collective-permute-start | bytes 196616 | tf_op jit(solution)/shard_map/ppermute | solution.py:31
  21.2 4.5 %collective-permute-start.6 = (f32[64,256]{1,0:T(8,128)S(1)}, f32[64,256]{1,0:T(8,128)S(1)}, u32[]{:S(2)}, u32[]{:S(2)}) collective-permute-start(f32[64,256]{1,0:T(8,128)S(1)} %get-tuple-element.31), channel_id=1, source_target_pairs={{0,2},{1,3},{2,0},{3,1},{4,6},{5,7},{6,4},{7,5},{8,10},{9,11},{10,... | collective-permute-start | bytes 196616 | tf_op jit(solution)/shard_map/ppermute | solution.py:31
  22.8 4.0 %collective-permute-start.7 = (f32[64,256]{1,0:T(8,128)S(1)}, f32[64,256]{1,0:T(8,128)S(1)}, u32[]{:S(2)}, u32[]{:S(2)}) collective-permute-start(f32[64,256]{1,0:T(8,128)S(1)} %get-tuple-element.32), channel_id=1, source_target_pairs={{0,3},{1,2},{2,1},{3,0},{4,7},{5,6},{6,5},{7,4},{8,11},{9,10},{10,... | collective-permute-start | bytes 196616 | tf_op jit(solution)/shard_map/ppermute | solution.py:31
  27.0 4.7 %collective-permute-start.8 = (f32[64,128]{1,0:T(8,128)S(1)}, f32[64,128]{1,0:T(8,128)S(1)}, u32[]{:S(2)}, u32[]{:S(2)}) collective-permute-start(f32[64,128]{1,0:T(8,128)S(1)} %get-tuple-element.34), channel_id=1, source_target_pairs={{0,4},{4,0},{8,12},{12,8},{1,5},{5,1},{9,13},{13,9},{2,6},{6,2},{1... | collective-permute-start | bytes 98312 | tf_op jit(solution)/shard_map/ppermute | solution.py:31
  31.7 4.7 %collective-permute-start.9 = (f32[32,128]{1,0:T(8,128)S(1)}, f32[32,128]{1,0:T(8,128)S(1)}, u32[]{:S(2)}, u32[]{:S(2)}) collective-permute-start(f32[32,128]{1,0:T(8,128)S(1)} %get-tuple-element.36), channel_id=1, source_target_pairs={{0,8},{4,12},{8,0},{12,4},{1,9},{5,13},{9,1},{13,5},{2,10},{6,14},... | collective-permute-start | bytes 49160 | tf_op jit(solution)/shard_map/ppermute | solution.py:31

commit v4 on v3

--- a/solution.py
+++ b/solution.py
@@ -48,8 +48,9 @@
     half = jnp.where(lax.broadcasted_iota(jnp.int32, (size, 128), 1) < 64, 0, 1)
     columns = []
     for h, value in enumerate(start):
-        value = jnp.where(places[0] == half + 2 * h, part, value)
-        columns.append(jnp.where(places[1] == half + 2 * h, turned, value))
+        block = (half + 2 * h).astype(places[0].dtype)
+        value = jnp.where(places[0] == block, part, value)
+        columns.append(jnp.where(places[1] == block, turned, value))
     return columns
 
 
@@ -73,7 +74,7 @@
 
 
 def near_kernel(share, size, screen_hbm, own_hbm, *refs):
-    outs, (screen_ref, own_ref, sems) = refs[:4], refs[4:]
+    raw, outs, (screen_ref, own_ref, sems) = refs[0], refs[1:4], refs[4:]
     r, s = lax.axis_index("row"), lax.axis_index("sub")
     aux_local = own_ref.shape[0] // size
     cut = outs[0].shape[0] // (share * size)
@@ -86,9 +87,16 @@
         copy.start()
     copies[0].wait()
     places = lanes(screen_ref, part_size)
+    even = lax.broadcasted_iota(jnp.int32, (8, 128), 0) % 2 == 0
+    raw[2 * share * size:, :] = jnp.where(even, places[0][:8], places[1][:8]).astype(F32)
     for i in range(2):
         copies[1 + i].wait()
-        for k, out in enumerate(outs):
+        for d in range(2):
+            for j in range(share):
+                p = ((r ^ 2) * 2 + (s ^ d)) * share + j + i * length
+                at = (d * share + j) * size + i * part_size
+                raw[at:at + part_size, :] = own_ref[pl.ds(p, part_size, stride=aux_local), :]
+        for k, out in zip((0, 1, 3), outs):
             for j in range(share):
                 p = ((r ^ k) * 2 + s) * share + j + i * length
                 part = own_ref[pl.ds(p, part_size, stride=aux_local), :]
@@ -99,13 +107,13 @@
 
 
 def far_kernel(share, screen_ref, par_ref, density_ref, *refs):
-    ins, outs = refs[:4], refs[4:]
+    ins, outs, corner = refs[:3], refs[3:6], refs[6]
     r, s = lax.axis_index("row"), lax.axis_index("sub")
     size, orbitals = density_ref.shape
     aux_local = par_ref.shape[0] // size
     places = lanes(screen_ref, size)
     cut = orbitals // 128
-    for k, (start, out) in enumerate(zip(ins, outs)):
+    for k, start, out in zip((0, 1, 3), ins, outs):
         for j in range(share):
             p = ((r ^ k) * 2 + s) * share + j
             part = par_ref[pl.ds(p, size, stride=aux_local), :]
@@ -117,10 +125,10 @@
     for h in range(cut):
         outs[1][at + h * size:at + (h + 1) * size, :] = density[:, h * 128:(h + 1) * 128]
     outs[2][at:, :] = half_of(density, r // 2)
-    outs[3][at:, :] = fold(column_block(density, r))
-
-
-def fock_kernel(share, own, one, two, three, density, *refs):
+    corner[...] = fold(column_block(density, r))
+
+
+def fock_kernel(share, own, one, two, two_other, three, corner2, density, *refs):
     outs, (dh, dl, bh, bl, total) = refs[:4], refs[4:]
     r = lax.axis_index("row")
     q = lax.axis_index("aux") * 2 + lax.axis_index("sub")
@@ -142,25 +150,38 @@
     keep(1, *beside)
     a, b = [jnp.where(h == 0, x[1], x[0]) for x in (mine, beside)]
     across = jnp.transpose(jnp.concatenate([jnp.where(odd, b, a), jnp.where(odd, a, b)], axis=0))
-    here = two[at:at + size, :]
+    here = three[at:at + size, :]
     mirror = jnp.transpose(jnp.concatenate([here, here], axis=0))
-    mirror = jnp.where(odd, mirror[:size], mirror[size:])
-    corner = unfold(three[at:, :])
-    corner = jnp.where(odd, corner, pltpu.roll(corner, 64, 1))
+    mirror = jnp.where(odd, mirror[size:], mirror[:size])
+    corner = unfold(corner2[...])
+    corner = jnp.where(odd, pltpu.roll(corner, 64, 1), corner)
     low = lax.broadcasted_iota(jnp.int32, (size, 128), 1) < 64
-    last = jnp.where(low ^ odd, mirror, corner)
+    last = jnp.where(low ^ odd, corner, mirror)
     for k, inner, outer in (
-        (2, here, jnp.where(odd, across[size:], across[:size])),
-        (3, last, jnp.where(odd, across[:size], across[size:])),
+        (2, last, jnp.where(odd, across[size:], across[:size])),
+        (3, here, jnp.where(odd, across[:size], across[size:])),
     ):
         keep(k, jnp.where(h == 0, outer, inner), jnp.where(h == 0, inner, outer))
-    for k, chunk in enumerate((own, one, two, three)):
+    for k, chunk in ((0, own), (1, one), (3, three)):
         for j in range(share):
             for x in range(cut):
                 at = (j * cut + x) * size
                 high, lower = split(chunk[at:at + size, :])
                 bh[j, rows_of(k), x * 128:(x + 1) * 128] = high
                 bl[j, rows_of(k), x * 128:(x + 1) * 128] = lower
+    at = 2 * share * size
+    spots = [
+        [jnp.broadcast_to(ref[at + i:at + i + 1, :], (size, 128)) for i in range(2)] for ref in (two, two_other)
+    ]
+    for j in range(share):
+        values = [jnp.zeros((size, 128), F32)] * cut
+        for d, ref in enumerate((two, two_other)):
+            x = (d * share + j) * size
+            values = spread(spots[d], ref[x:x + size, :], values)
+        for x, value in enumerate(values):
+            high, lower = split(value)
+            bh[j, rows_of(2), x * 128:(x + 1) * 128] = high
+            bl[j, rows_of(2), x * 128:(x + 1) * 128] = lower
     dot = functools.partial(jnp.dot, preferred_element_type=F32)
     dot_t = lambda a, b: lax.dot_general(a, b, (((1,), (1,)), ((), ())), preferred_element_type=F32)
     result = None
@@ -179,20 +200,14 @@
     ins, outs = refs[:4], refs[4:]
     r = lax.axis_index("row")
     value = ins[0][...] + ins[1][...] + (ins[2][...] + ins[3][...])
-    half = value.shape[0] // 2
     for k in range(4):
-        outs[k % 2][k // 2 * half:(k // 2 + 1) * half, :] = fold(column_block(value, r ^ k))
-
-
-def merge_kernel(kept, came, out, away):
-    value = kept[...] + came[...]
-    half = out.shape[0]
-    out[...] = value[:half]
-    away[...] = value[half:]
-
-
-def final_kernel(kept, came, out):
-    out[...] = jnp.transpose(unfold(kept[...] + came[...]))[:out.shape[0], :]
+        outs[k][:value.shape[0] // 2, :] = fold(column_block(value, r ^ k))
+
+
+def final_kernel(kept, one, two, three, out):
+    half = out.shape[0] // 2
+    value = kept[...] + one[:half, :] + (two[:half, :] + three[:half, :])
+    out[...] = jnp.transpose(unfold(value))[:out.shape[0], :]
 
 
 def dealt_body(factor, density, screen):
@@ -204,10 +219,10 @@
     row = lambda x, k: swap(x, "row", 4, k)
     core = lambda x: swap(x, "sub", 2, 1)
     other = core(flat)
-    shapes = [(packed + more, 128) for more in (0, orbitals // 2, block_size, block_size // 2)]
-    sent = call(
+    shapes = [(packed + more, 128) for more in (0, orbitals // 2, block_size)]
+    raw, *sent = call(
         functools.partial(near_kernel, share, block_size),
-        shapes,
+        [(2 * share * block_size + 8, 128)] + shapes,
         ins=[HBM] * 2,
         scratch=[
             pltpu.VMEM(screen.shape, jnp.int32),
@@ -216,13 +231,14 @@
         ],
         limit=FIRST,
     )(screen, flat)
-    sent = call(
+    two = row(raw, 2)
+    own, one, three, corner = call(
         functools.partial(far_kernel, share),
-        shapes,
-        count=7,
-        alias={3 + k: k for k in range(4)},
+        shapes + [(block_size // 2, 128)],
+        count=6,
+        alias={3 + k: k for k in range(3)},
     )(core(screen), other, density, *sent)
-    three, two, one = [row(sent[k], k) for k in (3, 2, 1)]
+    three, one, corner = row(three, 3), row(one, 1), row(corner, 2)
     parts = call(
         functools.partial(fock_kernel, share),
         [(block_size, orbitals)] * 4,
@@ -233,12 +249,12 @@
             pltpu.VMEM((share, orbitals, orbitals), BF16),
             pltpu.VMEM((orbitals, orbitals), F32),
         ],
-        count=5,
-    )(sent[0], one, two, three, density)
+        count=7,
+    )(own, one, two, core(two), three, corner, density)
     sums = [parts[0]] + [swap(parts[k], ("aux", "sub"), 4, k) for k in (1, 2, 3)]
-    kept, away = call(cut_kernel, [(block_size, 2 * block_size)] * 2, count=4)(*sums)
-    kept, away = call(merge_kernel, [(block_size // 2, 2 * block_size)] * 2, count=2)(kept, row(away, 1))
-    return call(final_kernel, [(block_size, block_size)], count=2)(kept, row(away, 2))[0]
+    cuts = call(cut_kernel, [(block_size // 2 + more, 2 * block_size) for more in (0, 0, 16, 8)], count=4)(*sums)
+    moved = [row(cuts[k], k) for k in (1, 2, 3)]
+    return call(final_kernel, [(block_size, block_size)], count=4)(cuts[0], *moved)[0]
 
 
 def pair_block(tiled, block_rows, block_cols):

time: 37.4 us -> 36.2 us (0.968)
  starting transfers between devices: 14.2 us -> 12.3 us
  waiting for transfers between devices: 19.4 us -> 20.1 us
    ppermute x10 -> x13, starting transfers between devices: 14.2 us -> 12.3 us  [swap(): return lax.ppermute(x, axes, [(a, a ^ k) for a in range(size)])]
    ppermute x10 -> x13, waiting for transfers between devices: 19.4 us -> 20.1 us  [swap(): return lax.ppermute(x, axes, [(a, a ^ k) for a in range(size)])]
    pallas_call x5 -> x4, Pallas kernels: 2.32 us -> 2.34 us  [the longest x1 1.22 us: dealt_body(): call(functools.partial(near_kernel, share, block_size), [(2 * share * blo...]
  transfers between devices with their start and end apart: 10 -> 13, of which waited for: 6 -> 8; matrix products, arithmetic and copies ran while one was open for 0% -> 0% of each run, Pallas kernels for 3% -> 4%
where the time goes in v4:
time: 36.2 us; the launch traced here: 36 us
  waiting for transfers between devices  20.1 us (56%)
  starting transfers between devices  12.3 us (34%)
  Pallas kernels  3.43 us (9%)
    ppermute x13, waiting for transfers between devices, swap(): return lax.ppermute(x, axes, [(a, a ^ k) for a in range(size)])  20.1 us
    ppermute x13, starting transfers between devices, swap(): return lax.ppermute(x, axes, [(a, a ^ k) for a in range(size)])  12.3 us
    pallas_call x1, Pallas kernels, dealt_body(): call(functools.partial(near_kernel, share, block_size), [(2 * share * blo...  1.22 us
    pallas_call x1, Pallas kernels, dealt_body(): call(functools.partial(fock_kernel, share), [(block_size, orbitals)] * 4,...  1.1 us
    pallas_call x1, Pallas kernels, dealt_body(): call(final_kernel, [(block_size, block_size)], count=4)(cuts[0], *moved)[0]  0.76 us
  transfers between devices with their start and end apart: 13, of which 8 were waited for; matrix products, arithmetic and copies ran while one was open for 0% of the time, Pallas kernels for 4%

profile of v4, /device:TPU:0, one launch (start us, length us, event | category | flops | bytes accessed | tf_op | source)
XLA Modules:
  0.0 36.0 jit_solution(11071446402566960366)
XLA Ops:
  0.0 0.5 %collective-permute-start.1 = (f32[1024,128]{1,0:T(8,128)}, f32[1024,128]{1,0:T(8,128)S(1)}, u32[]{:S(2)}, u32[]{:S(2)}) collective-permute-start(f32[1024,128]{1,0:T(8,128)} %bitcast.1), channel_id=1, source_target_pairs={{0,1},{1,0},{2,3},{3,2},{4,5},{5,4},{6,7},{7,6},{8,9},{9,8},{10,11... | collective-permute-start | bytes 1572872 | tf_op jit(solution)/shard_map/ppermute | solution.py:31
  0.5 0.2 copy-done.1
  0.7 1.2 %shard_map.37 = (f32[264,128]{1,0:T(8,128)S(1)}, f32[256,128]{1,0:T(8,128)S(1)}, f32[384,128]{1,0:T(8,128)S(1)}, f32[320,128]{1,0:T(8,128)S(1)}) custom-call(s32[1,2]{1,0:T(1,128)S(1)} %copy-done.1, f32[1024,128]{1,0:T(8,128)} %bitcast.2), custom_call_target="tpu_custom_call" | custom-call | tf_op jit(solution)/shard_map/pallas_call | solution.py:223
  1.9 4.1 %collective-permute-start.3 = (f32[264,128]{1,0:T(8,128)S(1)}, f32[264,128]{1,0:T(8,128)S(1)}, u32[]{:S(2)}, u32[]{:S(2)}) collective-permute-start(f32[264,128]{1,0:T(8,128)S(1)} %get-tuple-element.26), channel_id=1, source_target_pairs={{0,8},{4,12},{8,0},{12,4},{1,9},{5,13},{9,1},{13,5},{2,10},{6,14},... | collective-permute-start | bytes 405512 | tf_op jit(solution)/shard_map/ppermute | solution.py:31
  6.0 0.0 collective-permute-start
  6.0 1.1 %collective-permute-done.screen_ref = s32[1,2]{1,0:T(1,128)S(1)} collective-permute-done((s32[1,2]{1,0:T(1,128)S(1)}, s32[1,2]{1,0:T(1,128)S(1)}, u32[]{:S(2)}, u32[]{:S(2)}) %collective-permute-start) | collective-permute-done | bytes 40 | tf_op jit(solution)/shard_map/ppermute | solution.py:31
  7.1 0.2 shard_map.38
  7.3 1.6 %collective-permute-start.2 = (f32[384,128]{1,0:T(8,128)S(1)}, f32[384,128]{1,0:T(8,128)S(1)}, u32[]{:S(2)}, u32[]{:S(2)}) collective-permute-start(f32[384,128]{1,0:T(8,128)S(1)} %get-tuple-element.25), channel_id=1, source_target_pairs={{0,4},{4,0},{8,12},{12,8},{1,5},{5,1},{9,13},{13,9},{2,6},{6,2},{1... | collective-permute-start | bytes 589832 | tf_op jit(solution)/shard_map/ppermute | solution.py:31
  8.9 4.4 %collective-permute-done.3.two = f32[264,128]{1,0:T(8,128)S(1)} collective-permute-done((f32[264,128]{1,0:T(8,128)S(1)}, f32[264,128]{1,0:T(8,128)S(1)}, u32[]{:S(2)}, u32[]{:S(2)}) %collective-permute-start.3) | collective-permute-done | bytes 135200 | tf_op jit(solution)/shard_map/ppermute | solution.py:31
  13.3 1.3 %collective-permute-done.4.two_other = f32[264,128]{1,0:T(8,128)S(1)} collective-permute-done((f32[264,128]{1,0:T(8,128)S(1)}, f32[264,128]{1,0:T(8,128)S(1)}, u32[]{:S(2)}, u32[]{:S(2)}) %collective-permute-start.4) | collective-permute-done | bytes 135200 | tf_op jit(solution)/shard_map/ppermute | solution.py:31
  14.6 5.6 %collective-permute-done.6.corner2 = f32[32,128]{1,0:T(8,128)S(1)} collective-permute-done((f32[32,128]{1,0:T(8,128)S(1)}, f32[32,128]{1,0:T(8,128)S(1)}, u32[]{:S(2)}, u32[]{:S(2)}) %collective-permute-start.6) | collective-permute-done | bytes 16416 | tf_op jit(solution)/shard_map/ppermute | solution.py:31
  20.2 1.1 %shard_map.39 = (f32[64,256]{1,0:T(8,128)S(1)}, f32[64,256]{1,0:T(8,128)S(1)}, f32[64,256]{1,0:T(8,128)S(1)}, f32[64,256]{1,0:T(8,128)S(1)}) custom-call(f32[256,128]{1,0:T(8,128)S(1)} %get-tuple-element.24.own, f32[384,128]{1,0:T(8,128)S(1)} %collective-permute-done.2.one, f32[264,128]{1,0:T(8,128)S(1)} %collective-permute-done.3.two, ...), custom_call_target="tpu_custom_call" | custom-call | tf_op jit(solution)/shard_map/pallas_call | solution.py:242
  21.3 0.1 collective-permute-start.7
  21.4 1.6 %collective-permute-start.8 = (f32[64,256]{1,0:T(8,128)S(1)}, f32[64,256]{1,0:T(8,128)S(1)}, u32[]{:S(2)}, u32[]{:S(2)}) collective-permute-start(f32[64,256]{1,0:T(8,128)S(1)} %get-tuple-element.31), channel_id=1, source_target_pairs={{0,2},{1,3},{2,0},{3,1},{4,6},{5,7},{6,4},{7,5},{8,10},{9,11},{10,... | collective-permute-start | bytes 196616 | tf_op jit(solution)/shard_map/ppermute | solution.py:31
  23.0 0.3 collective-permute-start.9
  23.3 2.6 %collective-permute-done.8.refs_2_ = f32[64,256]{1,0:T(8,128)S(1)} collective-permute-done((f32[64,256]{1,0:T(8,128)S(1)}, f32[64,256]{1,0:T(8,128)S(1)}, u32[]{:S(2)}, u32[]{:S(2)}) %collective-permute-start.8) | collective-permute-done | bytes 65568 | tf_op jit(solution)/shard_map/ppermute | solution.py:31
  25.9 1.1 %collective-permute-done.9.refs_3_ = f32[64,256]{1,0:T(8,128)S(1)} collective-permute-done((f32[64,256]{1,0:T(8,128)S(1)}, f32[64,256]{1,0:T(8,128)S(1)}, u32[]{:S(2)}, u32[]{:S(2)}) %collective-permute-start.9) | collective-permute-done | bytes 65568 | tf_op jit(solution)/shard_map/ppermute | solution.py:31
  27.1 0.2 shard_map.40
  27.2 2.4 %collective-permute-start.11 = (f32[48,128]{1,0:T(8,128)S(1)}, f32[48,128]{1,0:T(8,128)S(1)}, u32[]{:S(2)}, u32[]{:S(2)}) collective-permute-start(f32[48,128]{1,0:T(8,128)S(1)} %get-tuple-element.35), channel_id=1, source_target_pairs={{0,8},{4,12},{8,0},{12,4},{1,9},{5,13},{9,1},{13,5},{2,10},{6,14},... | collective-permute-start | bytes 73736 | tf_op jit(solution)/shard_map/ppermute | solution.py:31
  29.7 1.2 %collective-permute-start.12 = (f32[40,128]{1,0:T(8,128)S(1)}, f32[40,128]{1,0:T(8,128)S(1)}, u32[]{:S(2)}, u32[]{:S(2)}) collective-permute-start(f32[40,128]{1,0:T(8,128)S(1)} %get-tuple-element.36), channel_id=1, source_target_pairs={{0,12},{4,8},{8,4},{12,0},{1,13},{5,9},{9,5},{13,1},{2,14},{6,10},... | collective-permute-start | bytes 61448 | tf_op jit(solution)/shard_map/ppermute | solution.py:31
  30.9 0.5 %collective-permute-start.10 = (f32[32,128]{1,0:T(8,128)S(1)}, f32[32,128]{1,0:T(8,128)S(1)}, u32[]{:S(2)}, u32[]{:S(2)}) collective-permute-start(f32[32,128]{1,0:T(8,128)S(1)} %get-tuple-element.34), channel_id=1, source_target_pairs={{0,4},{4,0},{8,12},{12,8},{1,5},{5,1},{9,13},{13,9},{2,6},{6,2},{1... | collective-permute-start | bytes 49160 | tf_op jit(solution)/shard_map/ppermute | solution.py:31
  31.4 3.3 %collective-permute-done.10.one = f32[32,128]{1,0:T(8,128)S(1)} collective-permute-done((f32[32,128]{1,0:T(8,128)S(1)}, f32[32,128]{1,0:T(8,128)S(1)}, u32[]{:S(2)}, u32[]{:S(2)}) %collective-permute-start.10) | collective-permute-done | bytes 16416 | tf_op jit(solution)/shard_map/ppermute | solution.py:31
  34.6 0.6 %collective-permute-done.12.three = f32[40,128]{1,0:T(8,128)S(1)} collective-permute-done((f32[40,128]{1,0:T(8,128)S(1)}, f32[40,128]{1,0:T(8,128)S(1)}, u32[]{:S(2)}, u32[]{:S(2)}) %collective-permute-start.12) | collective-permute-done | bytes 20512 | tf_op jit(solution)/shard_map/ppermute | solution.py:31
  35.3 0.8 %shard_map.41 = f32[64,64]{1,0:T(8,128)} custom-call(f32[32,128]{1,0:T(8,128)S(1)} %get-tuple-element.33.kept, f32[32,128]{1,0:T(8,128)S(1)} %collective-permute-done.10.one, f32[48,128]{1,0:T(8,128)S(1)} %collective-permute-done.11.two, f32[40,128]{1,0:T(8,128)S(1)} %collective-permute-done.12.three), custom_call_target="tpu_custom_call" | custom-call | tf_op jit(solution)/shard_map/pallas_call | solution.py:257
  (11 shorter events, 0.0 us)
Async XLA Ops:
  0.0 0.7 %copy-start.1 = (s32[1,2]{1,0:T(1,128)S(1)}, s32[1,2]{1,0:T(1,128)}, u32[]{:S(2)}) copy-start(s32[1,2]{1,0:T(1,128)} %screen_hbm.1) | copy-start | bytes 28
  0.0 7.1 %copy-start = (f32[64,256]{1,0:T(8,128)S(1)}, f32[64,256]{1,0:T(8,128)}, u32[]{:S(2)}) copy-start(f32[64,256]{1,0:T(8,128)} %density.1) | copy-start | bytes 196612
  0.0 7.1 %collective-permute-start.1 = (f32[1024,128]{1,0:T(8,128)}, f32[1024,128]{1,0:T(8,128)S(1)}, u32[]{:S(2)}, u32[]{:S(2)}) collective-permute-start(f32[1024,128]{1,0:T(8,128)} %bitcast.1), channel_id=1, source_target_pairs={{0,1},{1,0},{2,3},{3,2},{4,5},{5,4},{6,7},{7,6},{8,9},{9,8},{10,11... | collective-permute-start | bytes 1572872 | tf_op jit(solution)/shard_map/ppermute | solution.py:31
  1.9 11.4 %collective-permute-start.3 = (f32[264,128]{1,0:T(8,128)S(1)}, f32[264,128]{1,0:T(8,128)S(1)}, u32[]{:S(2)}, u32[]{:S(2)}) collective-permute-start(f32[264,128]{1,0:T(8,128)S(1)} %get-tuple-element.26), channel_id=1, source_target_pairs={{0,8},{4,12},{8,0},{12,4},{1,9},{5,13},{9,1},{13,5},{2,10},{6,14},... | collective-permute-start | bytes 405512 | tf_op jit(solution)/shard_map/ppermute | solution.py:31
  6.0 1.1 %collective-permute-start = (s32[1,2]{1,0:T(1,128)S(1)}, s32[1,2]{1,0:T(1,128)S(1)}, u32[]{:S(2)}, u32[]{:S(2)}) collective-permute-start(s32[1,2]{1,0:T(1,128)S(1)} %copy-done.1), channel_id=1, source_target_pairs={{0,1},{1,0},{2,3},{3,2},{4,5},{5,4},{6,7},{7,6},{8,9},{9,8},{10,11... | collective-permute-start | bytes 32 | tf_op jit(solution)/shard_map/ppermute | solution.py:31
  7.3 12.9 %collective-permute-start.2 = (f32[384,128]{1,0:T(8,128)S(1)}, f32[384,128]{1,0:T(8,128)S(1)}, u32[]{:S(2)}, u32[]{:S(2)}) collective-permute-start(f32[384,128]{1,0:T(8,128)S(1)} %get-tuple-element.25), channel_id=1, source_target_pairs={{0,4},{4,0},{8,12},{12,8},{1,5},{5,1},{9,13},{13,9},{2,6},{6,2},{1... | collective-permute-start | bytes 589832 | tf_op jit(solution)/shard_map/ppermute | solution.py:31
  8.9 11.3 %collective-permute-start.5 = (f32[320,128]{1,0:T(8,128)S(1)}, f32[320,128]{1,0:T(8,128)S(1)}, u32[]{:S(2)}, u32[]{:S(2)}) collective-permute-start(f32[320,128]{1,0:T(8,128)S(1)} %get-tuple-element.27), channel_id=1, source_target_pairs={{0,12},{4,8},{8,4},{12,0},{1,13},{5,9},{9,5},{13,1},{2,14},{6,10},... | collective-permute-start | bytes 491528 | tf_op jit(solution)/shard_map/ppermute | solution.py:31
  13.3 1.4 %collective-permute-start.4 = (f32[264,128]{1,0:T(8,128)S(1)}, f32[264,128]{1,0:T(8,128)S(1)}, u32[]{:S(2)}, u32[]{:S(2)}) collective-permute-start(f32[264,128]{1,0:T(8,128)S(1)} %collective-permute-done.3.two), channel_id=1, source_target_pairs={{0,1},{1,0},{2,3},{3,2},{4,5},{5,4},{6,7},{7,6},{8,9},{9,8},{10,11... | collective-permute-start | bytes 405512 | tf_op jit(solution)/shard_map/ppermute | solution.py:31
  13.3 6.9 %collective-permute-start.6 = (f32[32,128]{1,0:T(8,128)S(1)}, f32[32,128]{1,0:T(8,128)S(1)}, u32[]{:S(2)}, u32[]{:S(2)}) collective-permute-start(f32[32,128]{1,0:T(8,128)S(1)} %get-tuple-element.28), channel_id=1, source_target_pairs={{0,8},{4,12},{8,0},{12,4},{1,9},{5,13},{9,1},{13,5},{2,10},{6,14},... | collective-permute-start | bytes 49160 | tf_op jit(solution)/shard_map/ppermute | solution.py:31
  21.3 1.9 %collective-permute-start.7 = (f32[64,256]{1,0:T(8,128)S(1)}, f32[64,256]{1,0:T(8,128)S(1)}, u32[]{:S(2)}, u32[]{:S(2)}) collective-permute-start(f32[64,256]{1,0:T(8,128)S(1)} %get-tuple-element.30), channel_id=1, source_target_pairs={{0,1},{1,0},{2,3},{3,2},{4,5},{5,4},{6,7},{7,6},{8,9},{9,8},{10,11... | collective-permute-start | bytes 196616 | tf_op jit(solution)/shard_map/ppermute | solution.py:31
  21.4 4.5 %collective-permute-start.8 = (f32[64,256]{1,0:T(8,128)S(1)}, f32[64,256]{1,0:T(8,128)S(1)}, u32[]{:S(2)}, u32[]{:S(2)}) collective-permute-start(f32[64,256]{1,0:T(8,128)S(1)} %get-tuple-element.31), channel_id=1, source_target_pairs={{0,2},{1,3},{2,0},{3,1},{4,6},{5,7},{6,4},{7,5},{8,10},{9,11},{10,... | collective-permute-start | bytes 196616 | tf_op jit(solution)/shard_map/ppermute | solution.py:31
  23.0 4.0 %collective-permute-start.9 = (f32[64,256]{1,0:T(8,128)S(1)}, f32[64,256]{1,0:T(8,128)S(1)}, u32[]{:S(2)}, u32[]{:S(2)}) collective-permute-start(f32[64,256]{1,0:T(8,128)S(1)} %get-tuple-element.32), channel_id=1, source_target_pairs={{0,3},{1,2},{2,1},{3,0},{4,7},{5,6},{6,5},{7,4},{8,11},{9,10},{10,... | collective-permute-start | bytes 196616 | tf_op jit(solution)/shard_map/ppermute | solution.py:31
  27.2 8.0 %collective-permute-start.11 = (f32[48,128]{1,0:T(8,128)S(1)}, f32[48,128]{1,0:T(8,128)S(1)}, u32[]{:S(2)}, u32[]{:S(2)}) collective-permute-start(f32[48,128]{1,0:T(8,128)S(1)} %get-tuple-element.35), channel_id=1, source_target_pairs={{0,8},{4,12},{8,0},{12,4},{1,9},{5,13},{9,1},{13,5},{2,10},{6,14},... | collective-permute-start | bytes 73736 | tf_op jit(solution)/shard_map/ppermute | solution.py:31
  29.7 5.6 %collective-permute-start.12 = (f32[40,128]{1,0:T(8,128)S(1)}, f32[40,128]{1,0:T(8,128)S(1)}, u32[]{:S(2)}, u32[]{:S(2)}) collective-permute-start(f32[40,128]{1,0:T(8,128)S(1)} %get-tuple-element.36), channel_id=1, source_target_pairs={{0,12},{4,8},{8,4},{12,0},{1,13},{5,9},{9,5},{13,1},{2,14},{6,10},... | collective-permute-start | bytes 61448 | tf_op jit(solution)/shard_map/ppermute | solution.py:31
  30.9 3.7 %collective-permute-start.10 = (f32[32,128]{1,0:T(8,128)S(1)}, f32[32,128]{1,0:T(8,128)S(1)}, u32[]{:S(2)}, u32[]{:S(2)}) collective-permute-start(f32[32,128]{1,0:T(8,128)S(1)} %get-tuple-element.34), channel_id=1, source_target_pairs={{0,4},{4,0},{8,12},{12,8},{1,5},{5,1},{9,13},{13,9},{2,6},{6,2},{1... | collective-permute-start | bytes 49160 | tf_op jit(solution)/shard_map/ppermute | solution.py:31

commit v5 on v4

--- a/solution.py
+++ b/solution.py
@@ -15,14 +15,13 @@
 BF16 = jnp.bfloat16
 
 
-def call(kernel, outs, scratch=(), ins=None, count=0, limit=12 << 20, alias={}):
+def call(kernel, outs, scratch=(), ins=None, count=0, limit=12 << 20):
     return pl.pallas_call(
         kernel,
         out_shape=tuple(jax.ShapeDtypeStruct(s, F32) for s in outs),
         in_specs=ins if ins is not None else [VMEM] * count,
         out_specs=tuple(VMEM for _ in outs),
         scratch_shapes=list(scratch),
-        input_output_aliases=alias,
         compiler_params=pltpu.CompilerParams(vmem_limit_bytes=limit),
     )
 
@@ -73,62 +72,56 @@
     return jnp.where(b % 2 == 1, pltpu.roll(picked, 64, 1), picked)
 
 
-def near_kernel(share, size, screen_hbm, own_hbm, *refs):
-    raw, outs, (screen_ref, own_ref, sems) = refs[0], refs[1:4], refs[4:]
+def near_kernel(share, size, own_hbm, raw, own, sems):
     r, s = lax.axis_index("row"), lax.axis_index("sub")
-    aux_local = own_ref.shape[0] // size
-    cut = outs[0].shape[0] // (share * size)
+    aux_local = own.shape[0] // size
     part_size = size // 2
     length = part_size * aux_local
     halves = [pl.ds(i * length, length) for i in range(2)]
-    copies = [pltpu.make_async_copy(screen_hbm, screen_ref, sems.at[2])]
-    copies += [pltpu.make_async_copy(own_hbm.at[x], own_ref.at[x], sems.at[i]) for i, x in enumerate(halves)]
+    copies = [pltpu.make_async_copy(own_hbm.at[x], own.at[x], sems.at[i]) for i, x in enumerate(halves)]
     for copy in copies:
         copy.start()
-    copies[0].wait()
-    places = lanes(screen_ref, part_size)
-    even = lax.broadcasted_iota(jnp.int32, (8, 128), 0) % 2 == 0
-    raw[2 * share * size:, :] = jnp.where(even, places[0][:8], places[1][:8]).astype(F32)
     for i in range(2):
-        copies[1 + i].wait()
+        copies[i].wait()
         for d in range(2):
             for j in range(share):
                 p = ((r ^ 2) * 2 + (s ^ d)) * share + j + i * length
                 at = (d * share + j) * size + i * part_size
-                raw[at:at + part_size, :] = own_ref[pl.ds(p, part_size, stride=aux_local), :]
-        for k, out in zip((0, 1, 3), outs):
-            for j in range(share):
-                p = ((r ^ k) * 2 + s) * share + j + i * length
-                part = own_ref[pl.ds(p, part_size, stride=aux_local), :]
-                start = [jnp.zeros((part_size, 128), F32)] * cut
-                for h, value in enumerate(spread(places, part, start)):
-                    at = (j * cut + h) * size + i * part_size
-                    out[at:at + part_size, :] = value
-
-
-def far_kernel(share, screen_ref, par_ref, density_ref, *refs):
-    ins, outs, corner = refs[:3], refs[3:6], refs[6]
+                raw[at:at + part_size, :] = own[pl.ds(p, part_size, stride=aux_local), :]
+
+
+def far_kernel(share, screen_ref, other_ref, own_ref, par_ref, density_ref, *outs):
     r, s = lax.axis_index("row"), lax.axis_index("sub")
+    outs, extra = outs[:3], outs[3]
     size, orbitals = density_ref.shape
     aux_local = par_ref.shape[0] // size
-    places = lanes(screen_ref, size)
+    sources = [(lanes(places, size), part) for places, part in ((screen_ref, own_ref), (other_ref, par_ref))]
     cut = orbitals // 128
-    for k, start, out in zip((0, 1, 3), ins, outs):
+    for k, out in zip((0, 1, 3), outs):
         for j in range(share):
             p = ((r ^ k) * 2 + s) * share + j
-            part = par_ref[pl.ds(p, size, stride=aux_local), :]
-            spots = [slice((j * cut + h) * size, (j * cut + h + 1) * size) for h in range(cut)]
-            for spot, value in zip(spots, spread(places, part, [start[x, :] for x in spots])):
-                out[spot, :] = value
+            values = [jnp.zeros((size, 128), F32)] * cut
+            for places, part in sources:
+                values = spread(places, part[pl.ds(p, size, stride=aux_local), :], values)
+            for h, value in enumerate(values):
+                at = (j * cut + h) * size
+                out[at:at + size, :] = value
     at = share * cut * size
     density = density_ref[...]
     for h in range(cut):
         outs[1][at + h * size:at + (h + 1) * size, :] = density[:, h * 128:(h + 1) * 128]
     outs[2][at:, :] = half_of(density, r // 2)
-    corner[...] = fold(column_block(density, r))
-
-
-def fock_kernel(share, own, one, two, two_other, three, corner2, density, *refs):
+    at = size // 2
+    extra[:at, :] = fold(column_block(density, r))
+    places = sources[0][0] + sources[1][0]
+    row = lax.broadcasted_iota(jnp.int32, (8, 128), 0) % 4
+    value = places[3][:8]
+    for i in range(3):
+        value = jnp.where(row == i, places[i][:8], value)
+    extra[at:, :] = value.astype(F32)
+
+
+def fock_kernel(share, own, one, two, two_other, three, extra2, density, *refs):
     outs, (dh, dl, bh, bl, total) = refs[:4], refs[4:]
     r = lax.axis_index("row")
     q = lax.axis_index("aux") * 2 + lax.axis_index("sub")
@@ -153,7 +146,7 @@
     here = three[at:at + size, :]
     mirror = jnp.transpose(jnp.concatenate([here, here], axis=0))
     mirror = jnp.where(odd, mirror[size:], mirror[:size])
-    corner = unfold(corner2[...])
+    corner = unfold(extra2[:size // 2, :])
     corner = jnp.where(odd, pltpu.roll(corner, 64, 1), corner)
     low = lax.broadcasted_iota(jnp.int32, (size, 128), 1) < 64
     last = jnp.where(low ^ odd, corner, mirror)
@@ -169,9 +162,10 @@
                 high, lower = split(chunk[at:at + size, :])
                 bh[j, rows_of(k), x * 128:(x + 1) * 128] = high
                 bl[j, rows_of(k), x * 128:(x + 1) * 128] = lower
-    at = 2 * share * size
+    at = size // 2
     spots = [
-        [jnp.broadcast_to(ref[at + i:at + i + 1, :], (size, 128)) for i in range(2)] for ref in (two, two_other)
+        [jnp.broadcast_to(extra2[at + 2 * d + i:at + 2 * d + i + 1, :], (size, 128)) for i in range(2)]
+        for d in range(2)
     ]
     for j in range(share):
         values = [jnp.zeros((size, 128), F32)] * cut
@@ -219,26 +213,20 @@
     row = lambda x, k: swap(x, "row", 4, k)
     core = lambda x: swap(x, "sub", 2, 1)
     other = core(flat)
-    shapes = [(packed + more, 128) for more in (0, orbitals // 2, block_size)]
-    raw, *sent = call(
+    raw, mine = call(
         functools.partial(near_kernel, share, block_size),
-        [(2 * share * block_size + 8, 128)] + shapes,
-        ins=[HBM] * 2,
-        scratch=[
-            pltpu.VMEM(screen.shape, jnp.int32),
-            pltpu.VMEM(flat.shape, F32),
-            pltpu.SemaphoreType.DMA((3,)),
-        ],
+        [(2 * share * block_size, 128), flat.shape],
+        ins=[HBM],
+        scratch=[pltpu.SemaphoreType.DMA((2,))],
         limit=FIRST,
-    )(screen, flat)
+    )(flat)
     two = row(raw, 2)
-    own, one, three, corner = call(
+    own, one, three, extra = call(
         functools.partial(far_kernel, share),
-        shapes + [(block_size // 2, 128)],
-        count=6,
-        alias={3 + k: k for k in range(3)},
-    )(core(screen), other, density, *sent)
-    three, one, corner = row(three, 3), row(one, 1), row(corner, 2)
+        [(packed + more, 128) for more in (0, orbitals // 2, block_size)] + [(block_size // 2 + 8, 128)],
+        count=5,
+    )(screen, core(screen), mine, other, density)
+    three, one, extra = row(three, 3), row(one, 1), row(extra, 2)
     parts = call(
         functools.partial(fock_kernel, share),
         [(block_size, orbitals)] * 4,
@@ -250,7 +238,7 @@
             pltpu.VMEM((orbitals, orbitals), F32),
         ],
         count=7,
-    )(own, one, two, core(two), three, corner, density)
+    )(own, one, two, core(two), three, extra, density)
     sums = [parts[0]] + [swap(parts[k], ("aux", "sub"), 4, k) for k in (1, 2, 3)]
     cuts = call(cut_kernel, [(block_size // 2 + more, 2 * block_size) for more in (0, 0, 16, 8)], count=4)(*sums)
     moved = [row(cuts[k], k) for k in (1, 2, 3)]

time: 36.2 us -> 35.9 us (level)
  waiting for transfers between devices: 20.1 us -> 19.6 us
  starting transfers between devices: 12.3 us -> 12.7 us
    ppermute x13, waiting for transfers between devices: 20.1 us -> 19.6 us  [swap(): return lax.ppermute(x, axes, [(a, a ^ k) for a in range(size)])]
    ppermute x13, starting transfers between devices: 12.3 us -> 12.7 us  [swap(): return lax.ppermute(x, axes, [(a, a ^ k) for a in range(size)])]
where the time goes in v5:
time: 35.9 us; the launch traced here: 35.7 us
  waiting for transfers between devices  19.6 us (55%)
  starting transfers between devices  12.7 us (35%)
  Pallas kernels  3.35 us (9%)
    ppermute x13, waiting for transfers between devices, swap(): return lax.ppermute(x, axes, [(a, a ^ k) for a in range(size)])  19.6 us
    ppermute x13, starting transfers between devices, swap(): return lax.ppermute(x, axes, [(a, a ^ k) for a in range(size)])  12.7 us
    pallas_call x1, Pallas kernels, dealt_body(): call(functools.partial(fock_kernel, share), [(block_size, orbitals)] * 4,...  1.1 us
    pallas_call x1, Pallas kernels, dealt_body(): call(functools.partial(near_kernel, share, block_size), [(2 * share * blo...  1.07 us
    pallas_call x1, Pallas kernels, dealt_body(): call(final_kernel, [(block_size, block_size)], count=4)(cuts[0], *moved)[0]  0.76 us
  transfers between devices with their start and end apart: 13, of which 8 were waited for; matrix products, arithmetic and copies ran while one was open for 0% of the time, Pallas kernels for 4%

profile of v5, /device:TPU:0, one launch (start us, length us, event | category | flops | bytes accessed | tf_op | source)
XLA Modules:
  0.0 35.7 jit_solution(8735882556212638092)
XLA Ops:
  0.0 0.5 %collective-permute-start.1 = (f32[1024,128]{1,0:T(8,128)}, f32[1024,128]{1,0:T(8,128)S(1)}, u32[]{:S(2)}, u32[]{:S(2)}) collective-permute-start(f32[1024,128]{1,0:T(8,128)} %bitcast.1), channel_id=1, source_target_pairs={{0,1},{1,0},{2,3},{3,2},{4,5},{5,4},{6,7},{7,6},{8,9},{9,8},{10,11... | collective-permute-start | bytes 1572872 | tf_op jit(solution)/shard_map/ppermute | solution.py:30
  0.5 1.1 %shard_map.37 = (f32[256,128]{1,0:T(8,128)S(1)}, f32[1024,128]{1,0:T(8,128)S(1)}) custom-call(f32[1024,128]{1,0:T(8,128)} %bitcast.2), custom_call_target="tpu_custom_call" | custom-call | tf_op jit(solution)/shard_map/pallas_call | solution.py:216
  1.5 3.7 %collective-permute-start.3 = (f32[256,128]{1,0:T(8,128)S(1)}, f32[256,128]{1,0:T(8,128)S(1)}, u32[]{:S(2)}, u32[]{:S(2)}) collective-permute-start(f32[256,128]{1,0:T(8,128)S(1)} %get-tuple-element.22), channel_id=1, source_target_pairs={{0,8},{4,12},{8,0},{12,4},{1,9},{5,13},{9,1},{13,5},{2,10},{6,14},... | collective-permute-start | bytes 393224 | tf_op jit(solution)/shard_map/ppermute | solution.py:30
  5.2 0.2 collective-permute-start
  5.4 0.9 %collective-permute-done.other_ref = s32[1,2]{1,0:T(1,128)S(1)} collective-permute-done((s32[1,2]{1,0:T(1,128)S(1)}, s32[1,2]{1,0:T(1,128)S(1)}, u32[]{:S(2)}, u32[]{:S(2)}) %collective-permute-start) | collective-permute-done | bytes 40 | tf_op jit(solution)/shard_map/ppermute | solution.py:30
  6.4 0.3 shard_map.38
  6.6 1.6 %collective-permute-start.2 = (f32[384,128]{1,0:T(8,128)S(1)}, f32[384,128]{1,0:T(8,128)S(1)}, u32[]{:S(2)}, u32[]{:S(2)}) collective-permute-start(f32[384,128]{1,0:T(8,128)S(1)} %get-tuple-element.21), channel_id=1, source_target_pairs={{0,4},{4,0},{8,12},{12,8},{1,5},{5,1},{9,13},{13,9},{2,6},{6,2},{1... | collective-permute-start | bytes 589832 | tf_op jit(solution)/shard_map/ppermute | solution.py:30
  8.3 0.6 %collective-permute-start.5 = (f32[320,128]{1,0:T(8,128)S(1)}, f32[320,128]{1,0:T(8,128)S(1)}, u32[]{:S(2)}, u32[]{:S(2)}) collective-permute-start(f32[320,128]{1,0:T(8,128)S(1)} %get-tuple-element.23), channel_id=1, source_target_pairs={{0,12},{4,8},{8,4},{12,0},{1,13},{5,9},{9,5},{13,1},{2,14},{6,10},... | collective-permute-start | bytes 491528 | tf_op jit(solution)/shard_map/ppermute | solution.py:30
  8.9 3.5 %collective-permute-done.3.two = f32[256,128]{1,0:T(8,128)S(1)} collective-permute-done((f32[256,128]{1,0:T(8,128)S(1)}, f32[256,128]{1,0:T(8,128)S(1)}, u32[]{:S(2)}, u32[]{:S(2)}) %collective-permute-start.3) | collective-permute-done | bytes 131104 | tf_op jit(solution)/shard_map/ppermute | solution.py:30
  12.4 1.3 %collective-permute-done.4.two_other = f32[256,128]{1,0:T(8,128)S(1)} collective-permute-done((f32[256,128]{1,0:T(8,128)S(1)}, f32[256,128]{1,0:T(8,128)S(1)}, u32[]{:S(2)}, u32[]{:S(2)}) %collective-permute-start.4) | collective-permute-done | bytes 131104 | tf_op jit(solution)/shard_map/ppermute | solution.py:30
  13.8 6.3 %collective-permute-done.6.extra2 = f32[40,128]{1,0:T(8,128)S(1)} collective-permute-done((f32[40,128]{1,0:T(8,128)S(1)}, f32[40,128]{1,0:T(8,128)S(1)}, u32[]{:S(2)}, u32[]{:S(2)}) %collective-permute-start.6) | collective-permute-done | bytes 20512 | tf_op jit(solution)/shard_map/ppermute | solution.py:30
  20.1 1.1 %shard_map.39 = (f32[64,256]{1,0:T(8,128)S(1)}, f32[64,256]{1,0:T(8,128)S(1)}, f32[64,256]{1,0:T(8,128)S(1)}, f32[64,256]{1,0:T(8,128)S(1)}) custom-call(f32[256,128]{1,0:T(8,128)S(1)} %get-tuple-element.20.own, f32[384,128]{1,0:T(8,128)S(1)} %collective-permute-done.2.one, f32[256,128]{1,0:T(8,128)S(1)} %collective-permute-done.3.two, ...), custom_call_target="tpu_custom_call" | custom-call | tf_op jit(solution)/shard_map/pallas_call | solution.py:230
  21.2 0.1 collective-permute-start.7
  21.3 1.6 %collective-permute-start.8 = (f32[64,256]{1,0:T(8,128)S(1)}, f32[64,256]{1,0:T(8,128)S(1)}, u32[]{:S(2)}, u32[]{:S(2)}) collective-permute-start(f32[64,256]{1,0:T(8,128)S(1)} %get-tuple-element.27), channel_id=1, source_target_pairs={{0,2},{1,3},{2,0},{3,1},{4,6},{5,7},{6,4},{7,5},{8,10},{9,11},{10,... | collective-permute-start | bytes 196616 | tf_op jit(solution)/shard_map/ppermute | solution.py:30
  22.9 0.3 collective-permute-start.9
  23.2 2.6 %collective-permute-done.8.refs_2_ = f32[64,256]{1,0:T(8,128)S(1)} collective-permute-done((f32[64,256]{1,0:T(8,128)S(1)}, f32[64,256]{1,0:T(8,128)S(1)}, u32[]{:S(2)}, u32[]{:S(2)}) %collective-permute-start.8) | collective-permute-done | bytes 65568 | tf_op jit(solution)/shard_map/ppermute | solution.py:30
  25.8 1.1 %collective-permute-done.9.refs_3_ = f32[64,256]{1,0:T(8,128)S(1)} collective-permute-done((f32[64,256]{1,0:T(8,128)S(1)}, f32[64,256]{1,0:T(8,128)S(1)}, u32[]{:S(2)}, u32[]{:S(2)}) %collective-permute-start.9) | collective-permute-done | bytes 65568 | tf_op jit(solution)/shard_map/ppermute | solution.py:30
  26.9 0.2 shard_map.40
  27.1 2.3 %collective-permute-start.11 = (f32[48,128]{1,0:T(8,128)S(1)}, f32[48,128]{1,0:T(8,128)S(1)}, u32[]{:S(2)}, u32[]{:S(2)}) collective-permute-start(f32[48,128]{1,0:T(8,128)S(1)} %get-tuple-element.31), channel_id=1, source_target_pairs={{0,8},{4,12},{8,0},{12,4},{1,9},{5,13},{9,1},{13,5},{2,10},{6,14},... | collective-permute-start | bytes 73736 | tf_op jit(solution)/shard_map/ppermute | solution.py:30
  29.4 1.4 %collective-permute-start.12 = (f32[40,128]{1,0:T(8,128)S(1)}, f32[40,128]{1,0:T(8,128)S(1)}, u32[]{:S(2)}, u32[]{:S(2)}) collective-permute-start(f32[40,128]{1,0:T(8,128)S(1)} %get-tuple-element.32), channel_id=1, source_target_pairs={{0,12},{4,8},{8,4},{12,0},{1,13},{5,9},{9,5},{13,1},{2,14},{6,10},... | collective-permute-start | bytes 61448 | tf_op jit(solution)/shard_map/ppermute | solution.py:30
  30.8 0.5 %collective-permute-start.10 = (f32[32,128]{1,0:T(8,128)S(1)}, f32[32,128]{1,0:T(8,128)S(1)}, u32[]{:S(2)}, u32[]{:S(2)}) collective-permute-start(f32[32,128]{1,0:T(8,128)S(1)} %get-tuple-element.30), channel_id=1, source_target_pairs={{0,4},{4,0},{8,12},{12,8},{1,5},{5,1},{9,13},{13,9},{2,6},{6,2},{1... | collective-permute-start | bytes 49160 | tf_op jit(solution)/shard_map/ppermute | solution.py:30
  31.3 3.3 %collective-permute-done.10.one = f32[32,128]{1,0:T(8,128)S(1)} collective-permute-done((f32[32,128]{1,0:T(8,128)S(1)}, f32[32,128]{1,0:T(8,128)S(1)}, u32[]{:S(2)}, u32[]{:S(2)}) %collective-permute-start.10) | collective-permute-done | bytes 16416 | tf_op jit(solution)/shard_map/ppermute | solution.py:30
  34.5 0.5 %collective-permute-done.12.three = f32[40,128]{1,0:T(8,128)S(1)} collective-permute-done((f32[40,128]{1,0:T(8,128)S(1)}, f32[40,128]{1,0:T(8,128)S(1)}, u32[]{:S(2)}, u32[]{:S(2)}) %collective-permute-start.12) | collective-permute-done | bytes 20512 | tf_op jit(solution)/shard_map/ppermute | solution.py:30
  35.0 0.8 %shard_map.41 = f32[64,64]{1,0:T(8,128)} custom-call(f32[32,128]{1,0:T(8,128)S(1)} %get-tuple-element.29.kept, f32[32,128]{1,0:T(8,128)S(1)} %collective-permute-done.10.one, f32[48,128]{1,0:T(8,128)S(1)} %collective-permute-done.11.two, f32[40,128]{1,0:T(8,128)S(1)} %collective-permute-done.12.three), custom_call_target="tpu_custom_call" | custom-call | tf_op jit(solution)/shard_map/pallas_call | solution.py:245
  (11 shorter events, 0.0 us)
Async XLA Ops:
  0.0 6.4 %copy-start = (f32[64,256]{1,0:T(8,128)S(1)}, f32[64,256]{1,0:T(8,128)}, u32[]{:S(2)}) copy-start(f32[64,256]{1,0:T(8,128)} %density.1) | copy-start | bytes 196612
  0.0 6.4 %collective-permute-start.1 = (f32[1024,128]{1,0:T(8,128)}, f32[1024,128]{1,0:T(8,128)S(1)}, u32[]{:S(2)}, u32[]{:S(2)}) collective-permute-start(f32[1024,128]{1,0:T(8,128)} %bitcast.1), channel_id=1, source_target_pairs={{0,1},{1,0},{2,3},{3,2},{4,5},{5,4},{6,7},{7,6},{8,9},{9,8},{10,11... | collective-permute-start | bytes 1572872 | tf_op jit(solution)/shard_map/ppermute | solution.py:30
  1.5 3.7 %copy-start.1 = (s32[1,2]{1,0:T(1,128)S(1)}, s32[1,2]{1,0:T(1,128)}, u32[]{:S(2)}) copy-start(s32[1,2]{1,0:T(1,128)} %screen_ref.1) | copy-start | bytes 28
  1.5 10.9 %collective-permute-start.3 = (f32[256,128]{1,0:T(8,128)S(1)}, f32[256,128]{1,0:T(8,128)S(1)}, u32[]{:S(2)}, u32[]{:S(2)}) collective-permute-start(f32[256,128]{1,0:T(8,128)S(1)} %get-tuple-element.22), channel_id=1, source_target_pairs={{0,8},{4,12},{8,0},{12,4},{1,9},{5,13},{9,1},{13,5},{2,10},{6,14},... | collective-permute-start | bytes 393224 | tf_op jit(solution)/shard_map/ppermute | solution.py:30
  5.2 1.1 %collective-permute-start = (s32[1,2]{1,0:T(1,128)S(1)}, s32[1,2]{1,0:T(1,128)S(1)}, u32[]{:S(2)}, u32[]{:S(2)}) collective-permute-start(s32[1,2]{1,0:T(1,128)S(1)} %copy-done.1), channel_id=1, source_target_pairs={{0,1},{1,0},{2,3},{3,2},{4,5},{5,4},{6,7},{7,6},{8,9},{9,8},{10,11... | collective-permute-start | bytes 32 | tf_op jit(solution)/shard_map/ppermute | solution.py:30
  6.6 13.5 %collective-permute-start.2 = (f32[384,128]{1,0:T(8,128)S(1)}, f32[384,128]{1,0:T(8,128)S(1)}, u32[]{:S(2)}, u32[]{:S(2)}) collective-permute-start(f32[384,128]{1,0:T(8,128)S(1)} %get-tuple-element.21), channel_id=1, source_target_pairs={{0,4},{4,0},{8,12},{12,8},{1,5},{5,1},{9,13},{13,9},{2,6},{6,2},{1... | collective-permute-start | bytes 589832 | tf_op jit(solution)/shard_map/ppermute | solution.py:30
  8.3 11.9 %collective-permute-start.5 = (f32[320,128]{1,0:T(8,128)S(1)}, f32[320,128]{1,0:T(8,128)S(1)}, u32[]{:S(2)}, u32[]{:S(2)}) collective-permute-start(f32[320,128]{1,0:T(8,128)S(1)} %get-tuple-element.23), channel_id=1, source_target_pairs={{0,12},{4,8},{8,4},{12,0},{1,13},{5,9},{9,5},{13,1},{2,14},{6,10},... | collective-permute-start | bytes 491528 | tf_op jit(solution)/shard_map/ppermute | solution.py:30
  12.4 1.3 %collective-permute-start.4 = (f32[256,128]{1,0:T(8,128)S(1)}, f32[256,128]{1,0:T(8,128)S(1)}, u32[]{:S(2)}, u32[]{:S(2)}) collective-permute-start(f32[256,128]{1,0:T(8,128)S(1)} %collective-permute-done.3.two), channel_id=1, source_target_pairs={{0,1},{1,0},{2,3},{3,2},{4,5},{5,4},{6,7},{7,6},{8,9},{9,8},{10,11... | collective-permute-start | bytes 393224 | tf_op jit(solution)/shard_map/ppermute | solution.py:30
  12.4 7.7 %collective-permute-start.6 = (f32[40,128]{1,0:T(8,128)S(1)}, f32[40,128]{1,0:T(8,128)S(1)}, u32[]{:S(2)}, u32[]{:S(2)}) collective-permute-start(f32[40,128]{1,0:T(8,128)S(1)} %get-tuple-element.24), channel_id=1, source_target_pairs={{0,8},{4,12},{8,0},{12,4},{1,9},{5,13},{9,1},{13,5},{2,10},{6,14},... | collective-permute-start | bytes 61448 | tf_op jit(solution)/shard_map/ppermute | solution.py:30
  21.2 1.9 %collective-permute-start.7 = (f32[64,256]{1,0:T(8,128)S(1)}, f32[64,256]{1,0:T(8,128)S(1)}, u32[]{:S(2)}, u32[]{:S(2)}) collective-permute-start(f32[64,256]{1,0:T(8,128)S(1)} %get-tuple-element.26), channel_id=1, source_target_pairs={{0,1},{1,0},{2,3},{3,2},{4,5},{5,4},{6,7},{7,6},{8,9},{9,8},{10,11... | collective-permute-start | bytes 196616 | tf_op jit(solution)/shard_map/ppermute | solution.py:30
  21.3 4.5 %collective-permute-start.8 = (f32[64,256]{1,0:T(8,128)S(1)}, f32[64,256]{1,0:T(8,128)S(1)}, u32[]{:S(2)}, u32[]{:S(2)}) collective-permute-start(f32[64,256]{1,0:T(8,128)S(1)} %get-tuple-element.27), channel_id=1, source_target_pairs={{0,2},{1,3},{2,0},{3,1},{4,6},{5,7},{6,4},{7,5},{8,10},{9,11},{10,... | collective-permute-start | bytes 196616 | tf_op jit(solution)/shard_map/ppermute | solution.py:30
  22.9 4.0 %collective-permute-start.9 = (f32[64,256]{1,0:T(8,128)S(1)}, f32[64,256]{1,0:T(8,128)S(1)}, u32[]{:S(2)}, u32[]{:S(2)}) collective-permute-start(f32[64,256]{1,0:T(8,128)S(1)} %get-tuple-element.28), channel_id=1, source_target_pairs={{0,3},{1,2},{2,1},{3,0},{4,7},{5,6},{6,5},{7,4},{8,11},{9,10},{10,... | collective-permute-start | bytes 196616 | tf_op jit(solution)/shard_map/ppermute | solution.py:30
  27.1 7.9 %collective-permute-start.11 = (f32[48,128]{1,0:T(8,128)S(1)}, f32[48,128]{1,0:T(8,128)S(1)}, u32[]{:S(2)}, u32[]{:S(2)}) collective-permute-start(f32[48,128]{1,0:T(8,128)S(1)} %get-tuple-element.31), channel_id=1, source_target_pairs={{0,8},{4,12},{8,0},{12,4},{1,9},{5,13},{9,1},{13,5},{2,10},{6,14},... | collective-permute-start | bytes 73736 | tf_op jit(solution)/shard_map/ppermute | solution.py:30
  29.4 5.6 %collective-permute-start.12 = (f32[40,128]{1,0:T(8,128)S(1)}, f32[40,128]{1,0:T(8,128)S(1)}, u32[]{:S(2)}, u32[]{:S(2)}) collective-permute-start(f32[40,128]{1,0:T(8,128)S(1)} %get-tuple-element.32), channel_id=1, source_target_pairs={{0,12},{4,8},{8,4},{12,0},{1,13},{5,9},{9,5},{13,1},{2,14},{6,10},... | collective-permute-start | bytes 61448 | tf_op jit(solution)/shard_map/ppermute | solution.py:30
  30.8 3.7 %collective-permute-start.10 = (f32[32,128]{1,0:T(8,128)S(1)}, f32[32,128]{1,0:T(8,128)S(1)}, u32[]{:S(2)}, u32[]{:S(2)}) collective-permute-start(f32[32,128]{1,0:T(8,128)S(1)} %get-tuple-element.30), channel_id=1, source_target_pairs={{0,4},{4,0},{8,12},{12,8},{1,5},{5,1},{9,13},{13,9},{2,6},{6,2},{1... | collective-permute-start | bytes 49160 | tf_op jit(solution)/shard_map/ppermute | solution.py:30

commit v6 on v5

--- a/solution.py
+++ b/solution.py
@@ -90,9 +90,20 @@
                 raw[at:at + part_size, :] = own[pl.ds(p, part_size, stride=aux_local), :]
 
 
+def extend_kernel(raw, screen_ref, density_ref, out):
+    r, s = lax.axis_index("row"), lax.axis_index("sub")
+    at = raw.shape[0]
+    out[:at, :] = raw[...]
+    folded = fold(column_block(density_ref[...], r))
+    rows = folded.shape[0] // 2
+    out[at:at + rows, :] = jnp.where(s == 0, folded[:rows], folded[rows:])
+    direct, turned = lanes(screen_ref, 8)
+    even = lax.broadcasted_iota(jnp.int32, (8, 128), 0) % 2 == 0
+    out[at + rows:, :] = jnp.where(even, direct, turned).astype(F32)
+
+
 def far_kernel(share, screen_ref, other_ref, own_ref, par_ref, density_ref, *outs):
     r, s = lax.axis_index("row"), lax.axis_index("sub")
-    outs, extra = outs[:3], outs[3]
     size, orbitals = density_ref.shape
     aux_local = par_ref.shape[0] // size
     sources = [(lanes(places, size), part) for places, part in ((screen_ref, own_ref), (other_ref, par_ref))]
@@ -111,20 +122,12 @@
     for h in range(cut):
         outs[1][at + h * size:at + (h + 1) * size, :] = density[:, h * 128:(h + 1) * 128]
     outs[2][at:, :] = half_of(density, r // 2)
-    at = size // 2
-    extra[:at, :] = fold(column_block(density, r))
-    places = sources[0][0] + sources[1][0]
-    row = lax.broadcasted_iota(jnp.int32, (8, 128), 0) % 4
-    value = places[3][:8]
-    for i in range(3):
-        value = jnp.where(row == i, places[i][:8], value)
-    extra[at:, :] = value.astype(F32)
-
-
-def fock_kernel(share, own, one, two, two_other, three, extra2, density, *refs):
+
+
+def fock_kernel(share, own, one, two, two_other, three, density, *refs):
     outs, (dh, dl, bh, bl, total) = refs[:4], refs[4:]
-    r = lax.axis_index("row")
-    q = lax.axis_index("aux") * 2 + lax.axis_index("sub")
+    r, s = lax.axis_index("row"), lax.axis_index("sub")
+    q = lax.axis_index("aux") * 2 + s
     size, orbitals = density.shape
     cut = orbitals // 128
     h, odd = r // 2, r % 2 == 1
@@ -146,7 +149,9 @@
     here = three[at:at + size, :]
     mirror = jnp.transpose(jnp.concatenate([here, here], axis=0))
     mirror = jnp.where(odd, mirror[size:], mirror[:size])
-    corner = unfold(extra2[:size // 2, :])
+    at = 2 * share * size
+    a, b = [ref[at:at + size // 4, :] for ref in (two, two_other)]
+    corner = unfold(jnp.concatenate([jnp.where(s == 0, a, b), jnp.where(s == 0, b, a)], axis=0))
     corner = jnp.where(odd, pltpu.roll(corner, 64, 1), corner)
     low = lax.broadcasted_iota(jnp.int32, (size, 128), 1) < 64
     last = jnp.where(low ^ odd, corner, mirror)
@@ -162,10 +167,9 @@
                 high, lower = split(chunk[at:at + size, :])
                 bh[j, rows_of(k), x * 128:(x + 1) * 128] = high
                 bl[j, rows_of(k), x * 128:(x + 1) * 128] = lower
-    at = size // 2
+    at = 2 * share * size + size // 4
     spots = [
-        [jnp.broadcast_to(extra2[at + 2 * d + i:at + 2 * d + i + 1, :], (size, 128)) for i in range(2)]
-        for d in range(2)
+        [jnp.broadcast_to(ref[at + i:at + i + 1, :], (size, 128)) for i in range(2)] for ref in (two, two_other)
     ]
     for j in range(share):
         values = [jnp.zeros((size, 128), F32)] * cut
@@ -176,15 +180,17 @@
             high, lower = split(value)
             bh[j, rows_of(2), x * 128:(x + 1) * 128] = high
             bl[j, rows_of(2), x * 128:(x + 1) * 128] = lower
-    dot = functools.partial(jnp.dot, preferred_element_type=F32)
-    dot_t = lambda a, b: lax.dot_general(a, b, (((1,), (1,)), ((), ())), preferred_element_type=F32)
-    result = None
+    side = lambda *parts: jnp.concatenate(parts, axis=1)
+    whole = jnp.concatenate([dh[...], dl[...], dh[...]], axis=0)
+    lefts, rights = [], []
     for j in range(share):
         b1, b2 = bh[j], bl[j]
-        c = dot(b1, dh[...]) + (dot(b1, dl[...]) + dot(b2, dh[...]))
-        c1, c2 = split(c)
-        f = dot_t(c1, b1) + (dot_t(c1, b2) + dot_t(c2, b1))
-        result = f if result is None else result + f
+        c1, c2 = split(jnp.dot(side(b1, b1, b2), whole, preferred_element_type=F32))
+        lefts += [c1, c1, c2]
+        rights += [b1, b2, b1]
+    result = lax.dot_general(
+        side(*lefts), side(*rights), (((1,), (1,)), ((), ())), preferred_element_type=F32
+    )
     total[...] = result
     for dq in range(4):
         outs[dq][...] = total[pl.ds(pl.multiple_of((q ^ dq) * size, size), size), :]
@@ -220,13 +226,14 @@
         scratch=[pltpu.SemaphoreType.DMA((2,))],
         limit=FIRST,
     )(flat)
-    two = row(raw, 2)
-    own, one, three, extra = call(
+    extended = (raw.shape[0] + block_size // 4 + 8, 128)
+    two = row(call(extend_kernel, [extended], count=3)(raw, screen, density)[0], 2)
+    own, one, three = call(
         functools.partial(far_kernel, share),
-        [(packed + more, 128) for more in (0, orbitals // 2, block_size)] + [(block_size // 2 + 8, 128)],
+        [(packed + more, 128) for more in (0, orbitals // 2, block_size)],
         count=5,
     )(screen, core(screen), mine, other, density)
-    three, one, extra = row(three, 3), row(one, 1), row(extra, 2)
+    three, one = row(three, 3), row(one, 1)
     parts = call(
         functools.partial(fock_kernel, share),
         [(block_size, orbitals)] * 4,
@@ -237,10 +244,10 @@
             pltpu.VMEM((share, orbitals, orbitals), BF16),
             pltpu.VMEM((orbitals, orbitals), F32),
         ],
-        count=7,
-    )(own, one, two, core(two), three, extra, density)
+        count=6,
+    )(own, one, two, core(two), three, density)
     sums = [parts[0]] + [swap(parts[k], ("aux", "sub"), 4, k) for k in (1, 2, 3)]
-    cuts = call(cut_kernel, [(block_size // 2 + more, 2 * block_size) for more in (0, 0, 16, 8)], count=4)(*sums)
+    cuts = call(cut_kernel, [(block_size // 2 + more, 2 * block_size) for more in (0, 0, 8, 16)], count=4)(*sums)
     moved = [row(cuts[k], k) for k in (1, 2, 3)]
     return call(final_kernel, [(block_size, block_size)], count=4)(cuts[0], *moved)[0]
 

time: 35.9 us -> 35 us (0.975)
  waiting for transfers between devices: 19.6 us -> 18.3 us
  local copies, waits for them, and re-layouts: 0.01 us -> 0.64 us
    ppermute x13 -> x12, waiting for transfers between devices: 19.6 us -> 18.3 us  [swap(): return lax.ppermute(x, axes, [(a, a ^ k) for a in range(size)])]
    unnamed x4, local copies, waits for them, and re-layouts: 0.01 us -> 0.64 us
    ppermute x13 -> x12, starting transfers between devices: 12.7 us -> 12.4 us  [swap(): return lax.ppermute(x, axes, [(a, a ^ k) for a in range(size)])]
  transfers between devices with their start and end apart: 13 -> 12, of which waited for: 8 -> 8; matrix products, arithmetic and copies ran while one was open for 0% -> 0% of each run, Pallas kernels for 4% -> 4%
where the time goes in v6:
time: 35 us; the launch traced here: 34.9 us
  waiting for transfers between devices  18.3 us (52%)
  starting transfers between devices  12.4 us (35%)
  Pallas kernels  3.4 us (10%)
  local copies, waits for them, and re-layouts  0.64 us (2%)
    ppermute x12, waiting for transfers between devices, swap(): return lax.ppermute(x, axes, [(a, a ^ k) for a in range(size)])  18.3 us
    ppermute x12, starting transfers between devices, swap(): return lax.ppermute(x, axes, [(a, a ^ k) for a in range(size)])  12.4 us
    pallas_call x1, Pallas kernels, dealt_body(): call(functools.partial(near_kernel, share, block_size), [(2 * share * blo...  1.07 us
    pallas_call x1, Pallas kernels, dealt_body(): call(functools.partial(fock_kernel, share), [(block_size, orbitals)] * 4,...  1.02 us
    pallas_call x1, Pallas kernels, dealt_body(): call(final_kernel, [(block_size, block_size)], count=4)(cuts[0], *moved)[0]  0.76 us
  transfers between devices with their start and end apart: 12, of which 8 were waited for; matrix products, arithmetic and copies ran while one was open for 0% of the time, Pallas kernels for 4%

profile of v6, /device:TPU:0, one launch (start us, length us, event | category | flops | bytes accessed | tf_op | source)
XLA Modules:
  0.0 34.9 jit_solution(4543940945936584032)
XLA Ops:
  0.0 0.5 %collective-permute-start.1 = (f32[1024,128]{1,0:T(8,128)}, f32[1024,128]{1,0:T(8,128)S(1)}, u32[]{:S(2)}, u32[]{:S(2)}) collective-permute-start(f32[1024,128]{1,0:T(8,128)} %bitcast.1), channel_id=1, source_target_pairs={{0,1},{1,0},{2,3},{3,2},{4,5},{5,4},{6,7},{7,6},{8,9},{9,8},{10,11... | collective-permute-start | bytes 1572872 | tf_op jit(solution)/shard_map/ppermute | solution.py:30
  0.5 1.1 %shard_map.37 = (f32[256,128]{1,0:T(8,128)S(1)}, f32[1024,128]{1,0:T(8,128)S(1)}) custom-call(f32[1024,128]{1,0:T(8,128)} %bitcast.2), custom_call_target="tpu_custom_call" | custom-call | tf_op jit(solution)/shard_map/pallas_call | solution.py:222
  1.6 0.6 %copy-done.1 = s32[1,2]{1,0:T(1,128)S(1)} copy-done((s32[1,2]{1,0:T(1,128)S(1)}, s32[1,2]{1,0:T(1,128)}, u32[]{:S(2)}) %copy-start.1) | copy-done | bytes 32
  2.2 0.2 shard_map.39
  2.3 3.6 %collective-permute-start.3 = (f32[280,128]{1,0:T(8,128)S(1)}, f32[280,128]{1,0:T(8,128)S(1)}, u32[]{:S(2)}, u32[]{:S(2)}) collective-permute-start(f32[280,128]{1,0:T(8,128)S(1)} %shard_map.39), channel_id=1, source_target_pairs={{0,8},{4,12},{8,0},{12,4},{1,9},{5,13},{9,1},{13,5},{2,10},{6,14},... | collective-permute-start | bytes 430088 | tf_op jit(solution)/shard_map/ppermute | solution.py:30
  6.0 0.2 collective-permute-start
  6.2 0.9 %collective-permute-done.other_ref = s32[1,2]{1,0:T(1,128)S(1)} collective-permute-done((s32[1,2]{1,0:T(1,128)S(1)}, s32[1,2]{1,0:T(1,128)S(1)}, u32[]{:S(2)}, u32[]{:S(2)}) %collective-permute-start) | collective-permute-done | bytes 40 | tf_op jit(solution)/shard_map/ppermute | solution.py:30
  7.1 0.2 shard_map.38
  7.3 1.6 %collective-permute-start.2 = (f32[384,128]{1,0:T(8,128)S(1)}, f32[384,128]{1,0:T(8,128)S(1)}, u32[]{:S(2)}, u32[]{:S(2)}) collective-permute-start(f32[384,128]{1,0:T(8,128)S(1)} %get-tuple-element.20), channel_id=1, source_target_pairs={{0,4},{4,0},{8,12},{12,8},{1,5},{5,1},{9,13},{13,9},{2,6},{6,2},{1... | collective-permute-start | bytes 589832 | tf_op jit(solution)/shard_map/ppermute | solution.py:30
  9.1 4.6 %collective-permute-done.3.two = f32[280,128]{1,0:T(8,128)S(1)} collective-permute-done((f32[280,128]{1,0:T(8,128)S(1)}, f32[280,128]{1,0:T(8,128)S(1)}, u32[]{:S(2)}, u32[]{:S(2)}) %collective-permute-start.3) | collective-permute-done | bytes 143392 | tf_op jit(solution)/shard_map/ppermute | solution.py:30
  13.7 1.4 %collective-permute-done.4.two_other = f32[280,128]{1,0:T(8,128)S(1)} collective-permute-done((f32[280,128]{1,0:T(8,128)S(1)}, f32[280,128]{1,0:T(8,128)S(1)}, u32[]{:S(2)}, u32[]{:S(2)}) %collective-permute-start.4) | collective-permute-done | bytes 143392 | tf_op jit(solution)/shard_map/ppermute | solution.py:30
  15.1 4.3 %collective-permute-done.5.three = f32[320,128]{1,0:T(8,128)S(1)} collective-permute-done((f32[320,128]{1,0:T(8,128)S(1)}, f32[320,128]{1,0:T(8,128)S(1)}, u32[]{:S(2)}, u32[]{:S(2)}) %collective-permute-start.5) | collective-permute-done | bytes 163872 | tf_op jit(solution)/shard_map/ppermute | solution.py:30
  19.4 0.5 %collective-permute-done.2.one = f32[384,128]{1,0:T(8,128)S(1)} collective-permute-done((f32[384,128]{1,0:T(8,128)S(1)}, f32[384,128]{1,0:T(8,128)S(1)}, u32[]{:S(2)}, u32[]{:S(2)}) %collective-permute-start.2) | collective-permute-done | bytes 196640 | tf_op jit(solution)/shard_map/ppermute | solution.py:30
  19.8 1.0 %shard_map.40 = (f32[64,256]{1,0:T(8,128)S(1)}, f32[64,256]{1,0:T(8,128)S(1)}, f32[64,256]{1,0:T(8,128)S(1)}, f32[64,256]{1,0:T(8,128)S(1)}) custom-call(f32[256,128]{1,0:T(8,128)S(1)} %get-tuple-element.19.own, f32[384,128]{1,0:T(8,128)S(1)} %collective-permute-done.2.one, f32[280,128]{1,0:T(8,128)S(1)} %collective-permute-done.3.two, ...), custom_call_target="tpu_custom_call" | custom-call | tf_op jit(solution)/shard_map/pallas_call | solution.py:237
  20.9 1.6 %collective-permute-start.7 = (f32[64,256]{1,0:T(8,128)S(1)}, f32[64,256]{1,0:T(8,128)S(1)}, u32[]{:S(2)}, u32[]{:S(2)}) collective-permute-start(f32[64,256]{1,0:T(8,128)S(1)} %get-tuple-element.25), channel_id=1, source_target_pairs={{0,2},{1,3},{2,0},{3,1},{4,6},{5,7},{6,4},{7,5},{8,10},{9,11},{10,... | collective-permute-start | bytes 196616 | tf_op jit(solution)/shard_map/ppermute | solution.py:30
  22.6 0.3 collective-permute-start.8
  22.8 2.6 %collective-permute-done.7.refs_2_ = f32[64,256]{1,0:T(8,128)S(1)} collective-permute-done((f32[64,256]{1,0:T(8,128)S(1)}, f32[64,256]{1,0:T(8,128)S(1)}, u32[]{:S(2)}, u32[]{:S(2)}) %collective-permute-start.7) | collective-permute-done | bytes 65568 | tf_op jit(solution)/shard_map/ppermute | solution.py:30
  25.5 1.1 %collective-permute-done.8.refs_3_ = f32[64,256]{1,0:T(8,128)S(1)} collective-permute-done((f32[64,256]{1,0:T(8,128)S(1)}, f32[64,256]{1,0:T(8,128)S(1)}, u32[]{:S(2)}, u32[]{:S(2)}) %collective-permute-start.8) | collective-permute-done | bytes 65568 | tf_op jit(solution)/shard_map/ppermute | solution.py:30
  26.6 0.2 shard_map.41
  26.8 2.5 %collective-permute-start.11 = (f32[48,128]{1,0:T(8,128)S(1)}, f32[48,128]{1,0:T(8,128)S(1)}, u32[]{:S(2)}, u32[]{:S(2)}) collective-permute-start(f32[48,128]{1,0:T(8,128)S(1)} %get-tuple-element.30), channel_id=1, source_target_pairs={{0,12},{4,8},{8,4},{12,0},{1,13},{5,9},{9,5},{13,1},{2,14},{6,10},... | collective-permute-start | bytes 73736 | tf_op jit(solution)/shard_map/ppermute | solution.py:30
  29.2 0.9 %collective-permute-start.10 = (f32[40,128]{1,0:T(8,128)S(1)}, f32[40,128]{1,0:T(8,128)S(1)}, u32[]{:S(2)}, u32[]{:S(2)}) collective-permute-start(f32[40,128]{1,0:T(8,128)S(1)} %get-tuple-element.29), channel_id=1, source_target_pairs={{0,8},{4,12},{8,0},{12,4},{1,9},{5,13},{9,1},{13,5},{2,10},{6,14},... | collective-permute-start | bytes 61448 | tf_op jit(solution)/shard_map/ppermute | solution.py:30
  30.2 1.0 %collective-permute-start.9 = (f32[32,128]{1,0:T(8,128)S(1)}, f32[32,128]{1,0:T(8,128)S(1)}, u32[]{:S(2)}, u32[]{:S(2)}) collective-permute-start(f32[32,128]{1,0:T(8,128)S(1)} %get-tuple-element.28), channel_id=1, source_target_pairs={{0,4},{4,0},{8,12},{12,8},{1,5},{5,1},{9,13},{13,9},{2,6},{6,2},{1... | collective-permute-start | bytes 49160 | tf_op jit(solution)/shard_map/ppermute | solution.py:30
  31.2 2.9 %collective-permute-done.9.one = f32[32,128]{1,0:T(8,128)S(1)} collective-permute-done((f32[32,128]{1,0:T(8,128)S(1)}, f32[32,128]{1,0:T(8,128)S(1)}, u32[]{:S(2)}, u32[]{:S(2)}) %collective-permute-start.9) | collective-permute-done | bytes 16416 | tf_op jit(solution)/shard_map/ppermute | solution.py:30
  34.1 0.8 %shard_map.42 = f32[64,64]{1,0:T(8,128)} custom-call(f32[32,128]{1,0:T(8,128)S(1)} %get-tuple-element.27.kept, f32[32,128]{1,0:T(8,128)S(1)} %collective-permute-done.9.one, f32[40,128]{1,0:T(8,128)S(1)} %collective-permute-done.10.two, f32[48,128]{1,0:T(8,128)S(1)} %collective-permute-done.11.three), custom_call_target="tpu_custom_call" | custom-call | tf_op jit(solution)/shard_map/pallas_call | solution.py:252
  (10 shorter events, 0.2 us)
Async XLA Ops:
  0.0 1.5 %copy-start = (f32[64,256]{1,0:T(8,128)S(1)}, f32[64,256]{1,0:T(8,128)}, u32[]{:S(2)}) copy-start(f32[64,256]{1,0:T(8,128)} %density.1) | copy-start | bytes 196612
  0.0 7.1 %collective-permute-start.1 = (f32[1024,128]{1,0:T(8,128)}, f32[1024,128]{1,0:T(8,128)S(1)}, u32[]{:S(2)}, u32[]{:S(2)}) collective-permute-start(f32[1024,128]{1,0:T(8,128)} %bitcast.1), channel_id=1, source_target_pairs={{0,1},{1,0},{2,3},{3,2},{4,5},{5,4},{6,7},{7,6},{8,9},{9,8},{10,11... | collective-permute-start | bytes 1572872 | tf_op jit(solution)/shard_map/ppermute | solution.py:30
  1.5 0.7 %copy-start.1 = (s32[1,2]{1,0:T(1,128)S(1)}, s32[1,2]{1,0:T(1,128)}, u32[]{:S(2)}) copy-start(s32[1,2]{1,0:T(1,128)} %screen_ref.3) | copy-start | bytes 28
  2.3 11.4 %collective-permute-start.3 = (f32[280,128]{1,0:T(8,128)S(1)}, f32[280,128]{1,0:T(8,128)S(1)}, u32[]{:S(2)}, u32[]{:S(2)}) collective-permute-start(f32[280,128]{1,0:T(8,128)S(1)} %shard_map.39), channel_id=1, source_target_pairs={{0,8},{4,12},{8,0},{12,4},{1,9},{5,13},{9,1},{13,5},{2,10},{6,14},... | collective-permute-start | bytes 430088 | tf_op jit(solution)/shard_map/ppermute | solution.py:30
  6.0 1.1 %collective-permute-start = (s32[1,2]{1,0:T(1,128)S(1)}, s32[1,2]{1,0:T(1,128)S(1)}, u32[]{:S(2)}, u32[]{:S(2)}) collective-permute-start(s32[1,2]{1,0:T(1,128)S(1)} %copy-done.1), channel_id=1, source_target_pairs={{0,1},{1,0},{2,3},{3,2},{4,5},{5,4},{6,7},{7,6},{8,9},{9,8},{10,11... | collective-permute-start | bytes 32 | tf_op jit(solution)/shard_map/ppermute | solution.py:30
  7.3 12.5 %collective-permute-start.2 = (f32[384,128]{1,0:T(8,128)S(1)}, f32[384,128]{1,0:T(8,128)S(1)}, u32[]{:S(2)}, u32[]{:S(2)}) collective-permute-start(f32[384,128]{1,0:T(8,128)S(1)} %get-tuple-element.20), channel_id=1, source_target_pairs={{0,4},{4,0},{8,12},{12,8},{1,5},{5,1},{9,13},{13,9},{2,6},{6,2},{1... | collective-permute-start | bytes 589832 | tf_op jit(solution)/shard_map/ppermute | solution.py:30
  9.0 10.4 %collective-permute-start.5 = (f32[320,128]{1,0:T(8,128)S(1)}, f32[320,128]{1,0:T(8,128)S(1)}, u32[]{:S(2)}, u32[]{:S(2)}) collective-permute-start(f32[320,128]{1,0:T(8,128)S(1)} %get-tuple-element.22), channel_id=1, source_target_pairs={{0,12},{4,8},{8,4},{12,0},{1,13},{5,9},{9,5},{13,1},{2,14},{6,10},... | collective-permute-start | bytes 491528 | tf_op jit(solution)/shard_map/ppermute | solution.py:30
  13.7 1.4 %collective-permute-start.4 = (f32[280,128]{1,0:T(8,128)S(1)}, f32[280,128]{1,0:T(8,128)S(1)}, u32[]{:S(2)}, u32[]{:S(2)}) collective-permute-start(f32[280,128]{1,0:T(8,128)S(1)} %collective-permute-done.3.two), channel_id=1, source_target_pairs={{0,1},{1,0},{2,3},{3,2},{4,5},{5,4},{6,7},{7,6},{8,9},{9,8},{10,11... | collective-permute-start | bytes 430088 | tf_op jit(solution)/shard_map/ppermute | solution.py:30
  20.9 1.9 %collective-permute-start.6 = (f32[64,256]{1,0:T(8,128)S(1)}, f32[64,256]{1,0:T(8,128)S(1)}, u32[]{:S(2)}, u32[]{:S(2)}) collective-permute-start(f32[64,256]{1,0:T(8,128)S(1)} %get-tuple-element.24), channel_id=1, source_target_pairs={{0,1},{1,0},{2,3},{3,2},{4,5},{5,4},{6,7},{7,6},{8,9},{9,8},{10,11... | collective-permute-start | bytes 196616 | tf_op jit(solution)/shard_map/ppermute | solution.py:30
  20.9 4.5 %collective-permute-start.7 = (f32[64,256]{1,0:T(8,128)S(1)}, f32[64,256]{1,0:T(8,128)S(1)}, u32[]{:S(2)}, u32[]{:S(2)}) collective-permute-start(f32[64,256]{1,0:T(8,128)S(1)} %get-tuple-element.25), channel_id=1, source_target_pairs={{0,2},{1,3},{2,0},{3,1},{4,6},{5,7},{6,4},{7,5},{8,10},{9,11},{10,... | collective-permute-start | bytes 196616 | tf_op jit(solution)/shard_map/ppermute | solution.py:30
  22.6 4.0 %collective-permute-start.8 = (f32[64,256]{1,0:T(8,128)S(1)}, f32[64,256]{1,0:T(8,128)S(1)}, u32[]{:S(2)}, u32[]{:S(2)}) collective-permute-start(f32[64,256]{1,0:T(8,128)S(1)} %get-tuple-element.26), channel_id=1, source_target_pairs={{0,3},{1,2},{2,1},{3,0},{4,7},{5,6},{6,5},{7,4},{8,11},{9,10},{10,... | collective-permute-start | bytes 196616 | tf_op jit(solution)/shard_map/ppermute | solution.py:30
  26.8 7.3 %collective-permute-start.11 = (f32[48,128]{1,0:T(8,128)S(1)}, f32[48,128]{1,0:T(8,128)S(1)}, u32[]{:S(2)}, u32[]{:S(2)}) collective-permute-start(f32[48,128]{1,0:T(8,128)S(1)} %get-tuple-element.30), channel_id=1, source_target_pairs={{0,12},{4,8},{8,4},{12,0},{1,13},{5,9},{9,5},{13,1},{2,14},{6,10},... | collective-permute-start | bytes 73736 | tf_op jit(solution)/shard_map/ppermute | solution.py:30
  29.2 4.9 %collective-permute-start.10 = (f32[40,128]{1,0:T(8,128)S(1)}, f32[40,128]{1,0:T(8,128)S(1)}, u32[]{:S(2)}, u32[]{:S(2)}) collective-permute-start(f32[40,128]{1,0:T(8,128)S(1)} %get-tuple-element.29), channel_id=1, source_target_pairs={{0,8},{4,12},{8,0},{12,4},{1,9},{5,13},{9,1},{13,5},{2,10},{6,14},... | collective-permute-start | bytes 61448 | tf_op jit(solution)/shard_map/ppermute | solution.py:30
  30.2 3.9 %collective-permute-start.9 = (f32[32,128]{1,0:T(8,128)S(1)}, f32[32,128]{1,0:T(8,128)S(1)}, u32[]{:S(2)}, u32[]{:S(2)}) collective-permute-start(f32[32,128]{1,0:T(8,128)S(1)} %get-tuple-element.28), channel_id=1, source_target_pairs={{0,4},{4,0},{8,12},{12,8},{1,5},{5,1},{9,13},{13,9},{2,6},{6,2},{1... | collective-permute-start | bytes 49160 | tf_op jit(solution)/shard_map/ppermute | solution.py:30

commit v7 on v6

--- a/solution.py
+++ b/solution.py
@@ -90,14 +90,14 @@
                 raw[at:at + part_size, :] = own[pl.ds(p, part_size, stride=aux_local), :]
 
 
-def extend_kernel(raw, screen_ref, density_ref, out):
+def extend_kernel(raw, other_ref, density_ref, out):
     r, s = lax.axis_index("row"), lax.axis_index("sub")
     at = raw.shape[0]
     out[:at, :] = raw[...]
     folded = fold(column_block(density_ref[...], r))
     rows = folded.shape[0] // 2
     out[at:at + rows, :] = jnp.where(s == 0, folded[:rows], folded[rows:])
-    direct, turned = lanes(screen_ref, 8)
+    direct, turned = lanes(other_ref, 8)
     even = lax.broadcasted_iota(jnp.int32, (8, 128), 0) % 2 == 0
     out[at + rows:, :] = jnp.where(even, direct, turned).astype(F32)
 
@@ -169,7 +169,7 @@
                 bl[j, rows_of(k), x * 128:(x + 1) * 128] = lower
     at = 2 * share * size + size // 4
     spots = [
-        [jnp.broadcast_to(ref[at + i:at + i + 1, :], (size, 128)) for i in range(2)] for ref in (two, two_other)
+        [jnp.broadcast_to(ref[at + i:at + i + 1, :], (size, 128)) for i in range(2)] for ref in (two_other, two)
     ]
     for j in range(share):
         values = [jnp.zeros((size, 128), F32)] * cut
@@ -227,12 +227,13 @@
         limit=FIRST,
     )(flat)
     extended = (raw.shape[0] + block_size // 4 + 8, 128)
-    two = row(call(extend_kernel, [extended], count=3)(raw, screen, density)[0], 2)
+    other_screen = core(screen)
+    two = row(call(extend_kernel, [extended], count=3)(raw, other_screen, density)[0], 2)
     own, one, three = call(
         functools.partial(far_kernel, share),
         [(packed + more, 128) for more in (0, orbitals // 2, block_size)],
         count=5,
-    )(screen, core(screen), mine, other, density)
+    )(screen, other_screen, mine, other, density)
     three, one = row(three, 3), row(one, 1)
     parts = call(
         functools.partial(fock_kernel, share),

time: 35 us -> 34.9 us (level)
  local copies, waits for them, and re-layouts: 0.64 us -> 0.2 us
    unnamed x4, local copies, waits for them, and re-layouts: 0.64 us -> 0.2 us
  transfers between devices with their start and end apart: 12 -> 12, of which waited for: 8 -> 6; matrix products, arithmetic and copies ran while one was open for 0% -> 0% of each run, Pallas kernels for 4% -> 4%
where the time goes in v7:
time: 34.9 us; the launch traced here: 34.7 us
  waiting for transfers between devices  18.3 us (52%)
  starting transfers between devices  12.7 us (36%)
  Pallas kernels  3.41 us (10%)
    ppermute x12, waiting for transfers between devices, swap(): return lax.ppermute(x, axes, [(a, a ^ k) for a in range(size)])  18.3 us
    ppermute x12, starting transfers between devices, swap(): return lax.ppermute(x, axes, [(a, a ^ k) for a in range(size)])  12.7 us
    pallas_call x1, Pallas kernels, dealt_body(): call(functools.partial(near_kernel, share, block_size), [(2 * share * blo...  1.07 us
    pallas_call x1, Pallas kernels, dealt_body(): call(functools.partial(fock_kernel, share), [(block_size, orbitals)] * 4,...  1.02 us
    pallas_call x1, Pallas kernels, dealt_body(): call(final_kernel, [(block_size, block_size)], count=4)(cuts[0], *moved)[0]  0.76 us
  transfers between devices with their start and end apart: 12, of which 6 were waited for; matrix products, arithmetic and copies ran while one was open for 0% of the time, Pallas kernels for 4%

profile of v7, /device:TPU:0, one launch (start us, length us, event | category | flops | bytes accessed | tf_op | source)
XLA Modules:
  0.0 34.7 jit_solution(10306353871897050321)
XLA Ops:
  0.0 0.5 %collective-permute-start.1 = (f32[1024,128]{1,0:T(8,128)}, f32[1024,128]{1,0:T(8,128)S(1)}, u32[]{:S(2)}, u32[]{:S(2)}) collective-permute-start(f32[1024,128]{1,0:T(8,128)} %bitcast.1), channel_id=1, source_target_pairs={{0,1},{1,0},{2,3},{3,2},{4,5},{5,4},{6,7},{7,6},{8,9},{9,8},{10,11... | collective-permute-start | bytes 1572872 | tf_op jit(solution)/shard_map/ppermute | solution.py:30
  0.5 0.2 copy-done.1
  0.7 0.5 %collective-permute-start = (s32[1,2]{1,0:T(1,128)S(1)}, s32[1,2]{1,0:T(1,128)S(1)}, u32[]{:S(2)}, u32[]{:S(2)}) collective-permute-start(s32[1,2]{1,0:T(1,128)S(1)} %copy-done.1), channel_id=1, source_target_pairs={{0,1},{1,0},{2,3},{3,2},{4,5},{5,4},{6,7},{7,6},{8,9},{9,8},{10,11... | collective-permute-start | bytes 32 | tf_op jit(solution)/shard_map/ppermute | solution.py:30
  1.1 1.1 %shard_map.37 = (f32[256,128]{1,0:T(8,128)S(1)}, f32[1024,128]{1,0:T(8,128)S(1)}) custom-call(f32[1024,128]{1,0:T(8,128)} %bitcast.2), custom_call_target="tpu_custom_call" | custom-call | tf_op jit(solution)/shard_map/pallas_call | solution.py:222
  2.2 0.0 collective-permute-done.other_ref
  2.2 0.2 shard_map.39
  2.4 3.7 %collective-permute-start.3 = (f32[280,128]{1,0:T(8,128)S(1)}, f32[280,128]{1,0:T(8,128)S(1)}, u32[]{:S(2)}, u32[]{:S(2)}) collective-permute-start(f32[280,128]{1,0:T(8,128)S(1)} %shard_map.39), channel_id=1, source_target_pairs={{0,8},{4,12},{8,0},{12,4},{1,9},{5,13},{9,1},{13,5},{2,10},{6,14},... | collective-permute-start | bytes 430088 | tf_op jit(solution)/shard_map/ppermute | solution.py:30
  6.1 0.2 shard_map.38
  6.4 1.6 %collective-permute-start.2 = (f32[384,128]{1,0:T(8,128)S(1)}, f32[384,128]{1,0:T(8,128)S(1)}, u32[]{:S(2)}, u32[]{:S(2)}) collective-permute-start(f32[384,128]{1,0:T(8,128)S(1)} %get-tuple-element.20), channel_id=1, source_target_pairs={{0,4},{4,0},{8,12},{12,8},{1,5},{5,1},{9,13},{13,9},{2,6},{6,2},{1... | collective-permute-start | bytes 589832 | tf_op jit(solution)/shard_map/ppermute | solution.py:30
  8.0 5.8 %collective-permute-done.3.two = f32[280,128]{1,0:T(8,128)S(1)} collective-permute-done((f32[280,128]{1,0:T(8,128)S(1)}, f32[280,128]{1,0:T(8,128)S(1)}, u32[]{:S(2)}, u32[]{:S(2)}) %collective-permute-start.3) | collective-permute-done | bytes 143392 | tf_op jit(solution)/shard_map/ppermute | solution.py:30
  13.8 1.4 %collective-permute-done.4.two_other = f32[280,128]{1,0:T(8,128)S(1)} collective-permute-done((f32[280,128]{1,0:T(8,128)S(1)}, f32[280,128]{1,0:T(8,128)S(1)}, u32[]{:S(2)}, u32[]{:S(2)}) %collective-permute-start.4) | collective-permute-done | bytes 143392 | tf_op jit(solution)/shard_map/ppermute | solution.py:30
  15.2 4.2 %collective-permute-done.5.three = f32[320,128]{1,0:T(8,128)S(1)} collective-permute-done((f32[320,128]{1,0:T(8,128)S(1)}, f32[320,128]{1,0:T(8,128)S(1)}, u32[]{:S(2)}, u32[]{:S(2)}) %collective-permute-start.5) | collective-permute-done | bytes 163872 | tf_op jit(solution)/shard_map/ppermute | solution.py:30
  19.3 1.0 %shard_map.40 = (f32[64,256]{1,0:T(8,128)S(1)}, f32[64,256]{1,0:T(8,128)S(1)}, f32[64,256]{1,0:T(8,128)S(1)}, f32[64,256]{1,0:T(8,128)S(1)}) custom-call(f32[256,128]{1,0:T(8,128)S(1)} %get-tuple-element.19.own, f32[384,128]{1,0:T(8,128)S(1)} %collective-permute-done.2.one, f32[280,128]{1,0:T(8,128)S(1)} %collective-permute-done.3.two, ...), custom_call_target="tpu_custom_call" | custom-call | tf_op jit(solution)/shard_map/pallas_call | solution.py:238
  20.4 0.1 collective-permute-start.6
  20.4 1.6 %collective-permute-start.7 = (f32[64,256]{1,0:T(8,128)S(1)}, f32[64,256]{1,0:T(8,128)S(1)}, u32[]{:S(2)}, u32[]{:S(2)}) collective-permute-start(f32[64,256]{1,0:T(8,128)S(1)} %get-tuple-element.25), channel_id=1, source_target_pairs={{0,2},{1,3},{2,0},{3,1},{4,6},{5,7},{6,4},{7,5},{8,10},{9,11},{10,... | collective-permute-start | bytes 196616 | tf_op jit(solution)/shard_map/ppermute | solution.py:30
  22.0 0.3 collective-permute-start.8
  22.3 2.6 %collective-permute-done.7.refs_2_ = f32[64,256]{1,0:T(8,128)S(1)} collective-permute-done((f32[64,256]{1,0:T(8,128)S(1)}, f32[64,256]{1,0:T(8,128)S(1)}, u32[]{:S(2)}, u32[]{:S(2)}) %collective-permute-start.7) | collective-permute-done | bytes 65568 | tf_op jit(solution)/shard_map/ppermute | solution.py:30
  25.0 1.1 %collective-permute-done.8.refs_3_ = f32[64,256]{1,0:T(8,128)S(1)} collective-permute-done((f32[64,256]{1,0:T(8,128)S(1)}, f32[64,256]{1,0:T(8,128)S(1)}, u32[]{:S(2)}, u32[]{:S(2)}) %collective-permute-start.8) | collective-permute-done | bytes 65568 | tf_op jit(solution)/shard_map/ppermute | solution.py:30
  26.0 0.2 shard_map.41
  26.2 2.5 %collective-permute-start.11 = (f32[48,128]{1,0:T(8,128)S(1)}, f32[48,128]{1,0:T(8,128)S(1)}, u32[]{:S(2)}, u32[]{:S(2)}) collective-permute-start(f32[48,128]{1,0:T(8,128)S(1)} %get-tuple-element.30), channel_id=1, source_target_pairs={{0,12},{4,8},{8,4},{12,0},{1,13},{5,9},{9,5},{13,1},{2,14},{6,10},... | collective-permute-start | bytes 73736 | tf_op jit(solution)/shard_map/ppermute | solution.py:30
  28.8 1.4 %collective-permute-start.10 = (f32[40,128]{1,0:T(8,128)S(1)}, f32[40,128]{1,0:T(8,128)S(1)}, u32[]{:S(2)}, u32[]{:S(2)}) collective-permute-start(f32[40,128]{1,0:T(8,128)S(1)} %get-tuple-element.29), channel_id=1, source_target_pairs={{0,8},{4,12},{8,0},{12,4},{1,9},{5,13},{9,1},{13,5},{2,10},{6,14},... | collective-permute-start | bytes 61448 | tf_op jit(solution)/shard_map/ppermute | solution.py:30
  30.2 0.5 %collective-permute-start.9 = (f32[32,128]{1,0:T(8,128)S(1)}, f32[32,128]{1,0:T(8,128)S(1)}, u32[]{:S(2)}, u32[]{:S(2)}) collective-permute-start(f32[32,128]{1,0:T(8,128)S(1)} %get-tuple-element.28), channel_id=1, source_target_pairs={{0,4},{4,0},{8,12},{12,8},{1,5},{5,1},{9,13},{13,9},{2,6},{6,2},{1... | collective-permute-start | bytes 49160 | tf_op jit(solution)/shard_map/ppermute | solution.py:30
  30.7 3.3 %collective-permute-done.9.one = f32[32,128]{1,0:T(8,128)S(1)} collective-permute-done((f32[32,128]{1,0:T(8,128)S(1)}, f32[32,128]{1,0:T(8,128)S(1)}, u32[]{:S(2)}, u32[]{:S(2)}) %collective-permute-start.9) | collective-permute-done | bytes 16416 | tf_op jit(solution)/shard_map/ppermute | solution.py:30
  33.9 0.8 %shard_map.42 = f32[64,64]{1,0:T(8,128)} custom-call(f32[32,128]{1,0:T(8,128)S(1)} %get-tuple-element.27.kept, f32[32,128]{1,0:T(8,128)S(1)} %collective-permute-done.9.one, f32[40,128]{1,0:T(8,128)S(1)} %collective-permute-done.10.two, f32[48,128]{1,0:T(8,128)S(1)} %collective-permute-done.11.three), custom_call_target="tpu_custom_call" | custom-call | tf_op jit(solution)/shard_map/pallas_call | solution.py:253
  (10 shorter events, 0.0 us)
Async XLA Ops:
  0.0 0.7 %copy-start.1 = (s32[1,2]{1,0:T(1,128)S(1)}, s32[1,2]{1,0:T(1,128)}, u32[]{:S(2)}) copy-start(s32[1,2]{1,0:T(1,128)} %screen_ref.1) | copy-start | bytes 28
  0.0 2.2 %copy-start = (f32[64,256]{1,0:T(8,128)S(1)}, f32[64,256]{1,0:T(8,128)}, u32[]{:S(2)}) copy-start(f32[64,256]{1,0:T(8,128)} %density.1) | copy-start | bytes 196612
  0.0 6.1 %collective-permute-start.1 = (f32[1024,128]{1,0:T(8,128)}, f32[1024,128]{1,0:T(8,128)S(1)}, u32[]{:S(2)}, u32[]{:S(2)}) collective-permute-start(f32[1024,128]{1,0:T(8,128)} %bitcast.1), channel_id=1, source_target_pairs={{0,1},{1,0},{2,3},{3,2},{4,5},{5,4},{6,7},{7,6},{8,9},{9,8},{10,11... | collective-permute-start | bytes 1572872 | tf_op jit(solution)/shard_map/ppermute | solution.py:30
  0.7 1.5 %collective-permute-start = (s32[1,2]{1,0:T(1,128)S(1)}, s32[1,2]{1,0:T(1,128)S(1)}, u32[]{:S(2)}, u32[]{:S(2)}) collective-permute-start(s32[1,2]{1,0:T(1,128)S(1)} %copy-done.1), channel_id=1, source_target_pairs={{0,1},{1,0},{2,3},{3,2},{4,5},{5,4},{6,7},{7,6},{8,9},{9,8},{10,11... | collective-permute-start | bytes 32 | tf_op jit(solution)/shard_map/ppermute | solution.py:30
  2.4 11.4 %collective-permute-start.3 = (f32[280,128]{1,0:T(8,128)S(1)}, f32[280,128]{1,0:T(8,128)S(1)}, u32[]{:S(2)}, u32[]{:S(2)}) collective-permute-start(f32[280,128]{1,0:T(8,128)S(1)} %shard_map.39), channel_id=1, source_target_pairs={{0,8},{4,12},{8,0},{12,4},{1,9},{5,13},{9,1},{13,5},{2,10},{6,14},... | collective-permute-start | bytes 430088 | tf_op jit(solution)/shard_map/ppermute | solution.py:30
  6.4 13.0 %collective-permute-start.2 = (f32[384,128]{1,0:T(8,128)S(1)}, f32[384,128]{1,0:T(8,128)S(1)}, u32[]{:S(2)}, u32[]{:S(2)}) collective-permute-start(f32[384,128]{1,0:T(8,128)S(1)} %get-tuple-element.20), channel_id=1, source_target_pairs={{0,4},{4,0},{8,12},{12,8},{1,5},{5,1},{9,13},{13,9},{2,6},{6,2},{1... | collective-permute-start | bytes 589832 | tf_op jit(solution)/shard_map/ppermute | solution.py:30
  8.0 11.3 %collective-permute-start.5 = (f32[320,128]{1,0:T(8,128)S(1)}, f32[320,128]{1,0:T(8,128)S(1)}, u32[]{:S(2)}, u32[]{:S(2)}) collective-permute-start(f32[320,128]{1,0:T(8,128)S(1)} %get-tuple-element.22), channel_id=1, source_target_pairs={{0,12},{4,8},{8,4},{12,0},{1,13},{5,9},{9,5},{13,1},{2,14},{6,10},... | collective-permute-start | bytes 491528 | tf_op jit(solution)/shard_map/ppermute | solution.py:30
  13.8 1.4 %collective-permute-start.4 = (f32[280,128]{1,0:T(8,128)S(1)}, f32[280,128]{1,0:T(8,128)S(1)}, u32[]{:S(2)}, u32[]{:S(2)}) collective-permute-start(f32[280,128]{1,0:T(8,128)S(1)} %collective-permute-done.3.two), channel_id=1, source_target_pairs={{0,1},{1,0},{2,3},{3,2},{4,5},{5,4},{6,7},{7,6},{8,9},{9,8},{10,11... | collective-permute-start | bytes 430088 | tf_op jit(solution)/shard_map/ppermute | solution.py:30
  20.4 1.9 %collective-permute-start.6 = (f32[64,256]{1,0:T(8,128)S(1)}, f32[64,256]{1,0:T(8,128)S(1)}, u32[]{:S(2)}, u32[]{:S(2)}) collective-permute-start(f32[64,256]{1,0:T(8,128)S(1)} %get-tuple-element.24), channel_id=1, source_target_pairs={{0,1},{1,0},{2,3},{3,2},{4,5},{5,4},{6,7},{7,6},{8,9},{9,8},{10,11... | collective-permute-start | bytes 196616 | tf_op jit(solution)/shard_map/ppermute | solution.py:30
  20.4 4.5 %collective-permute-start.7 = (f32[64,256]{1,0:T(8,128)S(1)}, f32[64,256]{1,0:T(8,128)S(1)}, u32[]{:S(2)}, u32[]{:S(2)}) collective-permute-start(f32[64,256]{1,0:T(8,128)S(1)} %get-tuple-element.25), channel_id=1, source_target_pairs={{0,2},{1,3},{2,0},{3,1},{4,6},{5,7},{6,4},{7,5},{8,10},{9,11},{10,... | collective-permute-start | bytes 196616 | tf_op jit(solution)/shard_map/ppermute | solution.py:30
  22.0 4.0 %collective-permute-start.8 = (f32[64,256]{1,0:T(8,128)S(1)}, f32[64,256]{1,0:T(8,128)S(1)}, u32[]{:S(2)}, u32[]{:S(2)}) collective-permute-start(f32[64,256]{1,0:T(8,128)S(1)} %get-tuple-element.26), channel_id=1, source_target_pairs={{0,3},{1,2},{2,1},{3,0},{4,7},{5,6},{6,5},{7,4},{8,11},{9,10},{10,... | collective-permute-start | bytes 196616 | tf_op jit(solution)/shard_map/ppermute | solution.py:30
  26.2 7.7 %collective-permute-start.11 = (f32[48,128]{1,0:T(8,128)S(1)}, f32[48,128]{1,0:T(8,128)S(1)}, u32[]{:S(2)}, u32[]{:S(2)}) collective-permute-start(f32[48,128]{1,0:T(8,128)S(1)} %get-tuple-element.30), channel_id=1, source_target_pairs={{0,12},{4,8},{8,4},{12,0},{1,13},{5,9},{9,5},{13,1},{2,14},{6,10},... | collective-permute-start | bytes 73736 | tf_op jit(solution)/shard_map/ppermute | solution.py:30
  28.8 5.2 %collective-permute-start.10 = (f32[40,128]{1,0:T(8,128)S(1)}, f32[40,128]{1,0:T(8,128)S(1)}, u32[]{:S(2)}, u32[]{:S(2)}) collective-permute-start(f32[40,128]{1,0:T(8,128)S(1)} %get-tuple-element.29), channel_id=1, source_target_pairs={{0,8},{4,12},{8,0},{12,4},{1,9},{5,13},{9,1},{13,5},{2,10},{6,14},... | collective-permute-start | bytes 61448 | tf_op jit(solution)/shard_map/ppermute | solution.py:30
  30.2 3.7 %collective-permute-start.9 = (f32[32,128]{1,0:T(8,128)S(1)}, f32[32,128]{1,0:T(8,128)S(1)}, u32[]{:S(2)}, u32[]{:S(2)}) collective-permute-start(f32[32,128]{1,0:T(8,128)S(1)} %get-tuple-element.28), channel_id=1, source_target_pairs={{0,4},{4,0},{8,12},{12,8},{1,5},{5,1},{9,13},{13,9},{2,6},{6,2},{1... | collective-permute-start | bytes 49160 | tf_op jit(solution)/shard_map/ppermute | solution.py:30

commit v8 on v7

--- a/solution.py
+++ b/solution.py
@@ -86,20 +86,24 @@
         for d in range(2):
             for j in range(share):
                 p = ((r ^ 2) * 2 + (s ^ d)) * share + j + i * length
-                at = (d * share + j) * size + i * part_size
+                at = ((1 - d) * share + j) * size + i * part_size
                 raw[at:at + part_size, :] = own[pl.ds(p, part_size, stride=aux_local), :]
 
 
 def extend_kernel(raw, other_ref, density_ref, out):
     r, s = lax.axis_index("row"), lax.axis_index("sub")
-    at = raw.shape[0]
-    out[:at, :] = raw[...]
-    folded = fold(column_block(density_ref[...], r))
-    rows = folded.shape[0] // 2
-    out[at:at + rows, :] = jnp.where(s == 0, folded[:rows], folded[rows:])
+    at, rows = raw.shape[0] // 2, density_ref.shape[0] // 2
+    out[:at, :] = raw[:at, :]
+    some = pl.ds(pl.multiple_of(s * rows, rows), rows)
+    out[at:at + rows, :] = half_of(density_ref[some, :], r // 2)
     direct, turned = lanes(other_ref, 8)
     even = lax.broadcasted_iota(jnp.int32, (8, 128), 0) % 2 == 0
-    out[at + rows:, :] = jnp.where(even, direct, turned).astype(F32)
+    out[at + rows:at + rows + 8, :] = jnp.where(even, direct, turned).astype(F32)
+    out[at + rows + 8:, :] = raw[at:, :]
+
+
+def pass_kernel(two, out):
+    out[...] = two[:out.shape[0], :]
 
 
 def far_kernel(share, screen_ref, other_ref, own_ref, par_ref, density_ref, *outs):
@@ -121,7 +125,7 @@
     density = density_ref[...]
     for h in range(cut):
         outs[1][at + h * size:at + (h + 1) * size, :] = density[:, h * 128:(h + 1) * 128]
-    outs[2][at:, :] = half_of(density, r // 2)
+    outs[2][at:, :] = fold(column_block(density, r))
 
 
 def fock_kernel(share, own, one, two, two_other, three, density, *refs):
@@ -146,18 +150,18 @@
     keep(1, *beside)
     a, b = [jnp.where(h == 0, x[1], x[0]) for x in (mine, beside)]
     across = jnp.transpose(jnp.concatenate([jnp.where(odd, b, a), jnp.where(odd, a, b)], axis=0))
-    here = three[at:at + size, :]
+    middle = share * size
+    came = [ref[middle:middle + size // 2, :] for ref in (two, two_other)]
+    here = jnp.where(s == 0, jnp.concatenate(came, axis=0), jnp.concatenate(came[::-1], axis=0))
     mirror = jnp.transpose(jnp.concatenate([here, here], axis=0))
-    mirror = jnp.where(odd, mirror[size:], mirror[:size])
-    at = 2 * share * size
-    a, b = [ref[at:at + size // 4, :] for ref in (two, two_other)]
-    corner = unfold(jnp.concatenate([jnp.where(s == 0, a, b), jnp.where(s == 0, b, a)], axis=0))
-    corner = jnp.where(odd, pltpu.roll(corner, 64, 1), corner)
+    mirror = jnp.where(odd, mirror[:size], mirror[size:])
+    corner = unfold(three[at:, :])
+    corner = jnp.where(odd, corner, pltpu.roll(corner, 64, 1))
     low = lax.broadcasted_iota(jnp.int32, (size, 128), 1) < 64
-    last = jnp.where(low ^ odd, corner, mirror)
+    last = jnp.where(low ^ odd, mirror, corner)
     for k, inner, outer in (
-        (2, last, jnp.where(odd, across[size:], across[:size])),
-        (3, here, jnp.where(odd, across[:size], across[size:])),
+        (2, here, jnp.where(odd, across[size:], across[:size])),
+        (3, last, jnp.where(odd, across[:size], across[size:])),
     ):
         keep(k, jnp.where(h == 0, outer, inner), jnp.where(h == 0, inner, outer))
     for k, chunk in ((0, own), (1, one), (3, three)):
@@ -167,14 +171,14 @@
                 high, lower = split(chunk[at:at + size, :])
                 bh[j, rows_of(k), x * 128:(x + 1) * 128] = high
                 bl[j, rows_of(k), x * 128:(x + 1) * 128] = lower
-    at = 2 * share * size + size // 4
+    at = middle + size // 2
     spots = [
         [jnp.broadcast_to(ref[at + i:at + i + 1, :], (size, 128)) for i in range(2)] for ref in (two_other, two)
     ]
     for j in range(share):
         values = [jnp.zeros((size, 128), F32)] * cut
         for d, ref in enumerate((two, two_other)):
-            x = (d * share + j) * size
+            x = j * size + (0 if d else at + 8)
             values = spread(spots[d], ref[x:x + size, :], values)
         for x, value in enumerate(values):
             high, lower = split(value)
@@ -226,12 +230,13 @@
         scratch=[pltpu.SemaphoreType.DMA((2,))],
         limit=FIRST,
     )(flat)
-    extended = (raw.shape[0] + block_size // 4 + 8, 128)
+    extended = (raw.shape[0] + block_size // 2 + 8, 128)
+    passed = (extended[0] - share * block_size, 128)
     other_screen = core(screen)
     two = row(call(extend_kernel, [extended], count=3)(raw, other_screen, density)[0], 2)
     own, one, three = call(
         functools.partial(far_kernel, share),
-        [(packed + more, 128) for more in (0, orbitals // 2, block_size)],
+        [(packed + more, 128) for more in (0, orbitals // 2, block_size // 2)],
         count=5,
     )(screen, other_screen, mine, other, density)
     three, one = row(three, 3), row(one, 1)
@@ -246,7 +251,7 @@
             pltpu.VMEM((orbitals, orbitals), F32),
         ],
         count=6,
-    )(own, one, two, core(two), three, density)
+    )(own, one, two, core(call(pass_kernel, [passed], count=1)(two)[0]), three, density)
     sums = [parts[0]] + [swap(parts[k], ("aux", "sub"), 4, k) for k in (1, 2, 3)]
     cuts = call(cut_kernel, [(block_size // 2 + more, 2 * block_size) for more in (0, 0, 8, 16)], count=4)(*sums)
     moved = [row(cuts[k], k) for k in (1, 2, 3)]

time: 34.9 us -> 34.4 us (0.986)
  waiting for transfers between devices: 18.3 us -> 17.9 us
    ppermute x12, waiting for transfers between devices: 18.3 us -> 17.9 us  [swap(): return lax.ppermute(x, axes, [(a, a ^ k) for a in range(size)])]
where the time goes in v8:
time: 34.4 us; the launch traced here: 34.2 us
  waiting for transfers between devices  17.9 us (52%)
  starting transfers between devices  12.8 us (37%)
  Pallas kernels  3.27 us (10%)
    ppermute x12, waiting for transfers between devices, swap(): return lax.ppermute(x, axes, [(a, a ^ k) for a in range(size)])  17.9 us
    ppermute x12, starting transfers between devices, swap(): return lax.ppermute(x, axes, [(a, a ^ k) for a in range(size)])  12.8 us
    pallas_call x1, Pallas kernels, dealt_body(): call(functools.partial(near_kernel, share, block_size), [(2 * share * blo...  1.07 us
    pallas_call x1, Pallas kernels, dealt_body(): call(functools.partial(fock_kernel, share), [(block_size, orbitals)] * 4,...  0.95 us
    pallas_call x1, Pallas kernels, dealt_body(): call(final_kernel, [(block_size, block_size)], count=4)(cuts[0], *moved)[0]  0.76 us
  transfers between devices with their start and end apart: 12, of which 6 were waited for; matrix products, arithmetic and copies ran while one was open for 0% of the time, Pallas kernels for 4%

profile of v8, /device:TPU:0, one launch (start us, length us, event | category | flops | bytes accessed | tf_op | source)
XLA Modules:
  0.0 34.2 jit_solution(17859784326750876334)
XLA Ops:
  0.0 0.5 %collective-permute-start.1 = (f32[1024,128]{1,0:T(8,128)}, f32[1024,128]{1,0:T(8,128)S(1)}, u32[]{:S(2)}, u32[]{:S(2)}) collective-permute-start(f32[1024,128]{1,0:T(8,128)} %bitcast.1), channel_id=1, source_target_pairs={{0,1},{1,0},{2,3},{3,2},{4,5},{5,4},{6,7},{7,6},{8,9},{9,8},{10,11... | collective-permute-start | bytes 1572872 | tf_op jit(solution)/shard_map/ppermute | solution.py:30
  0.5 0.2 copy-done.1
  0.7 0.5 %collective-permute-start = (s32[1,2]{1,0:T(1,128)S(1)}, s32[1,2]{1,0:T(1,128)S(1)}, u32[]{:S(2)}, u32[]{:S(2)}) collective-permute-start(s32[1,2]{1,0:T(1,128)S(1)} %copy-done.1), channel_id=1, source_target_pairs={{0,1},{1,0},{2,3},{3,2},{4,5},{5,4},{6,7},{7,6},{8,9},{9,8},{10,11... | collective-permute-start | bytes 32 | tf_op jit(solution)/shard_map/ppermute | solution.py:30
  1.1 1.1 %shard_map.37 = (f32[256,128]{1,0:T(8,128)S(1)}, f32[1024,128]{1,0:T(8,128)S(1)}) custom-call(f32[1024,128]{1,0:T(8,128)} %bitcast.2), custom_call_target="tpu_custom_call" | custom-call | tf_op jit(solution)/shard_map/pallas_call | solution.py:226
  2.2 0.1 shard_map.39
  2.3 3.8 %collective-permute-start.3 = (f32[296,128]{1,0:T(8,128)S(1)}, f32[296,128]{1,0:T(8,128)S(1)}, u32[]{:S(2)}, u32[]{:S(2)}) collective-permute-start(f32[296,128]{1,0:T(8,128)S(1)} %shard_map.39), channel_id=1, source_target_pairs={{0,8},{4,12},{8,0},{12,4},{1,9},{5,13},{9,1},{13,5},{2,10},{6,14},... | collective-permute-start | bytes 454664 | tf_op jit(solution)/shard_map/ppermute | solution.py:30
  6.0 0.2 shard_map.38
  6.3 1.6 %collective-permute-start.2 = (f32[384,128]{1,0:T(8,128)S(1)}, f32[384,128]{1,0:T(8,128)S(1)}, u32[]{:S(2)}, u32[]{:S(2)}) collective-permute-start(f32[384,128]{1,0:T(8,128)S(1)} %get-tuple-element.20), channel_id=1, source_target_pairs={{0,4},{4,0},{8,12},{12,8},{1,5},{5,1},{9,13},{13,9},{2,6},{6,2},{1... | collective-permute-start | bytes 589832 | tf_op jit(solution)/shard_map/ppermute | solution.py:30
  7.9 6.1 %collective-permute-done.3.two = f32[296,128]{1,0:T(8,128)S(1)} collective-permute-done((f32[296,128]{1,0:T(8,128)S(1)}, f32[296,128]{1,0:T(8,128)S(1)}, u32[]{:S(2)}, u32[]{:S(2)}) %collective-permute-start.3) | collective-permute-done | bytes 151584 | tf_op jit(solution)/shard_map/ppermute | solution.py:30
  14.1 0.1 collective-permute-start.4
  14.2 1.3 %collective-permute-done.4.two_other = f32[168,128]{1,0:T(8,128)S(1)} collective-permute-done((f32[168,128]{1,0:T(8,128)S(1)}, f32[168,128]{1,0:T(8,128)S(1)}, u32[]{:S(2)}, u32[]{:S(2)}) %collective-permute-start.4) | collective-permute-done | bytes 86048 | tf_op jit(solution)/shard_map/ppermute | solution.py:30
  15.4 3.6 %collective-permute-done.5.three = f32[288,128]{1,0:T(8,128)S(1)} collective-permute-done((f32[288,128]{1,0:T(8,128)S(1)}, f32[288,128]{1,0:T(8,128)S(1)}, u32[]{:S(2)}, u32[]{:S(2)}) %collective-permute-start.5) | collective-permute-done | bytes 147488 | tf_op jit(solution)/shard_map/ppermute | solution.py:30
  19.1 0.9 %shard_map.41 = (f32[64,256]{1,0:T(8,128)S(1)}, f32[64,256]{1,0:T(8,128)S(1)}, f32[64,256]{1,0:T(8,128)S(1)}, f32[64,256]{1,0:T(8,128)S(1)}) custom-call(f32[256,128]{1,0:T(8,128)S(1)} %get-tuple-element.19.own, f32[384,128]{1,0:T(8,128)S(1)} %collective-permute-done.2.one, f32[296,128]{1,0:T(8,128)S(1)} %collective-permute-done.3.two, ...), custom_call_target="tpu_custom_call" | custom-call | tf_op jit(solution)/shard_map/pallas_call | solution.py:243
  20.0 0.1 collective-permute-start.6
  20.1 1.6 %collective-permute-start.7 = (f32[64,256]{1,0:T(8,128)S(1)}, f32[64,256]{1,0:T(8,128)S(1)}, u32[]{:S(2)}, u32[]{:S(2)}) collective-permute-start(f32[64,256]{1,0:T(8,128)S(1)} %get-tuple-element.25), channel_id=1, source_target_pairs={{0,2},{1,3},{2,0},{3,1},{4,6},{5,7},{6,4},{7,5},{8,10},{9,11},{10,... | collective-permute-start | bytes 196616 | tf_op jit(solution)/shard_map/ppermute | solution.py:30
  21.7 0.3 collective-permute-start.8
  22.0 2.6 %collective-permute-done.7.refs_2_ = f32[64,256]{1,0:T(8,128)S(1)} collective-permute-done((f32[64,256]{1,0:T(8,128)S(1)}, f32[64,256]{1,0:T(8,128)S(1)}, u32[]{:S(2)}, u32[]{:S(2)}) %collective-permute-start.7) | collective-permute-done | bytes 65568 | tf_op jit(solution)/shard_map/ppermute | solution.py:30
  24.6 1.1 %collective-permute-done.8.refs_3_ = f32[64,256]{1,0:T(8,128)S(1)} collective-permute-done((f32[64,256]{1,0:T(8,128)S(1)}, f32[64,256]{1,0:T(8,128)S(1)}, u32[]{:S(2)}, u32[]{:S(2)}) %collective-permute-start.8) | collective-permute-done | bytes 65568 | tf_op jit(solution)/shard_map/ppermute | solution.py:30
  25.7 0.2 shard_map.42
  25.9 2.5 %collective-permute-start.11 = (f32[48,128]{1,0:T(8,128)S(1)}, f32[48,128]{1,0:T(8,128)S(1)}, u32[]{:S(2)}, u32[]{:S(2)}) collective-permute-start(f32[48,128]{1,0:T(8,128)S(1)} %get-tuple-element.30), channel_id=1, source_target_pairs={{0,12},{4,8},{8,4},{12,0},{1,13},{5,9},{9,5},{13,1},{2,14},{6,10},... | collective-permute-start | bytes 73736 | tf_op jit(solution)/shard_map/ppermute | solution.py:30
  28.4 1.3 %collective-permute-start.10 = (f32[40,128]{1,0:T(8,128)S(1)}, f32[40,128]{1,0:T(8,128)S(1)}, u32[]{:S(2)}, u32[]{:S(2)}) collective-permute-start(f32[40,128]{1,0:T(8,128)S(1)} %get-tuple-element.29), channel_id=1, source_target_pairs={{0,8},{4,12},{8,0},{12,4},{1,9},{5,13},{9,1},{13,5},{2,10},{6,14},... | collective-permute-start | bytes 61448 | tf_op jit(solution)/shard_map/ppermute | solution.py:30
  29.7 0.6 %collective-permute-start.9 = (f32[32,128]{1,0:T(8,128)S(1)}, f32[32,128]{1,0:T(8,128)S(1)}, u32[]{:S(2)}, u32[]{:S(2)}) collective-permute-start(f32[32,128]{1,0:T(8,128)S(1)} %get-tuple-element.28), channel_id=1, source_target_pairs={{0,4},{4,0},{8,12},{12,8},{1,5},{5,1},{9,13},{13,9},{2,6},{6,2},{1... | collective-permute-start | bytes 49160 | tf_op jit(solution)/shard_map/ppermute | solution.py:30
  30.4 3.1 %collective-permute-done.9.one = f32[32,128]{1,0:T(8,128)S(1)} collective-permute-done((f32[32,128]{1,0:T(8,128)S(1)}, f32[32,128]{1,0:T(8,128)S(1)}, u32[]{:S(2)}, u32[]{:S(2)}) %collective-permute-start.9) | collective-permute-done | bytes 16416 | tf_op jit(solution)/shard_map/ppermute | solution.py:30
  33.5 0.8 %shard_map.43 = f32[64,64]{1,0:T(8,128)} custom-call(f32[32,128]{1,0:T(8,128)S(1)} %get-tuple-element.27.kept, f32[32,128]{1,0:T(8,128)S(1)} %collective-permute-done.9.one, f32[40,128]{1,0:T(8,128)S(1)} %collective-permute-done.10.two, f32[48,128]{1,0:T(8,128)S(1)} %collective-permute-done.11.three), custom_call_target="tpu_custom_call" | custom-call | tf_op jit(solution)/shard_map/pallas_call | solution.py:258
  (11 shorter events, 0.0 us)
Async XLA Ops:
  0.0 0.7 %copy-start.1 = (s32[1,2]{1,0:T(1,128)S(1)}, s32[1,2]{1,0:T(1,128)}, u32[]{:S(2)}) copy-start(s32[1,2]{1,0:T(1,128)} %screen_ref.1) | copy-start | bytes 28
  0.0 2.2 %copy-start = (f32[64,256]{1,0:T(8,128)S(1)}, f32[64,256]{1,0:T(8,128)}, u32[]{:S(2)}) copy-start(f32[64,256]{1,0:T(8,128)} %density.1) | copy-start | bytes 196612
  0.0 6.0 %collective-permute-start.1 = (f32[1024,128]{1,0:T(8,128)}, f32[1024,128]{1,0:T(8,128)S(1)}, u32[]{:S(2)}, u32[]{:S(2)}) collective-permute-start(f32[1024,128]{1,0:T(8,128)} %bitcast.1), channel_id=1, source_target_pairs={{0,1},{1,0},{2,3},{3,2},{4,5},{5,4},{6,7},{7,6},{8,9},{9,8},{10,11... | collective-permute-start | bytes 1572872 | tf_op jit(solution)/shard_map/ppermute | solution.py:30
  0.7 1.5 %collective-permute-start = (s32[1,2]{1,0:T(1,128)S(1)}, s32[1,2]{1,0:T(1,128)S(1)}, u32[]{:S(2)}, u32[]{:S(2)}) collective-permute-start(s32[1,2]{1,0:T(1,128)S(1)} %copy-done.1), channel_id=1, source_target_pairs={{0,1},{1,0},{2,3},{3,2},{4,5},{5,4},{6,7},{7,6},{8,9},{9,8},{10,11... | collective-permute-start | bytes 32 | tf_op jit(solution)/shard_map/ppermute | solution.py:30
  2.3 11.8 %collective-permute-start.3 = (f32[296,128]{1,0:T(8,128)S(1)}, f32[296,128]{1,0:T(8,128)S(1)}, u32[]{:S(2)}, u32[]{:S(2)}) collective-permute-start(f32[296,128]{1,0:T(8,128)S(1)} %shard_map.39), channel_id=1, source_target_pairs={{0,8},{4,12},{8,0},{12,4},{1,9},{5,13},{9,1},{13,5},{2,10},{6,14},... | collective-permute-start | bytes 454664 | tf_op jit(solution)/shard_map/ppermute | solution.py:30
  6.3 12.8 %collective-permute-start.2 = (f32[384,128]{1,0:T(8,128)S(1)}, f32[384,128]{1,0:T(8,128)S(1)}, u32[]{:S(2)}, u32[]{:S(2)}) collective-permute-start(f32[384,128]{1,0:T(8,128)S(1)} %get-tuple-element.20), channel_id=1, source_target_pairs={{0,4},{4,0},{8,12},{12,8},{1,5},{5,1},{9,13},{13,9},{2,6},{6,2},{1... | collective-permute-start | bytes 589832 | tf_op jit(solution)/shard_map/ppermute | solution.py:30
  7.9 11.1 %collective-permute-start.5 = (f32[288,128]{1,0:T(8,128)S(1)}, f32[288,128]{1,0:T(8,128)S(1)}, u32[]{:S(2)}, u32[]{:S(2)}) collective-permute-start(f32[288,128]{1,0:T(8,128)S(1)} %get-tuple-element.22), channel_id=1, source_target_pairs={{0,12},{4,8},{8,4},{12,0},{1,13},{5,9},{9,5},{13,1},{2,14},{6,10},... | collective-permute-start | bytes 442376 | tf_op jit(solution)/shard_map/ppermute | solution.py:30
  14.1 1.3 %collective-permute-start.4 = (f32[168,128]{1,0:T(8,128)S(1)}, f32[168,128]{1,0:T(8,128)S(1)}, u32[]{:S(2)}, u32[]{:S(2)}) collective-permute-start(f32[168,128]{1,0:T(8,128)S(1)} %shard_map.40), channel_id=1, source_target_pairs={{0,1},{1,0},{2,3},{3,2},{4,5},{5,4},{6,7},{7,6},{8,9},{9,8},{10,11... | collective-permute-start | bytes 258056 | tf_op jit(solution)/shard_map/ppermute | solution.py:30
  20.0 1.9 %collective-permute-start.6 = (f32[64,256]{1,0:T(8,128)S(1)}, f32[64,256]{1,0:T(8,128)S(1)}, u32[]{:S(2)}, u32[]{:S(2)}) collective-permute-start(f32[64,256]{1,0:T(8,128)S(1)} %get-tuple-element.24), channel_id=1, source_target_pairs={{0,1},{1,0},{2,3},{3,2},{4,5},{5,4},{6,7},{7,6},{8,9},{9,8},{10,11... | collective-permute-start | bytes 196616 | tf_op jit(solution)/shard_map/ppermute | solution.py:30
  20.1 4.5 %collective-permute-start.7 = (f32[64,256]{1,0:T(8,128)S(1)}, f32[64,256]{1,0:T(8,128)S(1)}, u32[]{:S(2)}, u32[]{:S(2)}) collective-permute-start(f32[64,256]{1,0:T(8,128)S(1)} %get-tuple-element.25), channel_id=1, source_target_pairs={{0,2},{1,3},{2,0},{3,1},{4,6},{5,7},{6,4},{7,5},{8,10},{9,11},{10,... | collective-permute-start | bytes 196616 | tf_op jit(solution)/shard_map/ppermute | solution.py:30
  21.7 4.0 %collective-permute-start.8 = (f32[64,256]{1,0:T(8,128)S(1)}, f32[64,256]{1,0:T(8,128)S(1)}, u32[]{:S(2)}, u32[]{:S(2)}) collective-permute-start(f32[64,256]{1,0:T(8,128)S(1)} %get-tuple-element.26), channel_id=1, source_target_pairs={{0,3},{1,2},{2,1},{3,0},{4,7},{5,6},{6,5},{7,4},{8,11},{9,10},{10,... | collective-permute-start | bytes 196616 | tf_op jit(solution)/shard_map/ppermute | solution.py:30
  25.9 7.6 %collective-permute-start.11 = (f32[48,128]{1,0:T(8,128)S(1)}, f32[48,128]{1,0:T(8,128)S(1)}, u32[]{:S(2)}, u32[]{:S(2)}) collective-permute-start(f32[48,128]{1,0:T(8,128)S(1)} %get-tuple-element.30), channel_id=1, source_target_pairs={{0,12},{4,8},{8,4},{12,0},{1,13},{5,9},{9,5},{13,1},{2,14},{6,10},... | collective-permute-start | bytes 73736 | tf_op jit(solution)/shard_map/ppermute | solution.py:30
  28.4 5.0 %collective-permute-start.10 = (f32[40,128]{1,0:T(8,128)S(1)}, f32[40,128]{1,0:T(8,128)S(1)}, u32[]{:S(2)}, u32[]{:S(2)}) collective-permute-start(f32[40,128]{1,0:T(8,128)S(1)} %get-tuple-element.29), channel_id=1, source_target_pairs={{0,8},{4,12},{8,0},{12,4},{1,9},{5,13},{9,1},{13,5},{2,10},{6,14},... | collective-permute-start | bytes 61448 | tf_op jit(solution)/shard_map/ppermute | solution.py:30
  29.7 3.8 %collective-permute-start.9 = (f32[32,128]{1,0:T(8,128)S(1)}, f32[32,128]{1,0:T(8,128)S(1)}, u32[]{:S(2)}, u32[]{:S(2)}) collective-permute-start(f32[32,128]{1,0:T(8,128)S(1)} %get-tuple-element.28), channel_id=1, source_target_pairs={{0,4},{4,0},{8,12},{12,8},{1,5},{5,1},{9,13},{13,9},{2,6},{6,2},{1... | collective-permute-start | bytes 49160 | tf_op jit(solution)/shard_map/ppermute | solution.py:30

commit v9 on v8

--- a/solution.py
+++ b/solution.py
@@ -15,12 +15,12 @@
 BF16 = jnp.bfloat16
 
 
-def call(kernel, outs, scratch=(), ins=None, count=0, limit=12 << 20):
+def call(kernel, outs, scratch=(), ins=None, count=0, limit=12 << 20, halved=()):
     return pl.pallas_call(
         kernel,
-        out_shape=tuple(jax.ShapeDtypeStruct(s, F32) for s in outs),
+        out_shape=tuple(jax.ShapeDtypeStruct(s, t) for x, t in ((outs, F32), (halved, BF16)) for s in x),
         in_specs=ins if ins is not None else [VMEM] * count,
-        out_specs=tuple(VMEM for _ in outs),
+        out_specs=(VMEM,) * (len(outs) + len(halved)),
         scratch_shapes=list(scratch),
         compiler_params=pltpu.CompilerParams(vmem_limit_bytes=limit),
     )
@@ -128,22 +128,30 @@
     outs[2][at:, :] = fold(column_block(density, r))
 
 
-def fock_kernel(share, own, one, two, two_other, three, density, *refs):
-    outs, (dh, dl, bh, bl, total) = refs[:4], refs[4:]
+def keep_parts(refs, j, at, values):
+    for x, value in enumerate(values):
+        for ref, part in zip(refs, split(value)):
+            ref[j, at:at + value.shape[0], x * 128:(x + 1) * 128] = part
+
+
+def chunk_parts(chunk, j, size, cut):
+    return [chunk[(j * cut + x) * size:(j * cut + x + 1) * size, :] for x in range(cut)]
+
+
+def early_kernel(own, one, two, two_other, density, eh, el, dh, dl):
     r, s = lax.axis_index("row"), lax.axis_index("sub")
-    q = lax.axis_index("aux") * 2 + s
     size, orbitals = density.shape
-    cut = orbitals // 128
+    share, cut = eh.shape[0], orbitals // 128
     h, odd = r // 2, r % 2 == 1
-    rows_of = lambda k: pl.ds(pl.multiple_of((r ^ k) * size, size), size)
-    at = share * cut * size
 
     def keep(k, left, right):
+        rows = pl.ds(pl.multiple_of((r ^ k) * size, size), size)
         for x, value in enumerate((left, right)):
             high, lower = split(value)
-            dh[rows_of(k), x * 128:(x + 1) * 128] = high
-            dl[rows_of(k), x * 128:(x + 1) * 128] = lower
-
+            dh[rows, x * 128:(x + 1) * 128] = high
+            dl[rows, x * 128:(x + 1) * 128] = lower
+
+    at = share * cut * size
     mine = [density[:, x * 128:(x + 1) * 128] for x in range(2)]
     beside = [one[at + x * size:at + (x + 1) * size, :] for x in range(2)]
     keep(0, *mine)
@@ -155,22 +163,11 @@
     here = jnp.where(s == 0, jnp.concatenate(came, axis=0), jnp.concatenate(came[::-1], axis=0))
     mirror = jnp.transpose(jnp.concatenate([here, here], axis=0))
     mirror = jnp.where(odd, mirror[:size], mirror[size:])
-    corner = unfold(three[at:, :])
-    corner = jnp.where(odd, corner, pltpu.roll(corner, 64, 1))
-    low = lax.broadcasted_iota(jnp.int32, (size, 128), 1) < 64
-    last = jnp.where(low ^ odd, mirror, corner)
     for k, inner, outer in (
         (2, here, jnp.where(odd, across[size:], across[:size])),
-        (3, last, jnp.where(odd, across[:size], across[size:])),
+        (3, mirror, jnp.where(odd, across[:size], across[size:])),
     ):
         keep(k, jnp.where(h == 0, outer, inner), jnp.where(h == 0, inner, outer))
-    for k, chunk in ((0, own), (1, one), (3, three)):
-        for j in range(share):
-            for x in range(cut):
-                at = (j * cut + x) * size
-                high, lower = split(chunk[at:at + size, :])
-                bh[j, rows_of(k), x * 128:(x + 1) * 128] = high
-                bl[j, rows_of(k), x * 128:(x + 1) * 128] = lower
     at = middle + size // 2
     spots = [
         [jnp.broadcast_to(ref[at + i:at + i + 1, :], (size, 128)) for i in range(2)] for ref in (two_other, two)
@@ -180,32 +177,50 @@
         for d, ref in enumerate((two, two_other)):
             x = j * size + (0 if d else at + 8)
             values = spread(spots[d], ref[x:x + size, :], values)
-        for x, value in enumerate(values):
-            high, lower = split(value)
-            bh[j, rows_of(2), x * 128:(x + 1) * 128] = high
-            bl[j, rows_of(2), x * 128:(x + 1) * 128] = lower
+        for i, parts in enumerate((chunk_parts(own, j, size, cut), values, chunk_parts(one, j, size, cut))):
+            keep_parts((eh, el), j, i * size, parts)
+
+
+def fock_kernel(eh, el, fh, fl, three, *refs):
+    outs, (dh, dl, lh, ll, total) = refs[:4], refs[4:]
+    r = lax.axis_index("row")
+    q = lax.axis_index("aux") * 2 + lax.axis_index("sub")
+    share, orbitals = eh.shape[0], fh.shape[0]
+    size, cut = orbitals - eh.shape[1], orbitals // 128
+    h, odd = r // 2, r % 2 == 1
+    corner = unfold(three[share * cut * size:, :])
+    low = lax.broadcasted_iota(jnp.int32, (size, 128), 1) < 64
+    corner = split(jnp.where(low, corner, pltpu.roll(corner, 64, 1)))
+    rows = pl.ds(pl.multiple_of((r ^ 3) * size, size), size)
+    for old, new, part in zip((fh, fl), (dh, dl), corner):
+        new[...] = old[...]
+        for x in range(cut):
+            columns = slice(x * 128, (x + 1) * 128)
+            other = jnp.logical_or(low ^ odd, h == x)
+            new[rows, columns] = jnp.where(other, old[rows, columns].astype(F32), part.astype(F32)).astype(BF16)
     side = lambda *parts: jnp.concatenate(parts, axis=1)
     whole = jnp.concatenate([dh[...], dl[...], dh[...]], axis=0)
     lefts, rights = [], []
     for j in range(share):
-        b1, b2 = bh[j], bl[j]
+        keep_parts((lh, ll), j, 0, chunk_parts(three, j, size, cut))
+        b1, b2 = [jnp.concatenate([x[j], y[j]], axis=0) for x, y in ((eh, lh), (el, ll))]
         c1, c2 = split(jnp.dot(side(b1, b1, b2), whole, preferred_element_type=F32))
         lefts += [c1, c1, c2]
         rights += [b1, b2, b1]
-    result = lax.dot_general(
+    total[...] = lax.dot_general(
         side(*lefts), side(*rights), (((1,), (1,)), ((), ())), preferred_element_type=F32
     )
-    total[...] = result
     for dq in range(4):
-        outs[dq][...] = total[pl.ds(pl.multiple_of((q ^ dq) * size, size), size), :]
+        k = q ^ dq ^ r
+        start = pl.multiple_of((k % 2 * 2 + k // 2) * size, size)
+        outs[dq][...] = total[pl.ds(start, size), :]
 
 
 def cut_kernel(*refs):
     ins, outs = refs[:4], refs[4:]
-    r = lax.axis_index("row")
     value = ins[0][...] + ins[1][...] + (ins[2][...] + ins[3][...])
     for k in range(4):
-        outs[k][:value.shape[0] // 2, :] = fold(column_block(value, r ^ k))
+        outs[k][:value.shape[0] // 2, :] = fold(column_block(value, k % 2 * 2 + k // 2))
 
 
 def final_kernel(kept, one, two, three, out):
@@ -240,18 +255,23 @@
         count=5,
     )(screen, other_screen, mine, other, density)
     three, one = row(three, 3), row(one, 1)
+    two_other = core(call(pass_kernel, [passed], count=1)(two)[0])
+    whole = (orbitals, orbitals)
+    early = call(
+        early_kernel, [], count=5, halved=((share, orbitals - block_size, orbitals),) * 2 + (whole,) * 2
+    )(own, one, two, two_other, density)
     parts = call(
-        functools.partial(fock_kernel, share),
+        fock_kernel,
         [(block_size, orbitals)] * 4,
         scratch=[
-            pltpu.VMEM((orbitals, orbitals), BF16),
-            pltpu.VMEM((orbitals, orbitals), BF16),
-            pltpu.VMEM((share, orbitals, orbitals), BF16),
-            pltpu.VMEM((share, orbitals, orbitals), BF16),
-            pltpu.VMEM((orbitals, orbitals), F32),
+            pltpu.VMEM(whole, BF16),
+            pltpu.VMEM(whole, BF16),
+            pltpu.VMEM((share, block_size, orbitals), BF16),
+            pltpu.VMEM((share, block_size, orbitals), BF16),
+            pltpu.VMEM(whole, F32),
         ],
-        count=6,
-    )(own, one, two, core(call(pass_kernel, [passed], count=1)(two)[0]), three, density)
+        count=5,
+    )(*early, three)
     sums = [parts[0]] + [swap(parts[k], ("aux", "sub"), 4, k) for k in (1, 2, 3)]
     cuts = call(cut_kernel, [(block_size // 2 + more, 2 * block_size) for more in (0, 0, 8, 16)], count=4)(*sums)
     moved = [row(cuts[k], k) for k in (1, 2, 3)]

time: 34.4 us -> 34.3 us (level)
    pallas_call x2 -> x3, Pallas kernels: 0.96 us -> 1.16 us  [the longest x1 0.94 us: dealt_body(): call(fock_kernel, [(block_size, orbitals)] * 4, scratch=[pltpu.VMEM(whole...]
  transfers between devices with their start and end apart: 12 -> 12, of which waited for: 6 -> 6; matrix products, arithmetic and copies ran while one was open for 0% -> 0% of each run, Pallas kernels for 4% -> 5%
where the time goes in v9:
time: 34.3 us; the launch traced here: 34.2 us
  waiting for transfers between devices  17.7 us (52%)
  starting transfers between devices  12.7 us (37%)
  Pallas kernels  3.45 us (10%)
    ppermute x12, waiting for transfers between devices, swap(): return lax.ppermute(x, axes, [(a, a ^ k) for a in range(size)])  17.7 us
    ppermute x12, starting transfers between devices, swap(): return lax.ppermute(x, axes, [(a, a ^ k) for a in range(size)])  12.7 us
    pallas_call x1, Pallas kernels, dealt_body(): call(functools.partial(near_kernel, share, block_size), [(2 * share * blo...  1.07 us
    pallas_call x1, Pallas kernels, dealt_body(): call(fock_kernel, [(block_size, orbitals)] * 4, scratch=[pltpu.VMEM(whole...  0.94 us
    pallas_call x1, Pallas kernels, dealt_body(): call(final_kernel, [(block_size, block_size)], count=4)(cuts[0], *moved)[0]  0.76 us
  transfers between devices with their start and end apart: 12, of which 6 were waited for; matrix products, arithmetic and copies ran while one was open for 0% of the time, Pallas kernels for 5%

profile of v9, /device:TPU:0, one launch (start us, length us, event | category | flops | bytes accessed | tf_op | source)
XLA Modules:
  0.0 34.2 jit_solution(9562273728111166705)
XLA Ops:
  0.0 0.5 %collective-permute-start.1 = (f32[1024,128]{1,0:T(8,128)}, f32[1024,128]{1,0:T(8,128)S(1)}, u32[]{:S(2)}, u32[]{:S(2)}) collective-permute-start(f32[1024,128]{1,0:T(8,128)} %bitcast.1), channel_id=1, source_target_pairs={{0,1},{1,0},{2,3},{3,2},{4,5},{5,4},{6,7},{7,6},{8,9},{9,8},{10,11... | collective-permute-start | bytes 1572872 | tf_op jit(solution)/shard_map/ppermute | solution.py:30
  0.5 0.2 copy-done.1
  0.7 0.5 %collective-permute-start = (s32[1,2]{1,0:T(1,128)S(1)}, s32[1,2]{1,0:T(1,128)S(1)}, u32[]{:S(2)}, u32[]{:S(2)}) collective-permute-start(s32[1,2]{1,0:T(1,128)S(1)} %copy-done.1), channel_id=1, source_target_pairs={{0,1},{1,0},{2,3},{3,2},{4,5},{5,4},{6,7},{7,6},{8,9},{9,8},{10,11... | collective-permute-start | bytes 32 | tf_op jit(solution)/shard_map/ppermute | solution.py:30
  1.1 1.1 %shard_map.37 = (f32[256,128]{1,0:T(8,128)S(1)}, f32[1024,128]{1,0:T(8,128)S(1)}) custom-call(f32[1024,128]{1,0:T(8,128)} %bitcast.2), custom_call_target="tpu_custom_call" | custom-call | tf_op jit(solution)/shard_map/pallas_call | solution.py:241
  2.2 0.1 shard_map.39
  2.3 3.8 %collective-permute-start.3 = (f32[296,128]{1,0:T(8,128)S(1)}, f32[296,128]{1,0:T(8,128)S(1)}, u32[]{:S(2)}, u32[]{:S(2)}) collective-permute-start(f32[296,128]{1,0:T(8,128)S(1)} %shard_map.39), channel_id=1, source_target_pairs={{0,8},{4,12},{8,0},{12,4},{1,9},{5,13},{9,1},{13,5},{2,10},{6,14},... | collective-permute-start | bytes 454664 | tf_op jit(solution)/shard_map/ppermute | solution.py:30
  6.0 0.2 shard_map.38
  6.3 1.6 %collective-permute-start.2 = (f32[384,128]{1,0:T(8,128)S(1)}, f32[384,128]{1,0:T(8,128)S(1)}, u32[]{:S(2)}, u32[]{:S(2)}) collective-permute-start(f32[384,128]{1,0:T(8,128)S(1)} %get-tuple-element.24), channel_id=1, source_target_pairs={{0,4},{4,0},{8,12},{12,8},{1,5},{5,1},{9,13},{13,9},{2,6},{6,2},{1... | collective-permute-start | bytes 589832 | tf_op jit(solution)/shard_map/ppermute | solution.py:30
  7.9 6.1 %collective-permute-done.3.two = f32[296,128]{1,0:T(8,128)S(1)} collective-permute-done((f32[296,128]{1,0:T(8,128)S(1)}, f32[296,128]{1,0:T(8,128)S(1)}, u32[]{:S(2)}, u32[]{:S(2)}) %collective-permute-start.3) | collective-permute-done | bytes 151584 | tf_op jit(solution)/shard_map/ppermute | solution.py:30
  14.2 1.3 %collective-permute-done.4.two_other = f32[168,128]{1,0:T(8,128)S(1)} collective-permute-done((f32[168,128]{1,0:T(8,128)S(1)}, f32[168,128]{1,0:T(8,128)S(1)}, u32[]{:S(2)}, u32[]{:S(2)}) %collective-permute-start.4) | collective-permute-done | bytes 86048 | tf_op jit(solution)/shard_map/ppermute | solution.py:30
  15.4 0.2 shard_map.41
  15.7 3.4 %collective-permute-done.5.three = f32[288,128]{1,0:T(8,128)S(1)} collective-permute-done((f32[288,128]{1,0:T(8,128)S(1)}, f32[288,128]{1,0:T(8,128)S(1)}, u32[]{:S(2)}, u32[]{:S(2)}) %collective-permute-start.5) | collective-permute-done | bytes 147488 | tf_op jit(solution)/shard_map/ppermute | solution.py:30
  19.1 0.9 %shard_map.42 = (f32[64,256]{1,0:T(8,128)S(1)}, f32[64,256]{1,0:T(8,128)S(1)}, f32[64,256]{1,0:T(8,128)S(1)}, f32[64,256]{1,0:T(8,128)S(1)}) custom-call(bf16[2,192,256]{2,1,0:T(8,128)(2,1)S(1)} %get-tuple-element.26.eh, bf16[2,192,256]{2,1,0:T(8,128)(2,1)S(1)} %get-tuple-element.27.el, bf16[256,256]{1,0:T(8,128)(2,1)S(1)} %get-tuple-element.28.fh, ...), custom_call_target="tpu_custom_call" | custom-call | tf_op jit(solution)/shard_map/pallas_call | solution.py:263
  20.0 0.1 collective-permute-start.6
  20.1 1.6 %collective-permute-start.7 = (f32[64,256]{1,0:T(8,128)S(1)}, f32[64,256]{1,0:T(8,128)S(1)}, u32[]{:S(2)}, u32[]{:S(2)}) collective-permute-start(f32[64,256]{1,0:T(8,128)S(1)} %get-tuple-element.33), channel_id=1, source_target_pairs={{0,2},{1,3},{2,0},{3,1},{4,6},{5,7},{6,4},{7,5},{8,10},{9,11},{10,... | collective-permute-start | bytes 196616 | tf_op jit(solution)/shard_map/ppermute | solution.py:30
  21.7 0.3 collective-permute-start.8
  22.0 2.6 %collective-permute-done.7.refs_2_ = f32[64,256]{1,0:T(8,128)S(1)} collective-permute-done((f32[64,256]{1,0:T(8,128)S(1)}, f32[64,256]{1,0:T(8,128)S(1)}, u32[]{:S(2)}, u32[]{:S(2)}) %collective-permute-start.7) | collective-permute-done | bytes 65568 | tf_op jit(solution)/shard_map/ppermute | solution.py:30
  24.6 1.1 %collective-permute-done.8.refs_3_ = f32[64,256]{1,0:T(8,128)S(1)} collective-permute-done((f32[64,256]{1,0:T(8,128)S(1)}, f32[64,256]{1,0:T(8,128)S(1)}, u32[]{:S(2)}, u32[]{:S(2)}) %collective-permute-start.8) | collective-permute-done | bytes 65568 | tf_op jit(solution)/shard_map/ppermute | solution.py:30
  25.7 0.1 shard_map.43
  25.9 2.5 %collective-permute-start.11 = (f32[48,128]{1,0:T(8,128)S(1)}, f32[48,128]{1,0:T(8,128)S(1)}, u32[]{:S(2)}, u32[]{:S(2)}) collective-permute-start(f32[48,128]{1,0:T(8,128)S(1)} %get-tuple-element.38), channel_id=1, source_target_pairs={{0,12},{4,8},{8,4},{12,0},{1,13},{5,9},{9,5},{13,1},{2,14},{6,10},... | collective-permute-start | bytes 73736 | tf_op jit(solution)/shard_map/ppermute | solution.py:30
  28.4 1.3 %collective-permute-start.10 = (f32[40,128]{1,0:T(8,128)S(1)}, f32[40,128]{1,0:T(8,128)S(1)}, u32[]{:S(2)}, u32[]{:S(2)}) collective-permute-start(f32[40,128]{1,0:T(8,128)S(1)} %get-tuple-element.37), channel_id=1, source_target_pairs={{0,8},{4,12},{8,0},{12,4},{1,9},{5,13},{9,1},{13,5},{2,10},{6,14},... | collective-permute-start | bytes 61448 | tf_op jit(solution)/shard_map/ppermute | solution.py:30
  29.6 0.6 %collective-permute-start.9 = (f32[32,128]{1,0:T(8,128)S(1)}, f32[32,128]{1,0:T(8,128)S(1)}, u32[]{:S(2)}, u32[]{:S(2)}) collective-permute-start(f32[32,128]{1,0:T(8,128)S(1)} %get-tuple-element.36), channel_id=1, source_target_pairs={{0,4},{4,0},{8,12},{12,8},{1,5},{5,1},{9,13},{13,9},{2,6},{6,2},{1... | collective-permute-start | bytes 49160 | tf_op jit(solution)/shard_map/ppermute | solution.py:30
  30.3 3.1 %collective-permute-done.9.one = f32[32,128]{1,0:T(8,128)S(1)} collective-permute-done((f32[32,128]{1,0:T(8,128)S(1)}, f32[32,128]{1,0:T(8,128)S(1)}, u32[]{:S(2)}, u32[]{:S(2)}) %collective-permute-start.9) | collective-permute-done | bytes 16416 | tf_op jit(solution)/shard_map/ppermute | solution.py:30
  33.4 0.8 %shard_map.44 = f32[64,64]{1,0:T(8,128)} custom-call(f32[32,128]{1,0:T(8,128)S(1)} %get-tuple-element.35.kept, f32[32,128]{1,0:T(8,128)S(1)} %collective-permute-done.9.one, f32[40,128]{1,0:T(8,128)S(1)} %collective-permute-done.10.two, f32[48,128]{1,0:T(8,128)S(1)} %collective-permute-done.11.three), custom_call_target="tpu_custom_call" | custom-call | tf_op jit(solution)/shard_map/pallas_call | solution.py:278
  (12 shorter events, 0.1 us)
Async XLA Ops:
  0.0 0.7 %copy-start.1 = (s32[1,2]{1,0:T(1,128)S(1)}, s32[1,2]{1,0:T(1,128)}, u32[]{:S(2)}) copy-start(s32[1,2]{1,0:T(1,128)} %screen_ref.1) | copy-start | bytes 28
  0.0 2.2 %copy-start = (f32[64,256]{1,0:T(8,128)S(1)}, f32[64,256]{1,0:T(8,128)}, u32[]{:S(2)}) copy-start(f32[64,256]{1,0:T(8,128)} %density.1) | copy-start | bytes 196612
  0.0 6.0 %collective-permute-start.1 = (f32[1024,128]{1,0:T(8,128)}, f32[1024,128]{1,0:T(8,128)S(1)}, u32[]{:S(2)}, u32[]{:S(2)}) collective-permute-start(f32[1024,128]{1,0:T(8,128)} %bitcast.1), channel_id=1, source_target_pairs={{0,1},{1,0},{2,3},{3,2},{4,5},{5,4},{6,7},{7,6},{8,9},{9,8},{10,11... | collective-permute-start | bytes 1572872 | tf_op jit(solution)/shard_map/ppermute | solution.py:30
  0.7 1.5 %collective-permute-start = (s32[1,2]{1,0:T(1,128)S(1)}, s32[1,2]{1,0:T(1,128)S(1)}, u32[]{:S(2)}, u32[]{:S(2)}) collective-permute-start(s32[1,2]{1,0:T(1,128)S(1)} %copy-done.1), channel_id=1, source_target_pairs={{0,1},{1,0},{2,3},{3,2},{4,5},{5,4},{6,7},{7,6},{8,9},{9,8},{10,11... | collective-permute-start | bytes 32 | tf_op jit(solution)/shard_map/ppermute | solution.py:30
  2.3 11.8 %collective-permute-start.3 = (f32[296,128]{1,0:T(8,128)S(1)}, f32[296,128]{1,0:T(8,128)S(1)}, u32[]{:S(2)}, u32[]{:S(2)}) collective-permute-start(f32[296,128]{1,0:T(8,128)S(1)} %shard_map.39), channel_id=1, source_target_pairs={{0,8},{4,12},{8,0},{12,4},{1,9},{5,13},{9,1},{13,5},{2,10},{6,14},... | collective-permute-start | bytes 454664 | tf_op jit(solution)/shard_map/ppermute | solution.py:30
  6.3 9.1 %collective-permute-start.2 = (f32[384,128]{1,0:T(8,128)S(1)}, f32[384,128]{1,0:T(8,128)S(1)}, u32[]{:S(2)}, u32[]{:S(2)}) collective-permute-start(f32[384,128]{1,0:T(8,128)S(1)} %get-tuple-element.24), channel_id=1, source_target_pairs={{0,4},{4,0},{8,12},{12,8},{1,5},{5,1},{9,13},{13,9},{2,6},{6,2},{1... | collective-permute-start | bytes 589832 | tf_op jit(solution)/shard_map/ppermute | solution.py:30
  7.9 11.1 %collective-permute-start.5 = (f32[288,128]{1,0:T(8,128)S(1)}, f32[288,128]{1,0:T(8,128)S(1)}, u32[]{:S(2)}, u32[]{:S(2)}) collective-permute-start(f32[288,128]{1,0:T(8,128)S(1)} %get-tuple-element.30), channel_id=1, source_target_pairs={{0,12},{4,8},{8,4},{12,0},{1,13},{5,9},{9,5},{13,1},{2,14},{6,10},... | collective-permute-start | bytes 442376 | tf_op jit(solution)/shard_map/ppermute | solution.py:30
  14.1 1.3 %collective-permute-start.4 = (f32[168,128]{1,0:T(8,128)S(1)}, f32[168,128]{1,0:T(8,128)S(1)}, u32[]{:S(2)}, u32[]{:S(2)}) collective-permute-start(f32[168,128]{1,0:T(8,128)S(1)} %shard_map.40), channel_id=1, source_target_pairs={{0,1},{1,0},{2,3},{3,2},{4,5},{5,4},{6,7},{7,6},{8,9},{9,8},{10,11... | collective-permute-start | bytes 258056 | tf_op jit(solution)/shard_map/ppermute | solution.py:30
  20.0 1.9 %collective-permute-start.6 = (f32[64,256]{1,0:T(8,128)S(1)}, f32[64,256]{1,0:T(8,128)S(1)}, u32[]{:S(2)}, u32[]{:S(2)}) collective-permute-start(f32[64,256]{1,0:T(8,128)S(1)} %get-tuple-element.32), channel_id=1, source_target_pairs={{0,1},{1,0},{2,3},{3,2},{4,5},{5,4},{6,7},{7,6},{8,9},{9,8},{10,11... | collective-permute-start | bytes 196616 | tf_op jit(solution)/shard_map/ppermute | solution.py:30
  20.1 4.5 %collective-permute-start.7 = (f32[64,256]{1,0:T(8,128)S(1)}, f32[64,256]{1,0:T(8,128)S(1)}, u32[]{:S(2)}, u32[]{:S(2)}) collective-permute-start(f32[64,256]{1,0:T(8,128)S(1)} %get-tuple-element.33), channel_id=1, source_target_pairs={{0,2},{1,3},{2,0},{3,1},{4,6},{5,7},{6,4},{7,5},{8,10},{9,11},{10,... | collective-permute-start | bytes 196616 | tf_op jit(solution)/shard_map/ppermute | solution.py:30
  21.7 4.0 %collective-permute-start.8 = (f32[64,256]{1,0:T(8,128)S(1)}, f32[64,256]{1,0:T(8,128)S(1)}, u32[]{:S(2)}, u32[]{:S(2)}) collective-permute-start(f32[64,256]{1,0:T(8,128)S(1)} %get-tuple-element.34), channel_id=1, source_target_pairs={{0,3},{1,2},{2,1},{3,0},{4,7},{5,6},{6,5},{7,4},{8,11},{9,10},{10,... | collective-permute-start | bytes 196616 | tf_op jit(solution)/shard_map/ppermute | solution.py:30
  25.9 7.5 %collective-permute-start.11 = (f32[48,128]{1,0:T(8,128)S(1)}, f32[48,128]{1,0:T(8,128)S(1)}, u32[]{:S(2)}, u32[]{:S(2)}) collective-permute-start(f32[48,128]{1,0:T(8,128)S(1)} %get-tuple-element.38), channel_id=1, source_target_pairs={{0,12},{4,8},{8,4},{12,0},{1,13},{5,9},{9,5},{13,1},{2,14},{6,10},... | collective-permute-start | bytes 73736 | tf_op jit(solution)/shard_map/ppermute | solution.py:30
  28.4 5.0 %collective-permute-start.10 = (f32[40,128]{1,0:T(8,128)S(1)}, f32[40,128]{1,0:T(8,128)S(1)}, u32[]{:S(2)}, u32[]{:S(2)}) collective-permute-start(f32[40,128]{1,0:T(8,128)S(1)} %get-tuple-element.37), channel_id=1, source_target_pairs={{0,8},{4,12},{8,0},{12,4},{1,9},{5,13},{9,1},{13,5},{2,10},{6,14},... | collective-permute-start | bytes 61448 | tf_op jit(solution)/shard_map/ppermute | solution.py:30
  29.6 3.8 %collective-permute-start.9 = (f32[32,128]{1,0:T(8,128)S(1)}, f32[32,128]{1,0:T(8,128)S(1)}, u32[]{:S(2)}, u32[]{:S(2)}) collective-permute-start(f32[32,128]{1,0:T(8,128)S(1)} %get-tuple-element.36), channel_id=1, source_target_pairs={{0,4},{4,0},{8,12},{12,8},{1,5},{5,1},{9,13},{13,9},{2,6},{6,2},{1... | collective-permute-start | bytes 49160 | tf_op jit(solution)/shard_map/ppermute | solution.py:30

commit v10 on v9

--- a/solution.py
+++ b/solution.py
@@ -181,46 +181,65 @@
             keep_parts((eh, el), j, i * size, parts)
 
 
-def fock_kernel(eh, el, fh, fl, three, *refs):
-    outs, (dh, dl, lh, ll, total) = refs[:4], refs[4:]
+def fock_rows(a, bh, bl, dh, dl, total, outs):
+    s = lax.axis_index("sub")
+    count, size = total.shape[0], outs[0].shape[0]
+    rows = pl.ds(pl.multiple_of(a * count, count), count)
+    side = lambda *parts: jnp.concatenate(parts, axis=1)
+    whole = jnp.concatenate([dh[...], dl[...], dh[...]], axis=0)
+    lefts, rights = [], []
+    for j in range(bh.shape[0]):
+        high, lower = bh[j, rows, :], bl[j, rows, :]
+        c1, c2 = split(jnp.dot(side(high, high, lower), whole, preferred_element_type=F32))
+        lefts += [c1, c1, c2]
+        rights += [bh[j], bl[j], bh[j]]
+    total[...] = lax.dot_general(
+        side(*lefts), side(*rights), (((1,), (1,)), ((), ())), preferred_element_type=F32
+    )
+    for d, out in enumerate(outs):
+        out[...] = total[pl.ds(pl.multiple_of((s ^ d) * size, size), size), :]
+
+
+def leave_kernel(eh, el, fh, fl, three, same, cross, bh, bl, dh, dl, total):
     r = lax.axis_index("row")
-    q = lax.axis_index("aux") * 2 + lax.axis_index("sub")
     share, orbitals = eh.shape[0], fh.shape[0]
     size, cut = orbitals - eh.shape[1], orbitals // 128
     h, odd = r // 2, r % 2 == 1
     corner = unfold(three[share * cut * size:, :])
     low = lax.broadcasted_iota(jnp.int32, (size, 128), 1) < 64
     corner = split(jnp.where(low, corner, pltpu.roll(corner, 64, 1)))
-    rows = pl.ds(pl.multiple_of((r ^ 3) * size, size), size)
+    rows_of = lambda k: pl.ds(pl.multiple_of((r ^ k) * size, size), size)
+    rows = rows_of(3)
     for old, new, part in zip((fh, fl), (dh, dl), corner):
         new[...] = old[...]
         for x in range(cut):
             columns = slice(x * 128, (x + 1) * 128)
             other = jnp.logical_or(low ^ odd, h == x)
             new[rows, columns] = jnp.where(other, old[rows, columns].astype(F32), part.astype(F32)).astype(BF16)
-    side = lambda *parts: jnp.concatenate(parts, axis=1)
-    whole = jnp.concatenate([dh[...], dl[...], dh[...]], axis=0)
-    lefts, rights = [], []
     for j in range(share):
-        keep_parts((lh, ll), j, 0, chunk_parts(three, j, size, cut))
-        b1, b2 = [jnp.concatenate([x[j], y[j]], axis=0) for x, y in ((eh, lh), (el, ll))]
-        c1, c2 = split(jnp.dot(side(b1, b1, b2), whole, preferred_element_type=F32))
-        lefts += [c1, c1, c2]
-        rights += [b1, b2, b1]
-    total[...] = lax.dot_general(
-        side(*lefts), side(*rights), (((1,), (1,)), ((), ())), preferred_element_type=F32
-    )
-    for dq in range(4):
-        k = q ^ dq ^ r
-        start = pl.multiple_of((k % 2 * 2 + k // 2) * size, size)
-        outs[dq][...] = total[pl.ds(start, size), :]
+        for i, k in enumerate((0, 2, 1)):
+            for old, new in ((eh, bh), (el, bl)):
+                new[j, rows_of(k), :] = old[j, i * size:(i + 1) * size, :]
+        for x, value in enumerate(chunk_parts(three, j, size, cut)):
+            for new, part in zip((bh, bl), split(value)):
+                new[j, rows, x * 128:(x + 1) * 128] = part
+    fock_rows(1 - lax.axis_index("aux"), bh, bl, dh, dl, total, (same, cross))
+
+
+def stay_kernel(bh, bl, dh, dl, same, upper, lower, total, whole):
+    fock_rows(lax.axis_index("aux"), bh, bl, dh, dl, total, (same, whole))
+    half = upper.shape[0]
+    upper[...] = whole[:half, :]
+    lower[...] = whole[half:, :]
 
 
 def cut_kernel(*refs):
-    ins, outs = refs[:4], refs[4:]
-    value = ins[0][...] + ins[1][...] + (ins[2][...] + ins[3][...])
+    ins, outs = refs[:5], refs[5:]
+    r = lax.axis_index("row")
+    near = jnp.concatenate([ins[3][...], ins[4][...]], axis=0)
+    value = ins[0][...] + near + (ins[1][...] + ins[2][...])
     for k in range(4):
-        outs[k][:value.shape[0] // 2, :] = fold(column_block(value, k % 2 * 2 + k // 2))
+        outs[k][:value.shape[0] // 2, :] = fold(column_block(value, r ^ k))
 
 
 def final_kernel(kept, one, two, three, out):
@@ -260,20 +279,15 @@
     early = call(
         early_kernel, [], count=5, halved=((share, orbitals - block_size, orbitals),) * 2 + (whole,) * 2
     )(own, one, two, two_other, density)
-    parts = call(
-        fock_kernel,
-        [(block_size, orbitals)] * 4,
-        scratch=[
-            pltpu.VMEM(whole, BF16),
-            pltpu.VMEM(whole, BF16),
-            pltpu.VMEM((share, block_size, orbitals), BF16),
-            pltpu.VMEM((share, block_size, orbitals), BF16),
-            pltpu.VMEM(whole, F32),
-        ],
-        count=5,
+    block = (block_size, orbitals)
+    scratch = [pltpu.VMEM((2 * block_size, orbitals), F32)]
+    far_same, far_cross, *pieces = call(
+        leave_kernel, [block] * 2, scratch, count=5, halved=((share,) + whole,) * 2 + (whole,) * 2
     )(*early, three)
-    sums = [parts[0]] + [swap(parts[k], ("aux", "sub"), 4, k) for k in (1, 2, 3)]
-    cuts = call(cut_kernel, [(block_size // 2 + more, 2 * block_size) for more in (0, 0, 8, 16)], count=4)(*sums)
+    piece = (block_size // 2, orbitals)
+    same, upper, lower = call(stay_kernel, [block, piece, piece], scratch + [pltpu.VMEM(block, F32)], count=4)(*pieces)
+    sums = [same, swap(far_same, "aux", 2, 1), swap(far_cross, ("aux", "sub"), 4, 3), core(upper), core(lower)]
+    cuts = call(cut_kernel, [(block_size // 2 + more, 2 * block_size) for more in (0, 0, 8, 16)], count=5)(*sums)
     moved = [row(cuts[k], k) for k in (1, 2, 3)]
     return call(final_kernel, [(block_size, block_size)], count=4)(cuts[0], *moved)[0]
 

time: 34.3 us -> 34.4 us (level)
  waiting for transfers between devices: 17.7 us -> 16.9 us
  starting transfers between devices: 12.7 us -> 13.2 us
  Pallas kernels: 3.45 us -> 3.85 us
    ppermute x12 -> x13, waiting for transfers between devices: 17.7 us -> 16.9 us  [swap(): return lax.ppermute(x, axes, [(a, a ^ k) for a in range(size)])]
    ppermute x12 -> x13, starting transfers between devices: 12.7 us -> 13.2 us  [swap(): return lax.ppermute(x, axes, [(a, a ^ k) for a in range(size)])]
    pallas_call x1 -> x2, Pallas kernels: 0.94 us -> 1.32 us  [the longest x1 0.73 us: dealt_body(): call(leave_kernel, [block] * 2, scratch, count=5, halved=((share,) + whol...]
  transfers between devices with their start and end apart: 12 -> 13, of which waited for: 6 -> 8; matrix products, arithmetic and copies ran while one was open for 0% -> 0% of each run, Pallas kernels for 5% -> 6%
where the time goes in v10:
time: 34.4 us; the launch traced here: 34.2 us
  waiting for transfers between devices  16.9 us (49%)
  starting transfers between devices  13.2 us (38%)
  Pallas kernels  3.85 us (11%)
    ppermute x13, waiting for transfers between devices, swap(): return lax.ppermute(x, axes, [(a, a ^ k) for a in range(size)])  16.9 us
    ppermute x13, starting transfers between devices, swap(): return lax.ppermute(x, axes, [(a, a ^ k) for a in range(size)])  13.2 us
    pallas_call x1, Pallas kernels, dealt_body(): call(functools.partial(near_kernel, share, block_size), [(2 * share * blo...  1.07 us
    pallas_call x1, Pallas kernels, dealt_body(): call(final_kernel, [(block_size, block_size)], count=4)(cuts[0], *moved)[0]  0.76 us
    pallas_call x1, Pallas kernels, dealt_body(): call(leave_kernel, [block] * 2, scratch, count=5, halved=((share,) + whol...  0.73 us
  transfers between devices with their start and end apart: 13, of which 8 were waited for; matrix products, arithmetic and copies ran while one was open for 0% of the time, Pallas kernels for 6%

profile of v10, /device:TPU:0, one launch (start us, length us, event | category | flops | bytes accessed | tf_op | source)
XLA Modules:
  0.0 34.2 jit_solution(441186322005581835)
XLA Ops:
  0.0 0.5 %collective-permute-start.1 = (f32[1024,128]{1,0:T(8,128)}, f32[1024,128]{1,0:T(8,128)S(1)}, u32[]{:S(2)}, u32[]{:S(2)}) collective-permute-start(f32[1024,128]{1,0:T(8,128)} %bitcast.1), channel_id=1, source_target_pairs={{0,1},{1,0},{2,3},{3,2},{4,5},{5,4},{6,7},{7,6},{8,9},{9,8},{10,11... | collective-permute-start | bytes 1572872 | tf_op jit(solution)/shard_map/ppermute | solution.py:30
  0.5 0.2 copy-done.1
  0.7 0.5 %collective-permute-start = (s32[1,2]{1,0:T(1,128)S(1)}, s32[1,2]{1,0:T(1,128)S(1)}, u32[]{:S(2)}, u32[]{:S(2)}) collective-permute-start(s32[1,2]{1,0:T(1,128)S(1)} %copy-done.1), channel_id=1, source_target_pairs={{0,1},{1,0},{2,3},{3,2},{4,5},{5,4},{6,7},{7,6},{8,9},{9,8},{10,11... | collective-permute-start | bytes 32 | tf_op jit(solution)/shard_map/ppermute | solution.py:30
  1.1 1.1 %shard_map.37 = (f32[256,128]{1,0:T(8,128)S(1)}, f32[1024,128]{1,0:T(8,128)S(1)}) custom-call(f32[1024,128]{1,0:T(8,128)} %bitcast.2), custom_call_target="tpu_custom_call" | custom-call | tf_op jit(solution)/shard_map/pallas_call | solution.py:260
  2.3 3.8 %collective-permute-start.3 = (f32[296,128]{1,0:T(8,128)S(1)}, f32[296,128]{1,0:T(8,128)S(1)}, u32[]{:S(2)}, u32[]{:S(2)}) collective-permute-start(f32[296,128]{1,0:T(8,128)S(1)} %shard_map.39), channel_id=1, source_target_pairs={{0,8},{4,12},{8,0},{12,4},{1,9},{5,13},{9,1},{13,5},{2,10},{6,14},... | collective-permute-start | bytes 454664 | tf_op jit(solution)/shard_map/ppermute | solution.py:30
  6.0 0.2 shard_map.38
  6.3 1.6 %collective-permute-start.2 = (f32[384,128]{1,0:T(8,128)S(1)}, f32[384,128]{1,0:T(8,128)S(1)}, u32[]{:S(2)}, u32[]{:S(2)}) collective-permute-start(f32[384,128]{1,0:T(8,128)S(1)} %get-tuple-element.29), channel_id=1, source_target_pairs={{0,4},{4,0},{8,12},{12,8},{1,5},{5,1},{9,13},{13,9},{2,6},{6,2},{1... | collective-permute-start | bytes 589832 | tf_op jit(solution)/shard_map/ppermute | solution.py:30
  7.9 6.1 %collective-permute-done.3.two = f32[296,128]{1,0:T(8,128)S(1)} collective-permute-done((f32[296,128]{1,0:T(8,128)S(1)}, f32[296,128]{1,0:T(8,128)S(1)}, u32[]{:S(2)}, u32[]{:S(2)}) %collective-permute-start.3) | collective-permute-done | bytes 151584 | tf_op jit(solution)/shard_map/ppermute | solution.py:30
  14.2 1.3 %collective-permute-done.4.two_other = f32[168,128]{1,0:T(8,128)S(1)} collective-permute-done((f32[168,128]{1,0:T(8,128)S(1)}, f32[168,128]{1,0:T(8,128)S(1)}, u32[]{:S(2)}, u32[]{:S(2)}) %collective-permute-start.4) | collective-permute-done | bytes 86048 | tf_op jit(solution)/shard_map/ppermute | solution.py:30
  15.4 0.2 shard_map.41
  15.7 3.4 %collective-permute-done.5.three = f32[288,128]{1,0:T(8,128)S(1)} collective-permute-done((f32[288,128]{1,0:T(8,128)S(1)}, f32[288,128]{1,0:T(8,128)S(1)}, u32[]{:S(2)}, u32[]{:S(2)}) %collective-permute-start.5) | collective-permute-done | bytes 147488 | tf_op jit(solution)/shard_map/ppermute | solution.py:30
  19.1 0.7 %shard_map.42 = (f32[64,256]{1,0:T(8,128)S(1)}, f32[64,256]{1,0:T(8,128)S(1)}, bf16[2,256,256]{2,1,0:T(8,128)(2,1)S(1)}, bf16[2,256,256]{2,1,0:T(8,128)(2,1)S(1)...) custom-call(bf16[2,192,256]{2,1,0:T(8,128)(2,1)S(1)} %get-tuple-element.31.eh, ...), custom_call_target="tpu_custom_call" | custom-call | tf_op jit(solution)/shard_map/pallas_call | solution.py:284
  19.8 1.6 %collective-permute-start.6 = (f32[64,256]{1,0:T(8,128)S(1)}, f32[64,256]{1,0:T(8,128)S(1)}, u32[]{:S(2)}, u32[]{:S(2)}) collective-permute-start(f32[64,256]{1,0:T(8,128)S(1)} %get-tuple-element.41), channel_id=1, source_target_pairs={{0,2},{2,0},{1,3},{3,1},{4,6},{6,4},{5,7},{7,5},{8,10},{10,8},{9,1... | collective-permute-start | bytes 196616 | tf_op jit(solution)/shard_map/ppermute | solution.py:30
  21.4 0.6 %shard_map.43 = (f32[64,256]{1,0:T(8,128)S(1)}, f32[32,256]{1,0:T(8,128)S(1)}, f32[32,256]{1,0:T(8,128)S(1)}) custom-call(bf16[2,256,256]{2,1,0:T(8,128)(2,1)S(1)} %get-tuple-element.36.bh, bf16[2,256,256]{2,1,0:T(8,128)(2,1)S(1)} %get-tuple-element.37.bl, bf16[256,256]{1,0:T(8,128)(2,1)S(1)} %get-tuple-element.38.dh, bf16[256,256]{1,0:T(8,128)(2,1)S(1)} %get-tuple-element.39.dl), custom_call_target="tpu_custom_call" | custom-call | tf_op jit(solution)/shard_map/pallas_call | solution.py:288
  22.0 0.7 %collective-permute-start.8 = (f32[32,256]{1,0:T(8,128)S(1)}, f32[32,256]{1,0:T(8,128)S(1)}, u32[]{:S(2)}, u32[]{:S(2)}) collective-permute-start(f32[32,256]{1,0:T(8,128)S(1)} %get-tuple-element.43), channel_id=1, source_target_pairs={{0,1},{1,0},{2,3},{3,2},{4,5},{5,4},{6,7},{7,6},{8,9},{9,8},{10,11... | collective-permute-start | bytes 98312 | tf_op jit(solution)/shard_map/ppermute | solution.py:30
  22.8 0.8 %collective-permute-done.8.refs_3_ = f32[32,256]{1,0:T(8,128)S(1)} collective-permute-done((f32[32,256]{1,0:T(8,128)S(1)}, f32[32,256]{1,0:T(8,128)S(1)}, u32[]{:S(2)}, u32[]{:S(2)}) %collective-permute-start.8) | collective-permute-done | bytes 32800 | tf_op jit(solution)/shard_map/ppermute | solution.py:30
  23.6 0.3 %collective-permute-done.9.refs_4_ = f32[32,256]{1,0:T(8,128)S(1)} collective-permute-done((f32[32,256]{1,0:T(8,128)S(1)}, f32[32,256]{1,0:T(8,128)S(1)}, u32[]{:S(2)}, u32[]{:S(2)}) %collective-permute-start.9) | collective-permute-done | bytes 32800 | tf_op jit(solution)/shard_map/ppermute | solution.py:30
  23.9 0.3 collective-permute-done.6.refs_1_
  24.2 1.4 %collective-permute-done.7.refs_2_ = f32[64,256]{1,0:T(8,128)S(1)} collective-permute-done((f32[64,256]{1,0:T(8,128)S(1)}, f32[64,256]{1,0:T(8,128)S(1)}, u32[]{:S(2)}, u32[]{:S(2)}) %collective-permute-start.7) | collective-permute-done | bytes 65568 | tf_op jit(solution)/shard_map/ppermute | solution.py:30
  25.7 2.5 %collective-permute-start.12 = (f32[48,128]{1,0:T(8,128)S(1)}, f32[48,128]{1,0:T(8,128)S(1)}, u32[]{:S(2)}, u32[]{:S(2)}) collective-permute-start(f32[48,128]{1,0:T(8,128)S(1)} %get-tuple-element.48), channel_id=1, source_target_pairs={{0,12},{4,8},{8,4},{12,0},{1,13},{5,9},{9,5},{13,1},{2,14},{6,10},... | collective-permute-start | bytes 73736 | tf_op jit(solution)/shard_map/ppermute | solution.py:30
  28.3 1.4 %collective-permute-start.11 = (f32[40,128]{1,0:T(8,128)S(1)}, f32[40,128]{1,0:T(8,128)S(1)}, u32[]{:S(2)}, u32[]{:S(2)}) collective-permute-start(f32[40,128]{1,0:T(8,128)S(1)} %get-tuple-element.47), channel_id=1, source_target_pairs={{0,8},{4,12},{8,0},{12,4},{1,9},{5,13},{9,1},{13,5},{2,10},{6,14},... | collective-permute-start | bytes 61448 | tf_op jit(solution)/shard_map/ppermute | solution.py:30
  29.7 0.5 %collective-permute-start.10 = (f32[32,128]{1,0:T(8,128)S(1)}, f32[32,128]{1,0:T(8,128)S(1)}, u32[]{:S(2)}, u32[]{:S(2)}) collective-permute-start(f32[32,128]{1,0:T(8,128)S(1)} %get-tuple-element.46), channel_id=1, source_target_pairs={{0,4},{4,0},{8,12},{12,8},{1,5},{5,1},{9,13},{13,9},{2,6},{6,2},{1... | collective-permute-start | bytes 49160 | tf_op jit(solution)/shard_map/ppermute | solution.py:30
  30.2 3.3 %collective-permute-done.10.one = f32[32,128]{1,0:T(8,128)S(1)} collective-permute-done((f32[32,128]{1,0:T(8,128)S(1)}, f32[32,128]{1,0:T(8,128)S(1)}, u32[]{:S(2)}, u32[]{:S(2)}) %collective-permute-start.10) | collective-permute-done | bytes 16416 | tf_op jit(solution)/shard_map/ppermute | solution.py:30
  33.5 0.8 %shard_map.45 = f32[64,64]{1,0:T(8,128)} custom-call(f32[32,128]{1,0:T(8,128)S(1)} %get-tuple-element.45.kept, f32[32,128]{1,0:T(8,128)S(1)} %collective-permute-done.10.one, f32[40,128]{1,0:T(8,128)S(1)} %collective-permute-done.11.two, f32[48,128]{1,0:T(8,128)S(1)} %collective-permute-done.12.three), custom_call_target="tpu_custom_call" | custom-call | tf_op jit(solution)/shard_map/pallas_call | solution.py:292
  (15 shorter events, 0.4 us)
Async XLA Ops:
  0.0 0.7 %copy-start.1 = (s32[1,2]{1,0:T(1,128)S(1)}, s32[1,2]{1,0:T(1,128)}, u32[]{:S(2)}) copy-start(s32[1,2]{1,0:T(1,128)} %screen_ref.1) | copy-start | bytes 28
  0.0 2.2 %copy-start = (f32[64,256]{1,0:T(8,128)S(1)}, f32[64,256]{1,0:T(8,128)}, u32[]{:S(2)}) copy-start(f32[64,256]{1,0:T(8,128)} %density.1) | copy-start | bytes 196612
  0.0 6.0 %collective-permute-start.1 = (f32[1024,128]{1,0:T(8,128)}, f32[1024,128]{1,0:T(8,128)S(1)}, u32[]{:S(2)}, u32[]{:S(2)}) collective-permute-start(f32[1024,128]{1,0:T(8,128)} %bitcast.1), channel_id=1, source_target_pairs={{0,1},{1,0},{2,3},{3,2},{4,5},{5,4},{6,7},{7,6},{8,9},{9,8},{10,11... | collective-permute-start | bytes 1572872 | tf_op jit(solution)/shard_map/ppermute | solution.py:30
  0.7 1.5 %collective-permute-start = (s32[1,2]{1,0:T(1,128)S(1)}, s32[1,2]{1,0:T(1,128)S(1)}, u32[]{:S(2)}, u32[]{:S(2)}) collective-permute-start(s32[1,2]{1,0:T(1,128)S(1)} %copy-done.1), channel_id=1, source_target_pairs={{0,1},{1,0},{2,3},{3,2},{4,5},{5,4},{6,7},{7,6},{8,9},{9,8},{10,11... | collective-permute-start | bytes 32 | tf_op jit(solution)/shard_map/ppermute | solution.py:30
  2.3 11.8 %collective-permute-start.3 = (f32[296,128]{1,0:T(8,128)S(1)}, f32[296,128]{1,0:T(8,128)S(1)}, u32[]{:S(2)}, u32[]{:S(2)}) collective-permute-start(f32[296,128]{1,0:T(8,128)S(1)} %shard_map.39), channel_id=1, source_target_pairs={{0,8},{4,12},{8,0},{12,4},{1,9},{5,13},{9,1},{13,5},{2,10},{6,14},... | collective-permute-start | bytes 454664 | tf_op jit(solution)/shard_map/ppermute | solution.py:30
  6.3 9.1 %collective-permute-start.2 = (f32[384,128]{1,0:T(8,128)S(1)}, f32[384,128]{1,0:T(8,128)S(1)}, u32[]{:S(2)}, u32[]{:S(2)}) collective-permute-start(f32[384,128]{1,0:T(8,128)S(1)} %get-tuple-element.29), channel_id=1, source_target_pairs={{0,4},{4,0},{8,12},{12,8},{1,5},{5,1},{9,13},{13,9},{2,6},{6,2},{1... | collective-permute-start | bytes 589832 | tf_op jit(solution)/shard_map/ppermute | solution.py:30
  7.9 11.1 %collective-permute-start.5 = (f32[288,128]{1,0:T(8,128)S(1)}, f32[288,128]{1,0:T(8,128)S(1)}, u32[]{:S(2)}, u32[]{:S(2)}) collective-permute-start(f32[288,128]{1,0:T(8,128)S(1)} %get-tuple-element.35), channel_id=1, source_target_pairs={{0,12},{4,8},{8,4},{12,0},{1,13},{5,9},{9,5},{13,1},{2,14},{6,10},... | collective-permute-start | bytes 442376 | tf_op jit(solution)/shard_map/ppermute | solution.py:30
  14.1 1.3 %collective-permute-start.4 = (f32[168,128]{1,0:T(8,128)S(1)}, f32[168,128]{1,0:T(8,128)S(1)}, u32[]{:S(2)}, u32[]{:S(2)}) collective-permute-start(f32[168,128]{1,0:T(8,128)S(1)} %shard_map.40), channel_id=1, source_target_pairs={{0,1},{1,0},{2,3},{3,2},{4,5},{5,4},{6,7},{7,6},{8,9},{9,8},{10,11... | collective-permute-start | bytes 258056 | tf_op jit(solution)/shard_map/ppermute | solution.py:30
  19.8 4.3 %collective-permute-start.6 = (f32[64,256]{1,0:T(8,128)S(1)}, f32[64,256]{1,0:T(8,128)S(1)}, u32[]{:S(2)}, u32[]{:S(2)}) collective-permute-start(f32[64,256]{1,0:T(8,128)S(1)} %get-tuple-element.41), channel_id=1, source_target_pairs={{0,2},{2,0},{1,3},{3,1},{4,6},{6,4},{5,7},{7,5},{8,10},{10,8},{9,1... | collective-permute-start | bytes 196616 | tf_op jit(solution)/shard_map/ppermute | solution.py:30
  21.4 4.2 %collective-permute-start.7 = (f32[64,256]{1,0:T(8,128)S(1)}, f32[64,256]{1,0:T(8,128)S(1)}, u32[]{:S(2)}, u32[]{:S(2)}) collective-permute-start(f32[64,256]{1,0:T(8,128)S(1)} %get-tuple-element.42), channel_id=1, source_target_pairs={{0,3},{1,2},{2,1},{3,0},{4,7},{5,6},{6,5},{7,4},{8,11},{9,10},{10,... | collective-permute-start | bytes 196616 | tf_op jit(solution)/shard_map/ppermute | solution.py:30
  22.0 1.6 %collective-permute-start.8 = (f32[32,256]{1,0:T(8,128)S(1)}, f32[32,256]{1,0:T(8,128)S(1)}, u32[]{:S(2)}, u32[]{:S(2)}) collective-permute-start(f32[32,256]{1,0:T(8,128)S(1)} %get-tuple-element.43), channel_id=1, source_target_pairs={{0,1},{1,0},{2,3},{3,2},{4,5},{5,4},{6,7},{7,6},{8,9},{9,8},{10,11... | collective-permute-start | bytes 98312 | tf_op jit(solution)/shard_map/ppermute | solution.py:30
  22.7 1.2 %collective-permute-start.9 = (f32[32,256]{1,0:T(8,128)S(1)}, f32[32,256]{1,0:T(8,128)S(1)}, u32[]{:S(2)}, u32[]{:S(2)}) collective-permute-start(f32[32,256]{1,0:T(8,128)S(1)} %get-tuple-element.44), channel_id=1, source_target_pairs={{0,1},{1,0},{2,3},{3,2},{4,5},{5,4},{6,7},{7,6},{8,9},{9,8},{10,11... | collective-permute-start | bytes 98312 | tf_op jit(solution)/shard_map/ppermute | solution.py:30
  25.7 7.7 %collective-permute-start.12 = (f32[48,128]{1,0:T(8,128)S(1)}, f32[48,128]{1,0:T(8,128)S(1)}, u32[]{:S(2)}, u32[]{:S(2)}) collective-permute-start(f32[48,128]{1,0:T(8,128)S(1)} %get-tuple-element.48), channel_id=1, source_target_pairs={{0,12},{4,8},{8,4},{12,0},{1,13},{5,9},{9,5},{13,1},{2,14},{6,10},... | collective-permute-start | bytes 73736 | tf_op jit(solution)/shard_map/ppermute | solution.py:30
  28.3 5.2 %collective-permute-start.11 = (f32[40,128]{1,0:T(8,128)S(1)}, f32[40,128]{1,0:T(8,128)S(1)}, u32[]{:S(2)}, u32[]{:S(2)}) collective-permute-start(f32[40,128]{1,0:T(8,128)S(1)} %get-tuple-element.47), channel_id=1, source_target_pairs={{0,8},{4,12},{8,0},{12,4},{1,9},{5,13},{9,1},{13,5},{2,10},{6,14},... | collective-permute-start | bytes 61448 | tf_op jit(solution)/shard_map/ppermute | solution.py:30
  29.7 3.7 %collective-permute-start.10 = (f32[32,128]{1,0:T(8,128)S(1)}, f32[32,128]{1,0:T(8,128)S(1)}, u32[]{:S(2)}, u32[]{:S(2)}) collective-permute-start(f32[32,128]{1,0:T(8,128)S(1)} %get-tuple-element.46), channel_id=1, source_target_pairs={{0,4},{4,0},{8,12},{12,8},{1,5},{5,1},{9,13},{13,9},{2,6},{6,2},{1... | collective-permute-start | bytes 49160 | tf_op jit(solution)/shard_map/ppermute | solution.py:30
